TPU v7x, 32 devices: a whole 2x2x4 slice. The times are simulated.
32 devices in a mesh: groups: 2 (over y), width: 4 (over z), store: 4 (over x, core).
Axes of the slice: x: 2, y: 2, z: 4, core: 2. Of those that a mesh axis runs over, the one named last changes fastest.
Arguments:
- activations: bfloat16 [8192, 8192], P(('groups', 'store'), 'width'), parts along dimension 0, may hold values from -6 to 6
- out_grads: bfloat16 [8192, 8192], P(('groups', 'store'), 'width'), parts along dimension 0, may hold values from -6 to 6
- example_of: int32 [8, 1024], P(('groups', 'store')), parts along dimension 0, may hold values from 0 to 127, never falling along the last dimension, each value on 1 to 16 neighbouring positions
- proj_in: bfloat16 [8192, 64], P('width'), may hold values from -0.0625 to 0.0625
- proj_out: bfloat16 [8192, 64], P('width'), may hold values from -0.0625 to 0.0625
- inverse_curvature: bfloat16 [4096, 4096], P('width'), may hold values from -1 to 3
- stored: bfloat16 [4096, 4096], P(('width', 'store')), may hold values from -0.3984375 to 0.3984375
Outputs:
- scores: float32 [1024, 4096], P('groups', ('width', 'store')), parts along dimension 0
There are 2 independent parts, one for each index of `groups`. A program takes and returns all parts, laid end to end along the dimension named above; an argument that names none is the same for every part. Nothing has to cross between parts.
Inputs may be any that keep to these rules, and one draw needn't show every extreme that they name: `example_of`: the tokens of one example are consecutive; every example of 0 to 127 has 1 to 16 tokens in each row.
All inputs are finite; a program needn't handle non-finite values.
Results may differ from a plain program's by a relative error of at most 0.0057.
Values may be sent and summed in bfloat16 or wider, within the bound.
No kernel may reach another device: no remote copies, remote signals or barrier semaphores. Data moves between devices by JAX's collectives and lax.ppermute only.
A program may use at most 64 MiB of HBM per device.

v0:
```python
import jax
import jax.numpy as jnp
from jax import lax
from jax.sharding import PartitionSpec as P

EX_DEV = 128


def body(activations, out_grads, example_of, proj_in, proj_out, inverse_curvature, stored):
    rank_dim = proj_in.shape[1]
    partial_value = jnp.concatenate(
        [
            jnp.dot(activations, proj_in, preferred_element_type=jnp.float32),
            jnp.dot(out_grads, proj_out, preferred_element_type=jnp.float32),
        ],
        axis=1,
    )
    factors = lax.psum(partial_value, "width").astype(jnp.bfloat16)
    act_proj = factors[:, :rank_dim]
    grad_proj = factors[:, rank_dim:]
    token_ids = example_of[0]
    member = token_ids[None, :] == jnp.arange(EX_DEV, dtype=jnp.int32)[:, None]
    counts = jnp.sum(member.astype(jnp.float32), axis=1)
    masked = jnp.where(member[:, :, None], grad_proj[None, :, :], jnp.zeros((), jnp.bfloat16))
    outer = lax.dot_general(
        masked, act_proj, (((1,), (0,)), ((), ())), preferred_element_type=jnp.float32
    )
    outer = outer / counts[:, None, None]
    flat_grads = outer.reshape(EX_DEV, rank_dim * rank_dim).astype(jnp.bfloat16)
    query = lax.dot_general(
        flat_grads, inverse_curvature, (((1,), (1,)), ((), ())), preferred_element_type=jnp.float32
    ).astype(jnp.bfloat16)
    gathered = lax.all_gather(query[None], ("width", "store"), axis=0, tiled=True)
    width_count = lax.axis_size("width")
    store_count = lax.axis_size("store")
    blocks = gathered.reshape(width_count, store_count, query.shape[0], query.shape[1])
    stored_blocks = stored.reshape(stored.shape[0], width_count, query.shape[1])
    scores = jnp.einsum("wsef,rwf->ser", blocks, stored_blocks, preferred_element_type=jnp.float32)
    scores = scores.reshape(store_count * query.shape[0], stored.shape[0])
    return scores


def solution(mesh):
    return jax.shard_map(
        body,
        mesh=mesh,
        in_specs=(
            P(("groups", "store"), "width"),
            P(("groups", "store"), "width"),
            P(("groups", "store"), None),
            P("width", None),
            P("width", None),
            P("width", None),
            P(("width", "store"), None),
        ),
        out_specs=P("groups", ("width", "store")),
        check_vma=False,
    )
```

profile of v0, /device:TPU:0, one launch (start us, length us, event | category | flops | bytes accessed | tf_op | source)
XLA Modules:
  0.0 118.7 jit_solution(6103164699858118851)
XLA Ops:
  6.5 0.0 copy-start
  6.5 0.0 copy-start.2
  6.5 0.0 all-gather.3.cloned.1.call-start
  6.5 0.0 copy-start.1
  6.5 1.0 convert_reduce_fusion
  7.5 1.2 %iota_compare_fusion = pred[128,1024]{1,0:T(8,128)(4,1)S(1)} fusion(s32[1024]{0:T(1024)} %bitcast.27), kind=kLoop, calls=%fused_computation.13 | loop fusion | flops 131072 | bytes 135168 | tf_op jit(solution)/shard_map/eq | solution.py:22
  8.7 0.0 copy-done
  8.7 3.6 %fusion.14 = f32[1024,64]{0,1:T(8,128)S(1)} fusion(bf16[1024,2048]{1,0:T(8,128)(2,1)} %param.7, bf16[2048,64]{0,1:T(8,128)(2,1)S(1)} %copy-done), kind=kOutput, calls=%fused_computation.16 | convolution fusion | flops 268435456 | bytes 4718592 | tf_op jit(solution)/shard_map/dot_general | solution.py:13
  12.3 0.0 copy-done.2
  12.3 0.0 copy-done.1
  12.3 1.4 %fusion.15 = f32[1024,64]{0,1:T(8,128)S(1)} fusion(bf16[1024,2048]{1,0:T(8,128)(2,1)S(1)} %copy-done.1, bf16[2048,64]{0,1:T(8,128)(2,1)S(1)} %copy-done.2), kind=kOutput, calls=%fused_computation.17 | convolution fusion | flops 268435456 | bytes 4718592 | tf_op jit(solution)/shard_map/dot_general | solution.py:14
  13.8 32.1 %all-reduce.1 = bf16[1024,128]{0,1:T(8,128)(2,1)S(1)} all-reduce(f32[1024,128]{0,1:T(8,128)S(1)} %pad_maximum_fusion), channel_id=1, replica_groups=mesh['groups'=2,'width'=4,'store'=4] {'width'}, use_global_device_ids=true, to_apply=%region_0.0 | all-reduce | flops 131072 | bytes 786432 | tf_op jit(solution)/shard_map/psum | solution.py:18
  45.9 5.2 %divide_convert_fusion = bf16[128,64,64]{0,2,1:T(8,128)(2,1)S(1)} fusion(f32[128]{0:T(128)S(1)} %convert_reduce_fusion, pred[128,1024]{1,0:T(8,128)(4,1)S(1)} %iota_compare_fusion, bf16[1024,64]{0,1:T(8,128)(2,1)S(1)} %slice.8, bf16[1024,128]{0,1:T(8,128)(2,1)S(1)} %all-reduce.1), kind=kOutput, calls=%fused_computation.8 | convolution fusion | flops 1083179008 | bytes 1442304 | tf_op jit(solution)/shard_map/dot_general | solution.py:25
  51.1 0.0 copy-start.3
  51.1 7.2 %convolution_convert_fusion = bf16[128,1024]{1,0:T(8,128)(2,1)} fusion(bf16[128,4096]{0,1:T(8,128)(2,1)S(1)} %bitcast.25, bf16[1024,4096]{1,0:T(8,128)(2,1)} %param.12), kind=kOutput, calls=%fused_computation.10 | convolution fusion | flops 1073872896 | bytes 9699328 | tf_op jit(solution)/shard_map/dot_general | solution.py:30
  58.2 0.0 all-gather.3.cloned.1.call-update
  58.3 49.3 %all-gather.3.cloned.1.call-done = bf16[2048,1024]{1,0:T(8,128)(2,1)} async-done(((bf16[128,1024]{1,0:T(8,128)(2,1)}), bf16[2048,1024]{1,0:T(8,128)(2,1)}) %all-gather.3.cloned.1.call-update) | async-done | bytes 4194320 | tf_op jit(solution)/shard_map/all_gather | solution.py:33
  107.5 0.0 copy-done.3
  107.6 4.3 %fusion.8 = f32[512,256]{1,0:T(8,128)} fusion(bf16[512,1024,4]{1,0,2:T(8,128)(2,1)} %bitcast.28, bf16[32,4,8,1024]{3,2,1,0:T(8,128)(2,1)S(1)} %bitcast.29), kind=kOutput, calls=%fused_computation.9 | convolution fusion | flops 1073741824 | bytes 6815744 | tf_op jit(solution)/shard_map/wsef,rwf->ser/dot_general | solution.py:38
  (2 shorter events, 0.1 us)
Async XLA Ops:
  6.5 2.2 %copy-start = (bf16[2048,64]{0,1:T(8,128)(2,1)S(1)}, bf16[2048,64]{0,1:T(8,128)(2,1)}, u32[]{:S(2)}) copy-start(bf16[2048,64]{0,1:T(8,128)(2,1)} %param.10) | copy-start | bytes 786436
  6.5 5.8 %copy-start.2 = (bf16[2048,64]{0,1:T(8,128)(2,1)S(1)}, bf16[2048,64]{0,1:T(8,128)(2,1)}, u32[]{:S(2)}) copy-start(bf16[2048,64]{0,1:T(8,128)(2,1)} %param.11) | copy-start | bytes 786436
  6.5 101.0 %all-gather.3.cloned.1.call-start = ((), (), s32[]{:S(2)}) async-start(), calls=%async_computation | async-start | bytes 4456448 | tf_op jit(solution)/shard_map/all_gather | solution.py:33
  6.5 5.8 %copy-start.1 = (bf16[1024,2048]{1,0:T(8,128)(2,1)S(1)}, bf16[1024,2048]{1,0:T(8,128)(2,1)}, u32[]{:S(2)}) copy-start(bf16[1024,2048]{1,0:T(8,128)(2,1)} %param.8) | copy-start | bytes 12582916
  51.1 56.5 %copy-start.3 = (bf16[256,4096]{1,0:T(8,128)(2,1)S(1)}, bf16[256,4096]{1,0:T(8,128)(2,1)}, u32[]{:S(2)}) copy-start(bf16[256,4096]{1,0:T(8,128)(2,1)} %param.13) | copy-start | bytes 6291460
Sparse Core Ops, SparseCore 0:
  58.4 49.1 all-gather.2
where the time goes:
time: 119 us
  waiting for transfers between devices  49.3 us (41%)
  blocking collectives  32.1 us (27%)
  matrix products  21.6 us (18%)
  between operations  13.5 us (11%)
  other arithmetic  2.23 us (2%)
    all_gather x1, waiting for transfers between devices, body(): lax.all_gather(query[None], ('width', 'store'), axis=0, tiled=True)  49.3 us
    psum x1, blocking collectives, body(): factors = lax.psum(partial_value, 'width').astype(jnp.bfloat16)  32.1 us
    dot_general x1, matrix products, body(): lax.dot_general(flat_grads, inverse_curvature, (((1,), (1,)), ((), ())),...  7.16 us
    dot_general x1, matrix products, body(): lax.dot_general(masked, act_proj, (((1,), (0,)), ((), ())), preferred_ele...  5.17 us
    dot_general x1, matrix products, body(): jnp.einsum('wsef,rwf->ser', blocks, stored_blocks, preferred_element_type...  4.27 us
    dot_general x1, matrix products, body(): jnp.dot(activations, proj_in, preferred_element_type=jnp.float32)  3.58 us
  transfers between devices with their start and end apart: 1, of which 1 were waited for; matrix products, arithmetic and copies ran while one was open for 0% of the time, Pallas kernels for 0%

commit v1 on v0

v1 whole, which is shorter than its diff:
```python
import functools

import jax
import jax.numpy as jnp
from jax import lax
from jax.experimental import pallas as pl
from jax.experimental.pallas import tpu as pltpu
from jax.sharding import PartitionSpec as P

EX_DEV = 128
MOST = 16
LANES = 128
EX_BLOCK = LANES // MOST
F32, BF16 = jnp.float32, jnp.bfloat16
NT = (((1,), (1,)), ((), ()))
VMEM_LIMIT = 48 * 2**20


def project_kernel(planes, act_ref, grad_ref, pin_ref, pout_ref, *rest):
    outs, (win, wout) = rest[:planes], rest[planes:]
    rank = pin_ref.shape[0]
    step = pl.program_id(0)

    @pl.when(step == 0)
    def _():
        zeros = jnp.zeros_like(pin_ref)
        win[:rank, :] = pin_ref[...]
        win[rank:, :] = zeros
        wout[:rank, :] = zeros
        wout[rank:, :] = pout_ref[...]

    part = lax.dot_general(act_ref[...], win[...], NT, preferred_element_type=F32)
    part += lax.dot_general(grad_ref[...], wout[...], NT, preferred_element_type=F32)
    away = lax.rem(step - lax.axis_index("width") + planes, planes)
    for d, out in enumerate(outs):

        @pl.when(away == d)
        def _(out=out):
            out[...] = part.astype(out.dtype)


def project(activations, out_grads, proj_in, proj_out, planes):
    tokens, depth = activations.shape
    rank = proj_in.shape[1]
    quarter = tokens // planes
    whole = lambda i: (0, 0)
    return pl.pallas_call(
        functools.partial(project_kernel, planes),
        grid=(planes,),
        in_specs=[
            pl.BlockSpec((quarter, depth), lambda i: (i, 0)),
            pl.BlockSpec((quarter, depth), lambda i: (i, 0)),
            pl.BlockSpec((rank, depth), whole),
            pl.BlockSpec((rank, depth), whole),
        ],
        out_specs=[pl.BlockSpec((quarter, 2 * rank), whole)] * planes,
        out_shape=[jax.ShapeDtypeStruct((quarter, 2 * rank), BF16 if d else F32) for d in range(planes)],
        scratch_shapes=[pltpu.VMEM((2 * rank, depth), BF16)] * 2,
        compiler_params=pltpu.CompilerParams(vmem_limit_bytes=VMEM_LIMIT),
        name="project",
    )(activations, out_grads, proj_in.T, proj_out.T)


def query_kernel(pieces, parts, start_ref, ids_ref, *rest):
    factor_refs, (ic_hbm, out_ref, tok, gt, a2, outer, pe, ic, sems) = rest[:pieces], rest[pieces:]
    rank = tok.shape[1] // 2
    rows = ic.shape[0] // parts
    copies = [
        pltpu.make_async_copy(ic_hbm.at[pl.ds(j * rows, rows)], ic.at[pl.ds(j * rows, rows)], sems.at[j])
        for j in range(parts)
    ]
    for copy in copies:
        copy.start()

    piece = tok.shape[0] // pieces
    me = lax.axis_index("width") if pieces > 1 else 0
    for d, ref in enumerate(factor_refs):
        at = lax.rem(me - d + pieces, pieces) if pieces > 1 else 0
        tok[pl.ds(pl.multiple_of(at * piece, piece), piece), :] = ref[...]

    lane = lax.broadcasted_iota(jnp.int32, (LANES, 2 * rank), 1)
    for k in range(tok.shape[0] // LANES):
        both = tok[pl.ds(k * LANES, LANES), :].astype(F32)
        gt[k] = both.T[rank:, :]
        a2[pl.ds(k * LANES, LANES), :] = jnp.where(lane < rank, both, pltpu.roll(both, rank, 1)).astype(BF16)

    slot = lax.broadcasted_iota(jnp.int32, (EX_BLOCK, LANES), 0)
    low = lax.broadcasted_iota(jnp.int32, (EX_BLOCK, 2 * rank), 1) < rank
    for pair in range(EX_DEV // EX_BLOCK // 2):
        inverse = []
        for half in range(2):
            first = (2 * pair + half) * EX_BLOCK
            k = start_ref[2 * pair + half]
            id0, id1 = ids_ref[pl.ds(k, 1), :], ids_ref[pl.ds(k + 1, 1), :]
            g0, g1 = gt[k], gt[k + 1]
            left = [
                jnp.concatenate(
                    [jnp.where(id0 == first + e, g0, 0.0), jnp.where(id1 == first + e, g1, 0.0)], axis=1
                ).astype(BF16)
                for e in range(EX_BLOCK)
            ]
            window = a2[pl.ds(pl.multiple_of(k * LANES, LANES), 2 * LANES), :]
            outer[pair % 2, half] = jnp.dot(jnp.concatenate(left, axis=0), window, preferred_element_type=F32)
            hits = (id0 == first + slot).astype(F32) + (id1 == first + slot).astype(F32)
            inverse.append(1.0 / jnp.sum(hits, axis=1, keepdims=True))
        for i in range(rank // 2):
            value = [
                jnp.where(
                    low,
                    outer[pair % 2, half, pl.ds(2 * i, EX_BLOCK, stride=rank), :],
                    outer[pair % 2, half, pl.ds(2 * i + 1, EX_BLOCK, stride=rank), :],
                )
                * inverse[half]
                for half in range(2)
            ]
            pe[pl.ds(pair * 2 * EX_BLOCK, 2 * EX_BLOCK), pl.ds(i * 2 * rank, 2 * rank)] = jnp.concatenate(
                value, axis=0
            ).astype(BF16)

    for j, copy in enumerate(copies):
        copy.wait()
        out_ref[pl.ds(j * rows, rows), :] = lax.dot_general(
            ic[pl.ds(j * rows, rows), :], pe[...], NT, preferred_element_type=F32
        ).astype(BF16)


def query_transposed(factors, example_of, inverse_curvature):
    tokens = example_of.shape[1]
    chunks = tokens // LANES
    firsts = jnp.arange(0, EX_DEV, EX_BLOCK, dtype=jnp.int32)
    before = jnp.sum((example_of < firsts[:, None]).astype(jnp.int32), axis=1)
    start = jnp.minimum(before // LANES, chunks - 2)
    rank = factors[0].shape[1] // 2
    feats, width = inverse_curvature.shape
    parts = 4 if feats % 512 == 0 else 1
    vmem = pl.BlockSpec(memory_space=pltpu.VMEM)
    return pl.pallas_call(
        functools.partial(query_kernel, len(factors), parts),
        in_specs=[pl.BlockSpec(memory_space=pltpu.SMEM), vmem] + [vmem] * len(factors) + [pl.BlockSpec(memory_space=pl.ANY)],
        out_specs=vmem,
        out_shape=jax.ShapeDtypeStruct((feats, EX_DEV), BF16),
        scratch_shapes=[
            pltpu.VMEM((tokens, 2 * rank), BF16),
            pltpu.VMEM((chunks, rank, LANES), F32),
            pltpu.VMEM((tokens, 2 * rank), BF16),
            pltpu.VMEM((2, 2, EX_BLOCK * rank, 2 * rank), F32),
            pltpu.VMEM((EX_DEV, width), BF16),
            pltpu.VMEM((feats, width), BF16),
            pltpu.SemaphoreType.DMA((parts,)),
        ],
        compiler_params=pltpu.CompilerParams(vmem_limit_bytes=VMEM_LIMIT),
        name="query",
    )(start, example_of.reshape(chunks, LANES), *factors, inverse_curvature)


def scores_kernel(places, planes, spots, mine_ref, other_ref, *rest):
    blocks, (keep_ref, send_ref, acc) = rest[: len(spots)], rest[len(spots) :]
    plane, index = lax.axis_index("width"), lax.axis_index("store")
    chip = index // 2
    here = chip * planes + jnp.where(chip % 2 == 0, plane, planes - 1 - plane)
    rows = mine_ref.shape[0]
    depth = mine_ref.shape[1] // planes
    acc[...] = jnp.zeros_like(acc)
    for block, (offset, first) in zip(blocks, spots):
        there = lax.rem(here + offset + places, places)
        that_chip, rest_of = there // planes, lax.rem(there, planes)
        that_plane = jnp.where(that_chip % 2 == 0, rest_of, planes - 1 - rest_of)
        columns = pl.ds(pl.multiple_of(that_plane * depth + first, LANES), block.shape[0])
        for n, ref in enumerate((mine_ref, other_ref)):
            acc[that_chip, n] += jnp.dot(ref[:, columns], block[...], preferred_element_type=F32)
    for chip_at in range(places // planes):
        at = pl.ds(chip_at * EX_DEV, EX_DEV)
        keep_ref[at, :] = acc[chip_at, 0].T
        send_ref[at, :] = acc[chip_at, 1].T


def scores_of(stored, others, blocks, spots, places, planes):
    rows = stored.shape[0]
    chips = places // planes
    vmem = pl.BlockSpec(memory_space=pltpu.VMEM)
    return pl.pallas_call(
        functools.partial(scores_kernel, places, planes, spots),
        in_specs=[vmem] * (2 + len(blocks)),
        out_specs=[vmem] * 2,
        out_shape=[jax.ShapeDtypeStruct((chips * EX_DEV, rows), F32)] * 2,
        scratch_shapes=[pltpu.VMEM((chips, 2, rows, EX_DEV), F32)],
        compiler_params=pltpu.CompilerParams(vmem_limit_bytes=VMEM_LIMIT),
        name="scores",
    )(stored, others, *blocks)


def ring_pairs(planes, stores, step):
    walk = [(x, z if x % 2 == 0 else planes - 1 - z) for x in range(stores // 2) for z in range(planes)]
    pairs = []
    for at, (x, z) in enumerate(walk):
        to_x, to_z = walk[(at + step) % len(walk)]
        pairs += [(z * stores + 2 * x + core, to_z * stores + 2 * to_x + core) for core in range(2)]
    return pairs


def sum_over_width(parts, planes):
    total = parts[0]
    turn = lambda d: [(i, (i + d) % planes) for i in range(planes)]
    for d in range(1, planes):
        total = total + lax.ppermute(parts[d], "width", turn(d)).astype(F32)
    total = total.astype(BF16)
    return [total] + [lax.ppermute(total, "width", turn(d)) for d in range(1, planes)]


def body(activations, out_grads, example_of, proj_in, proj_out, inverse_curvature, stored):
    planes, stores = lax.axis_size("width"), lax.axis_size("store")
    if planes * stores > 32 or stores % 2:
        partial_value = jnp.concatenate(
            [
                jnp.dot(activations, proj_in, preferred_element_type=F32),
                jnp.dot(out_grads, proj_out, preferred_element_type=F32),
            ],
            axis=1,
        )
        factors = lax.psum(partial_value, "width").astype(BF16)
        query = query_transposed([factors], example_of, inverse_curvature)
        gathered = lax.all_gather(query, ("width", "store"), axis=0)
        blocks = gathered.reshape(planes, stores, query.shape[0], EX_DEV)
        stored_blocks = stored.reshape(stored.shape[0], planes, query.shape[0])
        scores = jnp.einsum("wsfe,rwf->ser", blocks, stored_blocks, preferred_element_type=F32)
        return scores.reshape(stores * EX_DEV, stored.shape[0])

    swap = [(i, i ^ 1) for i in range(stores)]
    others = lax.ppermute(stored, "store", swap)
    parts = project(activations, out_grads, proj_in, proj_out, planes)
    factors = sum_over_width(parts, planes)
    query = query_transposed(factors, example_of, inverse_curvature)

    places = planes * stores // 2
    on = lambda x: lax.ppermute(x, ("width", "store"), ring_pairs(planes, stores, 1))
    back = lambda x: lax.ppermute(x, ("width", "store"), ring_pairs(planes, stores, -1))
    blocks, spots = [query], [(0, 0)]
    ahead = behind = query
    for k in range(1, places // 2):
        ahead, behind = on(ahead), back(behind)
        blocks += [ahead, behind]
        spots += [(-k, 0), (k, 0)]
    half = query.shape[0] // 2
    blocks += [on(ahead[:half]), back(behind[half:])]
    spots += [(places // 2, 0), (places // 2, half)]

    keep, send = scores_of(stored, others, blocks, spots, places, planes)
    got = lax.ppermute(send, "store", swap)
    rows = stored.shape[0]
    core = lax.rem(lax.axis_index("store"), 2)
    keep, got = (x.reshape(stores // 2, 1, EX_DEV, rows) for x in (keep, got))
    is_first = core == 0
    both = jnp.concatenate([jnp.where(is_first, keep, got), jnp.where(is_first, got, keep)], axis=1)
    return both.reshape(stores * EX_DEV, rows)


def solution(mesh):
    return jax.shard_map(
        body,
        mesh=mesh,
        in_specs=(
            P(("groups", "store"), "width"),
            P(("groups", "store"), "width"),
            P(("groups", "store"), None),
            P("width", None),
            P("width", None),
            P("width", None),
            P(("width", "store"), None),
        ),
        out_specs=P("groups", ("width", "store")),
        check_vma=False,
    )
```

time: 119 us -> 76.2 us (0.64)
  blocking collectives: 32.1 us -> 0 us
  matrix products: 21.6 us -> 0 us
  starting transfers between devices: 0.01 us -> 19.5 us
  Pallas kernels: 0 us -> 19.2 us
  waiting for transfers between devices: 49.3 us -> 30.5 us
  between operations: 13.5 us -> 0.09 us
  local copies, waits for them, and re-layouts: 0.03 us -> 6.27 us
  other arithmetic: 2.23 us -> 0.31 us
    all_gather x1 -> x0, waiting for transfers between devices: 49.3 us -> none  [body(): lax.all_gather(query[None], ('width', 'store'), axis=0, tiled=True)]
    psum x1 -> x0, blocking collectives: 32.1 us -> none  [body(): factors = lax.psum(partial_value, 'width').astype(jnp.bfloat16)]
    ppermute x0 -> x16, waiting for transfers between devices: none -> 30.5 us  [the longest x4 18.6 us: body(): lax.ppermute(x, ('width', 'store'), ring_pairs(planes, stores, 1))]
    dot_general x5 -> x0, matrix products: 21.6 us -> none  [the longest x1 7.16 us: body(): lax.dot_general(flat_grads, inverse_curvature, (((1,), (1,)), ((), ())),...]
    ppermute x0 -> x16, starting transfers between devices: none -> 19.5 us  [the longest x4 7.82 us: body(): lax.ppermute(x, ('width', 'store'), ring_pairs(planes, stores, 1))]
    pallas_call x0 -> x3, Pallas kernels: none -> 19.2 us  [the longest x1 10.3 us: query_transposed(): pl.pallas_call(functools.partial(query_kernel, len(factors), parts), in_s...]
    unnamed x8 -> x12, local copies, waits for them, and re-layouts: 0.02 us -> 5.42 us
    eq x1 -> x0, other arithmetic: 1.21 us -> none  [body(): member = token_ids[None, :] == jnp.arange(EX_DEV, dtype=jnp.int32)[:, None]]
  transfers between devices with their start and end apart: 1 -> 16, of which waited for: 1 -> 12; matrix products, arithmetic and copies ran while one was open for 0% -> 0% of each run, Pallas kernels for 0% -> 20%
where the time goes in v1:
time: 76.2 us; the launch traced here: 75.9 us
  waiting for transfers between devices  30.5 us (40%)
  starting transfers between devices  19.5 us (26%)
  Pallas kernels  19.2 us (25%)
  local copies, waits for them, and re-layouts  6.27 us (8%)
    ppermute x4, waiting for transfers between devices, body(): lax.ppermute(x, ('width', 'store'), ring_pairs(planes, stores, 1))  18.6 us
    pallas_call x1, Pallas kernels, query_transposed(): pl.pallas_call(functools.partial(query_kernel, len(factors), parts), in_s...  10.3 us
    ppermute x4, starting transfers between devices, body(): lax.ppermute(x, ('width', 'store'), ring_pairs(planes, stores, 1))  7.82 us
    ppermute x3, starting transfers between devices, sum_over_width(): total = total + lax.ppermute(parts[d], 'width', turn(d)).astype(F32)  6.56 us
    unnamed x12, local copies, waits for them, and re-layouts  5.42 us
    pallas_call x1, Pallas kernels, project(): pl.pallas_call(functools.partial(project_kernel, planes), grid=(planes,),...  4.8 us
    ppermute x3, waiting for transfers between devices, sum_over_width(): lax.ppermute(total, 'width', turn(d))  4.46 us
    pallas_call x1, Pallas kernels, scores_of(): pl.pallas_call(functools.partial(scores_kernel, places, planes, spots), i...  4.15 us
  transfers between devices with their start and end apart: 16, of which 12 were waited for; matrix products, arithmetic and copies ran while one was open for 0% of the time, Pallas kernels for 20%

profile of v1, /device:TPU:0, one launch (start us, length us, event | category | flops | bytes accessed | tf_op | source)
XLA Modules:
  0.0 75.9 jit_solution(13009216336359778199)
XLA Ops:
  0.0 0.5 collective-permute-start
  0.5 0.0 copy-start
  0.5 2.2 %copy-done = bf16[1024,2048]{1,0:T(8,128)(2,1)S(1)} copy-done((bf16[1024,2048]{1,0:T(8,128)(2,1)S(1)}, bf16[1024,2048]{1,0:T(8,128)(2,1)}, u32[]{:S(2)}) %copy-start) | copy-done | bytes 4194328
  2.6 0.0 copy-start.2
  2.6 0.9 %copy-done.2 = bf16[2048,64]{0,1:T(8,128)(2,1)S(1)} copy-done((bf16[2048,64]{0,1:T(8,128)(2,1)S(1)}, bf16[2048,64]{0,1:T(8,128)(2,1)}, u32[]{:S(2)}) %copy-start.2) | copy-done | bytes 262168
  3.6 0.0 copy-start.3
  3.6 0.9 %copy-done.3 = bf16[2048,64]{0,1:T(8,128)(2,1)S(1)} copy-done((bf16[2048,64]{0,1:T(8,128)(2,1)S(1)}, bf16[2048,64]{0,1:T(8,128)(2,1)}, u32[]{:S(2)}) %copy-start.3) | copy-done | bytes 262168
  4.5 0.0 copy-start.4
  4.5 4.8 %project.1 = (f32[256,128]{1,0:T(8,128)S(1)}, bf16[256,128]{1,0:T(8,128)(2,1)S(1)}, bf16[256,128]{1,0:T(8,128)(2,1)S(1)}, bf16[256,128]{1,0:T(8,128)(2,1)S(1)}) custom-call(bf16[1024,2048]{1,0:T(8,128)(2,1)S(1)} %copy-done, bf16[1024,2048]{1,0:T(8,128)(2,1)} %grad_ref.1, bf16[64,2048]{1,0:T(8,128)(2,1)S(1)} %bitcast.7, bf16[64,2048]{1,0:T(8,128)(2,1)S(1)} %bitcast.8), custom_call_target="tpu_custom_call" | custom-call | tf_op jit(solution)/shard_map/project/pallas_call | solution.py:47
  9.4 2.6 %collective-permute-start.1 = (bf16[256,128]{1,0:T(8,128)(2,1)S(1)}, bf16[256,128]{1,0:T(8,128)(2,1)S(1)}, u32[]{:S(2)}, u32[]{:S(2)}) collective-permute-start(bf16[256,128]{1,0:T(8,128)(2,1)S(1)} %get-tuple-element.12), channel_id=1, source_target_pairs={{0,4},{4,8},{8,12},{12,0},{1,5},{5,9},{9,13},{13,1},{2,6},{6,10},{... | collective-permute-start | bytes 196616 | tf_op jit(solution)/shard_map/ppermute | solution.py:205
  12.0 2.6 %collective-permute-start.2 = (bf16[256,128]{1,0:T(8,128)(2,1)S(1)}, bf16[256,128]{1,0:T(8,128)(2,1)S(1)}, u32[]{:S(2)}, u32[]{:S(2)}) collective-permute-start(bf16[256,128]{1,0:T(8,128)(2,1)S(1)} %get-tuple-element.13), channel_id=1, source_target_pairs={{0,8},{4,12},{8,0},{12,4},{1,9},{5,13},{9,1},{13,5},{2,10},{6,14},... | collective-permute-start | bytes 196616 | tf_op jit(solution)/shard_map/ppermute | solution.py:205
  14.6 1.3 %collective-permute-start.3 = (bf16[256,128]{1,0:T(8,128)(2,1)S(1)}, bf16[256,128]{1,0:T(8,128)(2,1)S(1)}, u32[]{:S(2)}, u32[]{:S(2)}) collective-permute-start(bf16[256,128]{1,0:T(8,128)(2,1)S(1)} %get-tuple-element.14), channel_id=1, source_target_pairs={{0,12},{4,0},{8,4},{12,8},{1,13},{5,1},{9,5},{13,9},{2,14},{6,2},{... | collective-permute-start | bytes 196616 | tf_op jit(solution)/shard_map/ppermute | solution.py:205
  15.9 0.0 copy-done.4
  15.9 0.2 convert_reduce_fusion
  16.1 0.8 %collective-permute-done.1 = bf16[256,128]{1,0:T(8,128)(2,1)S(1)} collective-permute-done((bf16[256,128]{1,0:T(8,128)(2,1)S(1)}, bf16[256,128]{1,0:T(8,128)(2,1)S(1)}, u32[]{:S(2)}, u32[]{:S(2)}) %collective-permute-start.1) | collective-permute-done | bytes 65568 | tf_op jit(solution)/shard_map/ppermute | solution.py:205
  16.9 2.8 %collective-permute-done.2 = bf16[256,128]{1,0:T(8,128)(2,1)S(1)} collective-permute-done((bf16[256,128]{1,0:T(8,128)(2,1)S(1)}, bf16[256,128]{1,0:T(8,128)(2,1)S(1)}, u32[]{:S(2)}, u32[]{:S(2)}) %collective-permute-start.2) | collective-permute-done | bytes 65568 | tf_op jit(solution)/shard_map/ppermute | solution.py:205
  19.7 0.2 collective-permute-done.3
  20.0 1.7 %collective-permute-start.4 = (bf16[256,128]{1,0:T(8,128)(2,1)S(1)}, bf16[256,128]{1,0:T(8,128)(2,1)S(1)}, u32[]{:S(2)}, u32[]{:S(2)}) collective-permute-start(bf16[256,128]{1,0:T(8,128)(2,1)S(1)} %add_convert_fusion.rest_0_), channel_id=1, source_target_pairs={{0,4},{4,8},{8,12},{12,0},{1,5},{5,9},{9,13},{13,1},{2,6},{6,10},{... | collective-permute-start | bytes 196616 | tf_op jit(solution)/shard_map/ppermute | solution.py:207
  21.6 1.6 %collective-permute-start.5 = (bf16[256,128]{1,0:T(8,128)(2,1)S(1)}, bf16[256,128]{1,0:T(8,128)(2,1)S(1)}, u32[]{:S(2)}, u32[]{:S(2)}) collective-permute-start(bf16[256,128]{1,0:T(8,128)(2,1)S(1)} %add_convert_fusion.rest_0_), channel_id=1, source_target_pairs={{0,8},{4,12},{8,0},{12,4},{1,9},{5,13},{9,1},{13,5},{2,10},{6,14},... | collective-permute-start | bytes 196616 | tf_op jit(solution)/shard_map/ppermute | solution.py:207
  23.3 0.8 %collective-permute-start.6 = (bf16[256,128]{1,0:T(8,128)(2,1)S(1)}, bf16[256,128]{1,0:T(8,128)(2,1)S(1)}, u32[]{:S(2)}, u32[]{:S(2)}) collective-permute-start(bf16[256,128]{1,0:T(8,128)(2,1)S(1)} %add_convert_fusion.rest_0_), channel_id=1, source_target_pairs={{0,12},{4,0},{8,4},{12,8},{1,13},{5,1},{9,5},{13,9},{2,14},{6,2},{... | collective-permute-start | bytes 196616 | tf_op jit(solution)/shard_map/ppermute | solution.py:207
  24.1 2.4 %collective-permute-done.4.rest_1_ = bf16[256,128]{1,0:T(8,128)(2,1)S(1)} collective-permute-done((bf16[256,128]{1,0:T(8,128)(2,1)S(1)}, bf16[256,128]{1,0:T(8,128)(2,1)S(1)}, u32[]{:S(2)}, u32[]{:S(2)}) %collective-permute-start.4) | collective-permute-done | bytes 65568 | tf_op jit(solution)/shard_map/ppermute | solution.py:207
  26.4 2.0 %collective-permute-done.5.rest_2_ = bf16[256,128]{1,0:T(8,128)(2,1)S(1)} collective-permute-done((bf16[256,128]{1,0:T(8,128)(2,1)S(1)}, bf16[256,128]{1,0:T(8,128)(2,1)S(1)}, u32[]{:S(2)}, u32[]{:S(2)}) %collective-permute-start.5) | collective-permute-done | bytes 65568 | tf_op jit(solution)/shard_map/ppermute | solution.py:207
  28.4 0.1 collective-permute-done.6.rest_3_
  28.6 0.0 copy-start.1
  28.6 10.3 %query.1.rest_0_ = bf16[1024,128]{1,0:T(8,128)(2,1)S(1)} custom-call(s32[16]{0:T(128)S(1)} %fusion.start_ref, s32[8,128]{1,0:T(8,128)S(1)} %bitcast.10, bf16[256,128]{1,0:T(8,128)(2,1)S(1)} %add_convert_fusion.rest_0_, bf16[256,128]{1,0:T(8,128)(2,1)S(1)} %collective-permute-done.4.rest_1_, bf16[256,128]{1,0:T(8,128)(2,1)S(1)} %collective-permute-done.5.rest_2_, ...), custom_call_target="tpu_custom_call" | custom-call | tf_op jit(solution)/shard_map/query/pallas_call | solution.py:137
  38.8 1.8 %collective-permute-start.7 = (bf16[1024,128]{1,0:T(8,128)(2,1)S(1)}, bf16[1024,128]{1,0:T(8,128)(2,1)S(1)}, u32[]{:S(2)}, u32[]{:S(2)}) collective-permute-start(bf16[1024,128]{1,0:T(8,128)(2,1)S(1)} %query.1.rest_0_), channel_id=1, source_target_pairs={{0,4},{1,5},{4,8},{5,9},{8,12},{9,13},{12,14},{13,15},{14,10},{15,... | collective-permute-start | bytes 786440 | tf_op jit(solution)/shard_map/ppermute | solution.py:235
  40.6 0.3 collective-permute-start.8
  40.9 6.0 %collective-permute-done.7.rest_1_ = bf16[1024,128]{1,0:T(8,128)(2,1)S(1)} collective-permute-done((bf16[1024,128]{1,0:T(8,128)(2,1)S(1)}, bf16[1024,128]{1,0:T(8,128)(2,1)S(1)}, u32[]{:S(2)}, u32[]{:S(2)}) %collective-permute-start.7) | collective-permute-done | bytes 262176 | tf_op jit(solution)/shard_map/ppermute | solution.py:235
  46.9 2.0 %collective-permute-start.9 = (bf16[1024,128]{1,0:T(8,128)(2,1)S(1)}, bf16[1024,128]{1,0:T(8,128)(2,1)S(1)}, u32[]{:S(2)}, u32[]{:S(2)}) collective-permute-start(bf16[1024,128]{1,0:T(8,128)(2,1)S(1)} %collective-permute-done.7.rest_1_), channel_id=1, source_target_pairs={{0,4},{1,5},{4,8},{5,9},{8,12},{9,13},{12,14},{13,15},{14,10},{15,... | collective-permute-start | bytes 786440 | tf_op jit(solution)/shard_map/ppermute | solution.py:235
  48.9 0.0 collective-permute-done.8.rest_2_
  48.9 0.1 collective-permute-start.10
  48.9 5.3 %collective-permute-done.9.rest_3_ = bf16[1024,128]{1,0:T(8,128)(2,1)S(1)} collective-permute-done((bf16[1024,128]{1,0:T(8,128)(2,1)S(1)}, bf16[1024,128]{1,0:T(8,128)(2,1)S(1)}, u32[]{:S(2)}, u32[]{:S(2)}) %collective-permute-start.9) | collective-permute-done | bytes 262176 | tf_op jit(solution)/shard_map/ppermute | solution.py:235
  54.3 2.0 %collective-permute-start.11 = (bf16[1024,128]{1,0:T(8,128)(2,1)S(1)}, bf16[1024,128]{1,0:T(8,128)(2,1)S(1)}, u32[]{:S(2)}, u32[]{:S(2)}) collective-permute-start(bf16[1024,128]{1,0:T(8,128)(2,1)S(1)} %collective-permute-done.9.rest_3_), channel_id=1, source_target_pairs={{0,4},{1,5},{4,8},{5,9},{8,12},{9,13},{12,14},{13,15},{14,10},{15,... | collective-permute-start | bytes 786440 | tf_op jit(solution)/shard_map/ppermute | solution.py:235
  56.3 0.0 collective-permute-done.10.rest_4_
  56.3 0.0 collective-permute-start.12
  56.3 4.4 %collective-permute-done.11.rest_5_ = bf16[1024,128]{1,0:T(8,128)(2,1)S(1)} collective-permute-done((bf16[1024,128]{1,0:T(8,128)(2,1)S(1)}, bf16[1024,128]{1,0:T(8,128)(2,1)S(1)}, u32[]{:S(2)}, u32[]{:S(2)}) %collective-permute-start.11) | collective-permute-done | bytes 262176 | tf_op jit(solution)/shard_map/ppermute | solution.py:235
  60.7 2.1 %collective-permute-start.13 = (bf16[512,128]{1,0:T(8,128)(2,1)S(1)}, bf16[512,128]{1,0:T(8,128)(2,1)S(1)}, u32[]{:S(2)}, u32[]{:S(2)}) collective-permute-start(bf16[512,128]{1,0:T(8,128)(2,1)S(1)} %slice.8), channel_id=1, source_target_pairs={{0,4},{1,5},{4,8},{5,9},{8,12},{9,13},{12,14},{13,15},{14,10},{15,... | collective-permute-start | bytes 393224 | tf_op jit(solution)/shard_map/ppermute | solution.py:235
  62.8 0.0 collective-permute-done.12.rest_6_
  62.8 0.1 collective-permute-start.14
  62.9 2.9 %collective-permute-done.13.rest_7_ = bf16[512,128]{1,0:T(8,128)(2,1)S(1)} collective-permute-done((bf16[512,128]{1,0:T(8,128)(2,1)S(1)}, bf16[512,128]{1,0:T(8,128)(2,1)S(1)}, u32[]{:S(2)}, u32[]{:S(2)}) %collective-permute-start.13) | collective-permute-done | bytes 131104 | tf_op jit(solution)/shard_map/ppermute | solution.py:235
  65.8 2.1 %collective-permute-done.14.rest_8_ = bf16[512,128]{1,0:T(8,128)(2,1)S(1)} collective-permute-done((bf16[512,128]{1,0:T(8,128)(2,1)S(1)}, bf16[512,128]{1,0:T(8,128)(2,1)S(1)}, u32[]{:S(2)}, u32[]{:S(2)}) %collective-permute-start.14) | collective-permute-done | bytes 131104 | tf_op jit(solution)/shard_map/ppermute | solution.py:236
  67.8 0.0 collective-permute-done.other_ref
  67.8 1.3 %copy-done.5 = bf16[256,4096]{1,0:T(8,128)(2,1)} copy-done((bf16[256,4096]{1,0:T(8,128)(2,1)}, bf16[256,4096]{1,0:T(8,128)(2,1)S(1)}, u32[]{:S(2)}) %copy-start.5) | copy-done | bytes 2097176
  69.2 0.0 copy-done.1
  69.2 4.2 %scores.1 = (f32[256,256]{1,0:T(8,128)S(1)}, f32[256,256]{1,0:T(8,128)S(1)}) custom-call(bf16[256,4096]{1,0:T(8,128)(2,1)S(1)} %copy-done.1, bf16[256,4096]{1,0:T(8,128)(2,1)} %copy-done.5, bf16[1024,128]{1,0:T(8,128)(2,1)S(1)} %query.1.rest_0_, bf16[1024,128]{1,0:T(8,128)(2,1)S(1)} %collective-permute-done.7.rest_1_, ...), custom_call_target="tpu_custom_call" | custom-call | tf_op jit(solution)/shard_map/scores/pallas_call | solution.py:181
  73.3 0.1 collective-permute-start.15
  73.4 1.5 %collective-permute-done.15 = f32[256,256]{1,0:T(8,128)S(1)} collective-permute-done((f32[256,256]{1,0:T(8,128)S(1)}, f32[256,256]{1,0:T(8,128)S(1)}, u32[]{:S(2)}, u32[]{:S(2)}) %collective-permute-start.15) | collective-permute-done | bytes 262176 | tf_op jit(solution)/shard_map/ppermute | solution.py:248
  75.0 0.8 %copy.9 = f32[2,2,128,256]{3,2,1,0:T(8,128)} copy(f32[2,2,128,256]{3,2,0,1:T(8,128)S(1)} %pad_maximum_fusion) | data formatting | bytes 1048576 | tf_op jit(solution)/shard_map/concatenate | solution.py:253
  (8 shorter events, 0.1 us)
Async XLA Ops:
  0.0 67.8 %collective-permute-start = (bf16[256,4096]{1,0:T(8,128)(2,1)}, bf16[256,4096]{1,0:T(8,128)(2,1)S(1)}, u32[]{:S(2)}, u32[]{:S(2)}) collective-permute-start(bf16[256,4096]{1,0:T(8,128)(2,1)} %mine_ref.1), channel_id=1, source_target_pairs={{0,1},{1,0},{2,3},{3,2},{4,5},{5,4},{6,7},{7,6},{8,9},{9,8},{10,11... | collective-permute-start | bytes 6291464 | tf_op jit(solution)/shard_map/ppermute | solution.py:229
  0.5 2.2 %copy-start = (bf16[1024,2048]{1,0:T(8,128)(2,1)S(1)}, bf16[1024,2048]{1,0:T(8,128)(2,1)}, u32[]{:S(2)}) copy-start(bf16[1024,2048]{1,0:T(8,128)(2,1)} %act_ref.1) | copy-start | bytes 12582916
  2.6 0.9 %copy-start.2 = (bf16[2048,64]{0,1:T(8,128)(2,1)S(1)}, bf16[2048,64]{0,1:T(8,128)(2,1)}, u32[]{:S(2)}) copy-start(bf16[2048,64]{0,1:T(8,128)(2,1)} %param.10) | copy-start | bytes 786436
  3.6 0.9 %copy-start.3 = (bf16[2048,64]{0,1:T(8,128)(2,1)S(1)}, bf16[2048,64]{0,1:T(8,128)(2,1)}, u32[]{:S(2)}) copy-start(bf16[2048,64]{0,1:T(8,128)(2,1)} %param.11) | copy-start | bytes 786436
  4.5 11.4 %copy-start.4 = (s32[1,1024]{1,0:T(1,128)S(1)}, s32[1,1024]{1,0:T(1,128)}, u32[]{:S(2)}) copy-start(s32[1,1024]{1,0:T(1,128)} %param.9) | copy-start | bytes 12292
  9.4 7.5 %collective-permute-start.1 = (bf16[256,128]{1,0:T(8,128)(2,1)S(1)}, bf16[256,128]{1,0:T(8,128)(2,1)S(1)}, u32[]{:S(2)}, u32[]{:S(2)}) collective-permute-start(bf16[256,128]{1,0:T(8,128)(2,1)S(1)} %get-tuple-element.12), channel_id=1, source_target_pairs={{0,4},{4,8},{8,12},{12,0},{1,5},{5,9},{9,13},{13,1},{2,6},{6,10},{... | collective-permute-start | bytes 196616 | tf_op jit(solution)/shard_map/ppermute | solution.py:205
  12.0 7.7 %collective-permute-start.2 = (bf16[256,128]{1,0:T(8,128)(2,1)S(1)}, bf16[256,128]{1,0:T(8,128)(2,1)S(1)}, u32[]{:S(2)}, u32[]{:S(2)}) collective-permute-start(bf16[256,128]{1,0:T(8,128)(2,1)S(1)} %get-tuple-element.13), channel_id=1, source_target_pairs={{0,8},{4,12},{8,0},{12,4},{1,9},{5,13},{9,1},{13,5},{2,10},{6,14},... | collective-permute-start | bytes 196616 | tf_op jit(solution)/shard_map/ppermute | solution.py:205
  14.6 5.4 %collective-permute-start.3 = (bf16[256,128]{1,0:T(8,128)(2,1)S(1)}, bf16[256,128]{1,0:T(8,128)(2,1)S(1)}, u32[]{:S(2)}, u32[]{:S(2)}) collective-permute-start(bf16[256,128]{1,0:T(8,128)(2,1)S(1)} %get-tuple-element.14), channel_id=1, source_target_pairs={{0,12},{4,0},{8,4},{12,8},{1,13},{5,1},{9,5},{13,9},{2,14},{6,2},{... | collective-permute-start | bytes 196616 | tf_op jit(solution)/shard_map/ppermute | solution.py:205
  20.0 6.5 %collective-permute-start.4 = (bf16[256,128]{1,0:T(8,128)(2,1)S(1)}, bf16[256,128]{1,0:T(8,128)(2,1)S(1)}, u32[]{:S(2)}, u32[]{:S(2)}) collective-permute-start(bf16[256,128]{1,0:T(8,128)(2,1)S(1)} %add_convert_fusion.rest_0_), channel_id=1, source_target_pairs={{0,4},{4,8},{8,12},{12,0},{1,5},{5,9},{9,13},{13,1},{2,6},{6,10},{... | collective-permute-start | bytes 196616 | tf_op jit(solution)/shard_map/ppermute | solution.py:207
  21.6 6.8 %collective-permute-start.5 = (bf16[256,128]{1,0:T(8,128)(2,1)S(1)}, bf16[256,128]{1,0:T(8,128)(2,1)S(1)}, u32[]{:S(2)}, u32[]{:S(2)}) collective-permute-start(bf16[256,128]{1,0:T(8,128)(2,1)S(1)} %add_convert_fusion.rest_0_), channel_id=1, source_target_pairs={{0,8},{4,12},{8,0},{12,4},{1,9},{5,13},{9,1},{13,5},{2,10},{6,14},... | collective-permute-start | bytes 196616 | tf_op jit(solution)/shard_map/ppermute | solution.py:207
  23.3 5.3 %collective-permute-start.6 = (bf16[256,128]{1,0:T(8,128)(2,1)S(1)}, bf16[256,128]{1,0:T(8,128)(2,1)S(1)}, u32[]{:S(2)}, u32[]{:S(2)}) collective-permute-start(bf16[256,128]{1,0:T(8,128)(2,1)S(1)} %add_convert_fusion.rest_0_), channel_id=1, source_target_pairs={{0,12},{4,0},{8,4},{12,8},{1,13},{5,1},{9,5},{13,9},{2,14},{6,2},{... | collective-permute-start | bytes 196616 | tf_op jit(solution)/shard_map/ppermute | solution.py:207
  28.6 40.6 %copy-start.1 = (bf16[256,4096]{1,0:T(8,128)(2,1)S(1)}, bf16[256,4096]{1,0:T(8,128)(2,1)}, u32[]{:S(2)}) copy-start(bf16[256,4096]{1,0:T(8,128)(2,1)} %mine_ref.1) | copy-start | bytes 6291460
  38.8 8.1 %collective-permute-start.7 = (bf16[1024,128]{1,0:T(8,128)(2,1)S(1)}, bf16[1024,128]{1,0:T(8,128)(2,1)S(1)}, u32[]{:S(2)}, u32[]{:S(2)}) collective-permute-start(bf16[1024,128]{1,0:T(8,128)(2,1)S(1)} %query.1.rest_0_), channel_id=1, source_target_pairs={{0,4},{1,5},{4,8},{5,9},{8,12},{9,13},{12,14},{13,15},{14,10},{15,... | collective-permute-start | bytes 786440 | tf_op jit(solution)/shard_map/ppermute | solution.py:235
  40.6 8.2 %collective-permute-start.8 = (bf16[1024,128]{1,0:T(8,128)(2,1)S(1)}, bf16[1024,128]{1,0:T(8,128)(2,1)S(1)}, u32[]{:S(2)}, u32[]{:S(2)}) collective-permute-start(bf16[1024,128]{1,0:T(8,128)(2,1)S(1)} %query.1.rest_0_), channel_id=1, source_target_pairs={{0,2},{1,3},{4,0},{5,1},{8,4},{9,5},{12,8},{13,9},{14,12},{15,13},... | collective-permute-start | bytes 786440 | tf_op jit(solution)/shard_map/ppermute | solution.py:236
  46.9 7.3 %collective-permute-start.9 = (bf16[1024,128]{1,0:T(8,128)(2,1)S(1)}, bf16[1024,128]{1,0:T(8,128)(2,1)S(1)}, u32[]{:S(2)}, u32[]{:S(2)}) collective-permute-start(bf16[1024,128]{1,0:T(8,128)(2,1)S(1)} %collective-permute-done.7.rest_1_), channel_id=1, source_target_pairs={{0,4},{1,5},{4,8},{5,9},{8,12},{9,13},{12,14},{13,15},{14,10},{15,... | collective-permute-start | bytes 786440 | tf_op jit(solution)/shard_map/ppermute | solution.py:235
  48.9 7.4 %collective-permute-start.10 = (bf16[1024,128]{1,0:T(8,128)(2,1)S(1)}, bf16[1024,128]{1,0:T(8,128)(2,1)S(1)}, u32[]{:S(2)}, u32[]{:S(2)}) collective-permute-start(bf16[1024,128]{1,0:T(8,128)(2,1)S(1)} %collective-permute-done.8.rest_2_), channel_id=1, source_target_pairs={{0,2},{1,3},{4,0},{5,1},{8,4},{9,5},{12,8},{13,9},{14,12},{15,13},... | collective-permute-start | bytes 786440 | tf_op jit(solution)/shard_map/ppermute | solution.py:236
  54.3 6.5 %collective-permute-start.11 = (bf16[1024,128]{1,0:T(8,128)(2,1)S(1)}, bf16[1024,128]{1,0:T(8,128)(2,1)S(1)}, u32[]{:S(2)}, u32[]{:S(2)}) collective-permute-start(bf16[1024,128]{1,0:T(8,128)(2,1)S(1)} %collective-permute-done.9.rest_3_), channel_id=1, source_target_pairs={{0,4},{1,5},{4,8},{5,9},{8,12},{9,13},{12,14},{13,15},{14,10},{15,... | collective-permute-start | bytes 786440 | tf_op jit(solution)/shard_map/ppermute | solution.py:235
  56.3 6.5 %collective-permute-start.12 = (bf16[1024,128]{1,0:T(8,128)(2,1)S(1)}, bf16[1024,128]{1,0:T(8,128)(2,1)S(1)}, u32[]{:S(2)}, u32[]{:S(2)}) collective-permute-start(bf16[1024,128]{1,0:T(8,128)(2,1)S(1)} %collective-permute-done.10.rest_4_), channel_id=1, source_target_pairs={{0,2},{1,3},{4,0},{5,1},{8,4},{9,5},{12,8},{13,9},{14,12},{15,13},... | collective-permute-start | bytes 786440 | tf_op jit(solution)/shard_map/ppermute | solution.py:236
  60.7 5.0 %collective-permute-start.13 = (bf16[512,128]{1,0:T(8,128)(2,1)S(1)}, bf16[512,128]{1,0:T(8,128)(2,1)S(1)}, u32[]{:S(2)}, u32[]{:S(2)}) collective-permute-start(bf16[512,128]{1,0:T(8,128)(2,1)S(1)} %slice.8), channel_id=1, source_target_pairs={{0,4},{1,5},{4,8},{5,9},{8,12},{9,13},{12,14},{13,15},{14,10},{15,... | collective-permute-start | bytes 393224 | tf_op jit(solution)/shard_map/ppermute | solution.py:235
  62.8 5.0 %collective-permute-start.14 = (bf16[512,128]{1,0:T(8,128)(2,1)S(1)}, bf16[512,128]{1,0:T(8,128)(2,1)S(1)}, u32[]{:S(2)}, u32[]{:S(2)}) collective-permute-start(bf16[512,128]{1,0:T(8,128)(2,1)S(1)} %slice.9), channel_id=1, source_target_pairs={{0,2},{1,3},{4,0},{5,1},{8,4},{9,5},{12,8},{13,9},{14,12},{15,13},... | collective-permute-start | bytes 393224 | tf_op jit(solution)/shard_map/ppermute | solution.py:236
  67.8 1.3 %copy-start.5 = (bf16[256,4096]{1,0:T(8,128)(2,1)}, bf16[256,4096]{1,0:T(8,128)(2,1)S(1)}, u32[]{:S(2)}) copy-start(bf16[256,4096]{1,0:T(8,128)(2,1)S(1)} %collective-permute-done.other_ref) | copy-start | bytes 6291460
  73.3 1.6 %collective-permute-start.15 = (f32[256,256]{1,0:T(8,128)S(1)}, f32[256,256]{1,0:T(8,128)S(1)}, u32[]{:S(2)}, u32[]{:S(2)}) collective-permute-start(f32[256,256]{1,0:T(8,128)S(1)} %get-tuple-element.16), channel_id=1, source_target_pairs={{0,1},{1,0},{2,3},{3,2},{4,5},{5,4},{6,7},{7,6},{8,9},{9,8},{10,11... | collective-permute-start | bytes 786440 | tf_op jit(solution)/shard_map/ppermute | solution.py:248

commit v2 on v0

v2 whole, which is shorter than its diff:
```python
import functools

import jax
import jax.numpy as jnp
from jax import lax
from jax.experimental import pallas as pl
from jax.experimental.pallas import tpu as pltpu
from jax.sharding import PartitionSpec as P

EX_DEV = 128
MOST = 16
LANES = 128
EX_BLOCK = LANES // MOST
F32, BF16 = jnp.float32, jnp.bfloat16
NT = (((1,), (1,)), ((), ()))
MIB = 2**20


def project_kernel(planes, act_hbm, grad_hbm, pin_hbm, pout_hbm, *rest):
    outs, (act, grad, win, wout, weight, sems) = rest[:planes], rest[planes:]
    rank = pin_hbm.shape[0]
    rows = act.shape[0] // planes
    loads = [
        pltpu.make_async_copy(pin_hbm, win.at[pl.ds(0, rank)], sems.at[0]),
        pltpu.make_async_copy(pout_hbm, wout.at[pl.ds(rank, rank)], sems.at[1]),
    ]
    copies = [
        [
            pltpu.make_async_copy(hbm.at[pl.ds(i * rows, rows)], ref.at[pl.ds(i * rows, rows)], sems.at[2 + 2 * i + n])
            for n, (hbm, ref) in enumerate(((act_hbm, act), (grad_hbm, grad)))
        ]
        for i in range(planes)
    ]
    for copy in sum(copies, loads):
        copy.start()
    win[rank:, :] = jnp.zeros(win[rank:, :].shape, BF16)
    wout[:rank, :] = jnp.zeros(wout[:rank, :].shape, BF16)
    for copy in loads:
        copy.wait()
    weight[0] = win[...].T
    weight[1] = wout[...].T
    me = lax.axis_index("width")
    for i, pair in enumerate(copies):
        away = lax.rem(i - me + planes, planes)
        at = pl.ds(i * rows, rows)
        for copy in pair:
            copy.wait()
        part = jnp.dot(act[at, :], weight[0], preferred_element_type=F32)
        part += jnp.dot(grad[at, :], weight[1], preferred_element_type=F32)
        for d, out in enumerate(outs):

            @pl.when(away == d)
            def _(out=out, part=part):
                out[...] = part.astype(out.dtype)


def project(activations, out_grads, proj_in, proj_out, planes):
    tokens, depth = activations.shape
    rank = proj_in.shape[1]
    quarter = tokens // planes
    return pl.pallas_call(
        functools.partial(project_kernel, planes),
        in_specs=[pl.BlockSpec(memory_space=pltpu.HBM)] * 4,
        out_specs=[pl.BlockSpec(memory_space=pltpu.VMEM)] * planes,
        out_shape=[jax.ShapeDtypeStruct((quarter, 2 * rank), BF16 if d else F32) for d in range(planes)],
        scratch_shapes=[
            pltpu.VMEM((tokens, depth), BF16),
            pltpu.VMEM((tokens, depth), BF16),
            pltpu.VMEM((2 * rank, depth), BF16),
            pltpu.VMEM((2 * rank, depth), BF16),
            pltpu.VMEM((2, depth, 2 * rank), BF16),
            pltpu.SemaphoreType.DMA((2 + 2 * planes,)),
        ],
        compiler_params=pltpu.CompilerParams(vmem_limit_bytes=60 * MIB),
        name="project",
    )(activations, out_grads, proj_in.T, proj_out.T)


def query_kernel(pieces, start_ref, ids_ref, *rest):
    factor_refs, (ic_ref, *outs), (tok, spread, twice, pe) = rest[:pieces], rest[pieces:-4], rest[-4:]
    tokens, rank = tok.shape[0], tok.shape[1] // 2
    piece = tokens // pieces
    me = lax.axis_index("width") if pieces > 1 else 0
    for d, ref in enumerate(factor_refs):
        at = lax.rem(me - d + pieces, pieces) if pieces > 1 else 0
        tok[pl.ds(pl.multiple_of(at * piece, piece), piece), :] = ref[...]

    entry = lax.broadcasted_iota(jnp.int32, (EX_BLOCK * rank, 2 * rank), 0) // EX_BLOCK + rank
    column = lax.broadcasted_iota(jnp.int32, (EX_BLOCK * rank, 2 * rank), 1)
    pick = (entry == column).astype(F32).astype(BF16)
    source = lax.broadcasted_iota(jnp.int32, (2 * rank, 2 * rank), 0)
    target = lax.broadcasted_iota(jnp.int32, (2 * rank, 2 * rank), 1) % rank
    double = (source == target).astype(F32).astype(BF16)
    spread[...] = lax.dot_general(pick, tok[...], NT, preferred_element_type=F32).astype(BF16)
    twice[...] = jnp.dot(tok[...], double, preferred_element_type=F32).astype(BF16)

    slot = lax.broadcasted_iota(jnp.int32, (EX_BLOCK, 2 * LANES), 0)
    low = lax.broadcasted_iota(jnp.int32, (EX_BLOCK, 2 * rank), 1) < rank
    for pair in range(EX_DEV // EX_BLOCK // 2):
        halves = []
        for block in (2 * pair, 2 * pair + 1):
            k = start_ref[block]
            ids = jnp.concatenate([ids_ref[pl.ds(k, 1), :], ids_ref[pl.ds(k + 1, 1), :]], axis=1)
            hits = (ids == block * EX_BLOCK + slot).astype(F32)
            mask = jnp.concatenate([hits, hits], axis=0).astype(BF16)
            at = pl.multiple_of(k * LANES, LANES)
            left = spread[:, pl.ds(at, 2 * LANES)].reshape(rank // 2, 2 * EX_BLOCK, 2 * LANES) * mask[None]
            left = left.reshape(rank * EX_BLOCK, 2 * LANES)
            outer = jnp.dot(left, twice[pl.ds(at, 2 * LANES), :], preferred_element_type=F32)
            outer = outer.reshape(rank // 2, 2, EX_BLOCK, 2 * rank)
            inverse = 1.0 / jnp.sum(hits, axis=1, keepdims=True)
            halves.append(jnp.where(low[None], outer[:, 0], outer[:, 1]) * inverse[None])
        both = jnp.concatenate(halves, axis=1).astype(BF16)
        for i in range(rank // 2):
            pe[pl.ds(pair * 2 * EX_BLOCK, 2 * EX_BLOCK), pl.ds(i * 2 * rank, 2 * rank)] = both[i]

    rows = ic_ref.shape[0] // len(outs)
    for j, out in enumerate(outs):
        out[...] = lax.dot_general(
            ic_ref[pl.ds(j * rows, rows), :], pe[...], NT, preferred_element_type=F32
        ).astype(BF16)


def query_transposed(factors, example_of, inverse_curvature, cuts):
    tokens = example_of.shape[1]
    chunks = tokens // LANES
    firsts = jnp.arange(0, EX_DEV, EX_BLOCK, dtype=jnp.int32)
    before = jnp.sum((example_of < firsts[:, None]).astype(jnp.int32), axis=1)
    start = jnp.minimum(before // LANES, chunks - 2)
    rank = factors[0].shape[1] // 2
    feats, width = inverse_curvature.shape
    vmem = pl.BlockSpec(memory_space=pltpu.VMEM)
    return pl.pallas_call(
        functools.partial(query_kernel, len(factors)),
        in_specs=[pl.BlockSpec(memory_space=pltpu.SMEM)] + [vmem] * (2 + len(factors)),
        out_specs=[vmem] * cuts,
        out_shape=[jax.ShapeDtypeStruct((feats // cuts, EX_DEV), BF16)] * cuts,
        scratch_shapes=[
            pltpu.VMEM((tokens, 2 * rank), BF16),
            pltpu.VMEM((EX_BLOCK * rank, tokens), BF16),
            pltpu.VMEM((tokens, 2 * rank), BF16),
            pltpu.VMEM((EX_DEV, width), BF16),
        ],
        compiler_params=pltpu.CompilerParams(vmem_limit_bytes=20 * MIB),
        name="query",
    )(start, example_of.reshape(chunks, LANES), *factors, inverse_curvature)


def place_of(offset, places, planes):
    plane, chip = lax.axis_index("width"), lax.axis_index("store") // 2
    here = chip * planes + jnp.where(chip % 2 == 0, plane, planes - 1 - plane)
    there = lax.rem(here + offset + places, places)
    that_chip, left = there // planes, lax.rem(there, planes)
    return that_chip, jnp.where(that_chip % 2 == 0, left, planes - 1 - left)


def early_kernel(places, planes, spots, has_total, last, mine_ref, other_ref, *rest):
    blocks, rest = rest[: len(spots)], rest[len(spots) :]
    if has_total:
        total_ref, *rest = rest
    *outs, acc = rest if last else [*rest, rest[0]]
    depth = mine_ref.shape[1] // planes
    acc[...] = total_ref[...] if has_total else jnp.zeros_like(acc)
    for block, (offset, first) in zip(blocks, spots):
        chip, plane = place_of(offset, places, planes)
        columns = pl.ds(pl.multiple_of(plane * depth + first, LANES), block.shape[0])
        for n, ref in enumerate((mine_ref, other_ref)):
            acc[chip, n] += jnp.dot(ref[:, columns], block[...], preferred_element_type=F32)
    if last:
        for chip in range(places // planes):
            for n, out in enumerate(outs):
                out[pl.ds(chip * EX_DEV, EX_DEV), :] = acc[chip, n].T


def early_scores(stored, others, blocks, spots, total, last, places, planes):
    rows, chips = stored.shape[0], places // planes
    sums = (chips, 2, rows, EX_DEV)
    vmem = pl.BlockSpec(memory_space=pltpu.VMEM)
    totals = [] if total is None else [total]
    return pl.pallas_call(
        functools.partial(early_kernel, places, planes, spots, bool(totals), last),
        in_specs=[vmem] * (2 + len(blocks) + len(totals)),
        out_specs=[vmem] * 2 if last else vmem,
        out_shape=[jax.ShapeDtypeStruct((chips * EX_DEV, rows), F32)] * 2 if last else jax.ShapeDtypeStruct(sums, F32),
        scratch_shapes=[pltpu.VMEM(sums, F32)] if last else [],
        compiler_params=pltpu.CompilerParams(vmem_limit_bytes=20 * MIB),
        name="early_scores",
    )(stored, others, *blocks, *totals)


def final_kernel(places, planes, spots, stored_ref, keep_ref, got_ref, *rest):
    blocks, out_ref = rest[:-1], rest[-1]
    core = lax.rem(lax.axis_index("store"), 2)
    depth = stored_ref.shape[1] // planes
    for n, ref in enumerate((keep_ref, got_ref)):
        which = core if n == 0 else 1 - core
        for chip in range(places // planes):
            at = pl.multiple_of((2 * chip + which) * EX_DEV, EX_DEV)
            out_ref[pl.ds(at, EX_DEV), :] = ref[pl.ds(chip * EX_DEV, EX_DEV), :]
        part = None
        for block, (offset, first) in zip(blocks[n * len(spots) : (n + 1) * len(spots)], spots):
            chip, plane = place_of(offset, places, planes)
            columns = pl.ds(pl.multiple_of(plane * depth + first, LANES), block.shape[0])
            more = jnp.dot(stored_ref[:, columns], block[...], preferred_element_type=F32)
            part = more if part is None else part + more
        at = pl.multiple_of((2 * chip + which) * EX_DEV, EX_DEV)
        out_ref[pl.ds(at, EX_DEV), :] += part.T


def final_scores(stored, keep, got, blocks, spots, places, planes):
    vmem = pl.BlockSpec(memory_space=pltpu.VMEM)
    return pl.pallas_call(
        functools.partial(final_kernel, places, planes, spots),
        in_specs=[vmem] * (3 + len(blocks)),
        out_specs=vmem,
        out_shape=jax.ShapeDtypeStruct((2 * keep.shape[0], keep.shape[1]), F32),
        compiler_params=pltpu.CompilerParams(vmem_limit_bytes=20 * MIB),
        name="final_scores",
    )(stored, keep, got, *blocks)


def ring_pairs(planes, stores, step):
    walk = [(x, z if x % 2 == 0 else planes - 1 - z) for x in range(stores // 2) for z in range(planes)]
    pairs = []
    for at, (x, z) in enumerate(walk):
        to_x, to_z = walk[(at + step) % len(walk)]
        pairs += [(z * stores + 2 * x + core, to_z * stores + 2 * to_x + core) for core in range(2)]
    return pairs


def sum_over_width(parts, planes):
    total = parts[0]
    turn = lambda d: [(i, (i + d) % planes) for i in range(planes)]
    for d in range(1, planes):
        total = total + lax.ppermute(parts[d], "width", turn(d)).astype(F32)
    total = total.astype(BF16)
    return [total] + [lax.ppermute(total, "width", turn(d)) for d in range(1, planes)]


def body(activations, out_grads, example_of, proj_in, proj_out, inverse_curvature, stored):
    planes, stores = lax.axis_size("width"), lax.axis_size("store")
    if planes * stores > 32 or stores % 2:
        partial_value = jnp.concatenate(
            [
                jnp.dot(activations, proj_in, preferred_element_type=F32),
                jnp.dot(out_grads, proj_out, preferred_element_type=F32),
            ],
            axis=1,
        )
        factors = lax.psum(partial_value, "width").astype(BF16)
        (query,) = query_transposed([factors], example_of, inverse_curvature, 1)
        gathered = lax.all_gather(query, ("width", "store"), axis=0)
        blocks = gathered.reshape(planes, stores, query.shape[0], EX_DEV)
        stored_blocks = stored.reshape(stored.shape[0], planes, query.shape[0])
        scores = jnp.einsum("wsfe,rwf->ser", blocks, stored_blocks, preferred_element_type=F32)
        return scores.reshape(stores * EX_DEV, stored.shape[0])

    swap = [(i, i ^ 1) for i in range(stores)]
    others = lax.ppermute(stored, "store", swap)
    parts = project(activations, out_grads, proj_in, proj_out, planes)
    factors = sum_over_width(parts, planes)
    streams = 2
    query = query_transposed(factors, example_of, inverse_curvature, streams)

    places = planes * stores // 2
    on = lambda x: lax.ppermute(x, ("width", "store"), ring_pairs(planes, stores, 1))
    back = lambda x: lax.ppermute(x, ("width", "store"), ring_pairs(planes, stores, -1))
    firsts = [j * query[0].shape[0] for j in range(streams)]
    ahead, behind = list(query), list(query)
    early, spots = list(query), [(0, first) for first in firsts]
    total = None
    for k in range(1, places // 2):
        if k == places // 2 - 1:
            total = early_scores(stored, others, early, spots, None, False, places, planes)
            early, spots = [], []
        for j in range(streams):
            ahead[j], behind[j] = on(ahead[j]), back(behind[j])
            early += [ahead[j], behind[j]]
            spots += [(-k, firsts[j]), (k, firsts[j])]
    far = [on(ahead[0]), back(behind[1])]
    spots_far = [(places // 2, first) for first in firsts]
    keep, send = early_scores(stored, others, early, spots, total, True, places, planes)
    got = lax.ppermute(send, "store", swap)
    far += [lax.ppermute(x, "store", swap) for x in far]
    return final_scores(stored, keep, got, far, spots_far, places, planes)


def solution(mesh):
    return jax.shard_map(
        body,
        mesh=mesh,
        in_specs=(
            P(("groups", "store"), "width"),
            P(("groups", "store"), "width"),
            P(("groups", "store"), None),
            P("width", None),
            P("width", None),
            P("width", None),
            P(("width", "store"), None),
        ),
        out_specs=P("groups", ("width", "store")),
        check_vma=False,
    )
```

time: 119 us -> 62 us (0.52)
  blocking collectives: 32.1 us -> 0 us
  waiting for transfers between devices: 49.3 us -> 18 us
  starting transfers between devices: 0.01 us -> 25.5 us
  matrix products: 21.6 us -> 0 us
  Pallas kernels: 0 us -> 13.7 us
  between operations: 13.5 us -> 0.09 us
  local copies, waits for them, and re-layouts: 0.03 us -> 3.39 us
    all_gather x1 -> x0, waiting for transfers between devices: 49.3 us -> none  [body(): lax.all_gather(query[None], ('width', 'store'), axis=0, tiled=True)]
    psum x1 -> x0, blocking collectives: 32.1 us -> none  [body(): factors = lax.psum(partial_value, 'width').astype(jnp.bfloat16)]
    ppermute x0 -> x24, starting transfers between devices: none -> 25.5 us  [the longest x7 9.81 us: body(): lax.ppermute(x, ('width', 'store'), ring_pairs(planes, stores, 1))]
    dot_general x5 -> x0, matrix products: 21.6 us -> none  [the longest x1 7.16 us: body(): lax.dot_general(flat_grads, inverse_curvature, (((1,), (1,)), ((), ())),...]
    ppermute x0 -> x24, waiting for transfers between devices: none -> 18 us  [the longest x7 6.29 us: body(): lax.ppermute(x, ('width', 'store'), ring_pairs(planes, stores, -1))]
    pallas_call x0 -> x5, Pallas kernels: none -> 13.7 us  [the longest x1 5.35 us: project(): pl.pallas_call(functools.partial(project_kernel, planes), in_specs=[pl.Bl...]
    unnamed x8 -> x6, local copies, waits for them, and re-layouts: 0.02 us -> 3.39 us
    eq x1 -> x0, other arithmetic: 1.21 us -> none  [body(): member = token_ids[None, :] == jnp.arange(EX_DEV, dtype=jnp.int32)[:, None]]
  transfers between devices with their start and end apart: 1 -> 24, of which waited for: 1 -> 14; matrix products, arithmetic and copies ran while one was open for 0% -> 2% of each run, Pallas kernels for 0% -> 20%
where the time goes in v2:
time: 62 us; the launch traced here: 61.8 us
  starting transfers between devices  25.5 us (41%)
  waiting for transfers between devices  18 us (29%)
  Pallas kernels  13.7 us (22%)
  local copies, waits for them, and re-layouts  3.39 us (5%)
  other arithmetic  1.14 us (2%)
    ppermute x7, starting transfers between devices, body(): lax.ppermute(x, ('width', 'store'), ring_pairs(planes, stores, 1))  9.81 us
    ppermute x3, starting transfers between devices, sum_over_width(): total = total + lax.ppermute(parts[d], 'width', turn(d)).astype(F32)  6.56 us
    ppermute x7, waiting for transfers between devices, body(): lax.ppermute(x, ('width', 'store'), ring_pairs(planes, stores, -1))  6.29 us
    pallas_call x1, Pallas kernels, project(): pl.pallas_call(functools.partial(project_kernel, planes), in_specs=[pl.Bl...  5.35 us
    pallas_call x1, Pallas kernels, query_transposed(): pl.pallas_call(functools.partial(query_kernel, len(factors)), in_specs=[p...  4.52 us
    ppermute x3, waiting for transfers between devices, sum_over_width(): lax.ppermute(total, 'width', turn(d))  4.46 us
    ppermute x7, starting transfers between devices, body(): lax.ppermute(x, ('width', 'store'), ring_pairs(planes, stores, -1))  4.31 us
    ppermute x3, starting transfers between devices, sum_over_width(): lax.ppermute(total, 'width', turn(d))  4.11 us
  transfers between devices with their start and end apart: 24, of which 14 were waited for; matrix products, arithmetic and copies ran while one was open for 2% of the time, Pallas kernels for 20%

profile of v2, /device:TPU:0, one launch (start us, length us, event | category | flops | bytes accessed | tf_op | source)
XLA Modules:
  0.0 61.8 jit_solution(18379872996158108554)
XLA Ops:
  0.0 0.5 collective-permute-start
  0.5 5.3 %project.1 = (f32[256,128]{1,0:T(8,128)}, bf16[256,128]{1,0:T(8,128)(2,1)}, bf16[256,128]{1,0:T(8,128)(2,1)}, bf16[256,128]{1,0:T(8,128)(2,1)}) custom-call(bf16[1024,2048]{1,0:T(8,128)(2,1)} %act_hbm.1, bf16[1024,2048]{1,0:T(8,128)(2,1)} %grad_hbm.1, bf16[64,2048]{1,0:T(8,128)(2,1)} %bitcast.6, bf16[64,2048]{1,0:T(8,128)(2,1)} %bitcast.7), custom_call_target="tpu_custom_call" | custom-call | tf_op jit(solution)/shard_map/project/pallas_call | solution.py:61
  5.8 2.6 %collective-permute-start.1 = (bf16[256,128]{1,0:T(8,128)(2,1)}, bf16[256,128]{1,0:T(8,128)(2,1)S(1)}, u32[]{:S(2)}, u32[]{:S(2)}) collective-permute-start(bf16[256,128]{1,0:T(8,128)(2,1)} %get-tuple-element.14), channel_id=1, source_target_pairs={{0,4},{4,8},{8,12},{12,0},{1,5},{5,9},{9,13},{13,1},{2,6},{6,10},{... | collective-permute-start | bytes 196616 | tf_op jit(solution)/shard_map/ppermute | solution.py:235
  8.4 2.6 %collective-permute-start.2 = (bf16[256,128]{1,0:T(8,128)(2,1)}, bf16[256,128]{1,0:T(8,128)(2,1)S(1)}, u32[]{:S(2)}, u32[]{:S(2)}) collective-permute-start(bf16[256,128]{1,0:T(8,128)(2,1)} %get-tuple-element.15), channel_id=1, source_target_pairs={{0,8},{4,12},{8,0},{12,4},{1,9},{5,13},{9,1},{13,5},{2,10},{6,14},... | collective-permute-start | bytes 196616 | tf_op jit(solution)/shard_map/ppermute | solution.py:235
  11.0 1.3 %collective-permute-start.3 = (bf16[256,128]{1,0:T(8,128)(2,1)}, bf16[256,128]{1,0:T(8,128)(2,1)S(1)}, u32[]{:S(2)}, u32[]{:S(2)}) collective-permute-start(bf16[256,128]{1,0:T(8,128)(2,1)} %get-tuple-element.16), channel_id=1, source_target_pairs={{0,12},{4,0},{8,4},{12,8},{1,13},{5,1},{9,5},{13,9},{2,14},{6,2},{... | collective-permute-start | bytes 196616 | tf_op jit(solution)/shard_map/ppermute | solution.py:235
  12.4 0.2 convert_reduce_fusion
  12.6 1.0 %collective-permute-done.1 = bf16[256,128]{1,0:T(8,128)(2,1)S(1)} collective-permute-done((bf16[256,128]{1,0:T(8,128)(2,1)}, bf16[256,128]{1,0:T(8,128)(2,1)S(1)}, u32[]{:S(2)}, u32[]{:S(2)}) %collective-permute-start.1) | collective-permute-done | bytes 65568 | tf_op jit(solution)/shard_map/ppermute | solution.py:235
  13.6 2.8 %collective-permute-done.2 = bf16[256,128]{1,0:T(8,128)(2,1)S(1)} collective-permute-done((bf16[256,128]{1,0:T(8,128)(2,1)}, bf16[256,128]{1,0:T(8,128)(2,1)S(1)}, u32[]{:S(2)}, u32[]{:S(2)}) %collective-permute-start.2) | collective-permute-done | bytes 65568 | tf_op jit(solution)/shard_map/ppermute | solution.py:235
  16.3 0.2 collective-permute-done.3
  16.6 0.9 %add_convert_fusion.rest_0_ = bf16[256,128]{1,0:T(8,128)(2,1)S(1)} fusion(bf16[256,128]{1,0:T(8,128)(2,1)S(1)} %collective-permute-done.3, bf16[256,128]{1,0:T(8,128)(2,1)S(1)} %collective-permute-done.2, f32[256,128]{1,0:T(8,128)} %get-tuple-element.13, bf16[256,128]{1,0:T(8,128)(2,1)S(1)} %collective-permute-done.1), kind=kLoop, calls=%fused_computation | loop fusion | flops 229376 | bytes 393216 | tf_op jit(solution)/shard_map/convert_element_type | solution.py:236
  17.5 1.7 %collective-permute-start.4 = (bf16[256,128]{1,0:T(8,128)(2,1)S(1)}, bf16[256,128]{1,0:T(8,128)(2,1)S(1)}, u32[]{:S(2)}, u32[]{:S(2)}) collective-permute-start(bf16[256,128]{1,0:T(8,128)(2,1)S(1)} %add_convert_fusion.rest_0_), channel_id=1, source_target_pairs={{0,4},{4,8},{8,12},{12,0},{1,5},{5,9},{9,13},{13,1},{2,6},{6,10},{... | collective-permute-start | bytes 196616 | tf_op jit(solution)/shard_map/ppermute | solution.py:237
  19.2 1.6 %collective-permute-start.5 = (bf16[256,128]{1,0:T(8,128)(2,1)S(1)}, bf16[256,128]{1,0:T(8,128)(2,1)S(1)}, u32[]{:S(2)}, u32[]{:S(2)}) collective-permute-start(bf16[256,128]{1,0:T(8,128)(2,1)S(1)} %add_convert_fusion.rest_0_), channel_id=1, source_target_pairs={{0,8},{4,12},{8,0},{12,4},{1,9},{5,13},{9,1},{13,5},{2,10},{6,14},... | collective-permute-start | bytes 196616 | tf_op jit(solution)/shard_map/ppermute | solution.py:237
  20.8 0.8 %collective-permute-start.6 = (bf16[256,128]{1,0:T(8,128)(2,1)S(1)}, bf16[256,128]{1,0:T(8,128)(2,1)S(1)}, u32[]{:S(2)}, u32[]{:S(2)}) collective-permute-start(bf16[256,128]{1,0:T(8,128)(2,1)S(1)} %add_convert_fusion.rest_0_), channel_id=1, source_target_pairs={{0,12},{4,0},{8,4},{12,8},{1,13},{5,1},{9,5},{13,9},{2,14},{6,2},{... | collective-permute-start | bytes 196616 | tf_op jit(solution)/shard_map/ppermute | solution.py:237
  21.7 2.4 %collective-permute-done.4.rest_1_ = bf16[256,128]{1,0:T(8,128)(2,1)S(1)} collective-permute-done((bf16[256,128]{1,0:T(8,128)(2,1)S(1)}, bf16[256,128]{1,0:T(8,128)(2,1)S(1)}, u32[]{:S(2)}, u32[]{:S(2)}) %collective-permute-start.4) | collective-permute-done | bytes 65568 | tf_op jit(solution)/shard_map/ppermute | solution.py:237
  24.0 2.0 %collective-permute-done.5.rest_2_ = bf16[256,128]{1,0:T(8,128)(2,1)S(1)} collective-permute-done((bf16[256,128]{1,0:T(8,128)(2,1)S(1)}, bf16[256,128]{1,0:T(8,128)(2,1)S(1)}, u32[]{:S(2)}, u32[]{:S(2)}) %collective-permute-start.5) | collective-permute-done | bytes 65568 | tf_op jit(solution)/shard_map/ppermute | solution.py:237
  26.0 0.1 collective-permute-done.6.rest_3_
  26.1 3.4 %copy-done.1 = bf16[1024,4096]{1,0:T(8,128)(2,1)S(1)} copy-done((bf16[1024,4096]{1,0:T(8,128)(2,1)S(1)}, bf16[1024,4096]{1,0:T(8,128)(2,1)}, u32[]{:S(2)}) %copy-start.1) | copy-done | bytes 8388632
  29.5 4.5 %query.1 = (bf16[512,128]{1,0:T(8,128)(2,1)S(1)}, bf16[512,128]{1,0:T(8,128)(2,1)S(1)}) custom-call(s32[16]{0:T(128)S(1)} %fusion.start_ref, s32[8,128]{1,0:T(8,128)S(1)} %bitcast.5, bf16[256,128]{1,0:T(8,128)(2,1)S(1)} %add_convert_fusion.rest_0_, bf16[256,128]{1,0:T(8,128)(2,1)S(1)} %collective-permute-done.4.rest_1_, ...), custom_call_target="tpu_custom_call" | custom-call | tf_op jit(solution)/shard_map/query/pallas_call | solution.py:133
  34.0 1.8 %collective-permute-start.7 = (bf16[512,128]{1,0:T(8,128)(2,1)S(1)}, bf16[512,128]{1,0:T(8,128)(2,1)S(1)}, u32[]{:S(2)}, u32[]{:S(2)}) collective-permute-start(bf16[512,128]{1,0:T(8,128)(2,1)S(1)} %get-tuple-element.17.rest_0_), channel_id=1, source_target_pairs={{0,4},{1,5},{4,8},{5,9},{8,12},{9,13},{12,14},{13,15},{14,10},{15,... | collective-permute-start | bytes 393224 | tf_op jit(solution)/shard_map/ppermute | solution.py:266
  35.8 0.3 collective-permute-start.16
  36.1 1.5 %collective-permute-start.10 = (bf16[512,128]{1,0:T(8,128)(2,1)S(1)}, bf16[512,128]{1,0:T(8,128)(2,1)S(1)}, u32[]{:S(2)}, u32[]{:S(2)}) collective-permute-start(bf16[512,128]{1,0:T(8,128)(2,1)S(1)} %get-tuple-element.17.rest_0_), channel_id=1, source_target_pairs={{0,2},{1,3},{4,0},{5,1},{8,4},{9,5},{12,8},{13,9},{14,12},{15,13},... | collective-permute-start | bytes 393224 | tf_op jit(solution)/shard_map/ppermute | solution.py:267
  37.6 0.5 collective-permute-start.13
  38.1 1.6 %collective-permute-done.7.rest_2_ = bf16[512,128]{1,0:T(8,128)(2,1)S(1)} collective-permute-done((bf16[512,128]{1,0:T(8,128)(2,1)S(1)}, bf16[512,128]{1,0:T(8,128)(2,1)S(1)}, u32[]{:S(2)}, u32[]{:S(2)}) %collective-permute-start.7) | collective-permute-done | bytes 131104 | tf_op jit(solution)/shard_map/ppermute | solution.py:266
  39.7 2.5 %collective-permute-start.8 = (bf16[512,128]{1,0:T(8,128)(2,1)S(1)}, bf16[512,128]{1,0:T(8,128)(2,1)S(1)}, u32[]{:S(2)}, u32[]{:S(2)}) collective-permute-start(bf16[512,128]{1,0:T(8,128)(2,1)S(1)} %collective-permute-done.7.rest_2_), channel_id=1, source_target_pairs={{0,4},{1,5},{4,8},{5,9},{8,12},{9,13},{12,14},{13,15},{14,10},{15,... | collective-permute-start | bytes 393224 | tf_op jit(solution)/shard_map/ppermute | solution.py:266
  42.2 0.0 collective-permute-done.16.rest_5_
  42.2 0.3 collective-permute-start.17
  42.5 2.2 %collective-permute-done.10.rest_3_ = bf16[512,128]{1,0:T(8,128)(2,1)S(1)} collective-permute-done((bf16[512,128]{1,0:T(8,128)(2,1)S(1)}, bf16[512,128]{1,0:T(8,128)(2,1)S(1)}, u32[]{:S(2)}, u32[]{:S(2)}) %collective-permute-start.10) | collective-permute-done | bytes 131104 | tf_op jit(solution)/shard_map/ppermute | solution.py:267
  44.7 0.3 collective-permute-start.11
  45.0 0.0 collective-permute-done.13.rest_4_
  45.0 1.7 %collective-permute-start.14 = (bf16[512,128]{1,0:T(8,128)(2,1)S(1)}, bf16[512,128]{1,0:T(8,128)(2,1)S(1)}, u32[]{:S(2)}, u32[]{:S(2)}) collective-permute-start(bf16[512,128]{1,0:T(8,128)(2,1)S(1)} %collective-permute-done.13.rest_4_), channel_id=1, source_target_pairs={{0,4},{1,5},{4,8},{5,9},{8,12},{9,13},{12,14},{13,15},{14,10},{15,... | collective-permute-start | bytes 393224 | tf_op jit(solution)/shard_map/ppermute | solution.py:266
  46.8 0.5 collective-permute-start.9
  47.3 0.9 %collective-permute-done.17.rest_9_ = bf16[512,128]{1,0:T(8,128)(2,1)S(1)} collective-permute-done((bf16[512,128]{1,0:T(8,128)(2,1)S(1)}, bf16[512,128]{1,0:T(8,128)(2,1)S(1)}, u32[]{:S(2)}, u32[]{:S(2)}) %collective-permute-start.17) | collective-permute-done | bytes 131104 | tf_op jit(solution)/shard_map/ppermute | solution.py:267
  48.2 0.7 %collective-permute-start.18 = (bf16[512,128]{1,0:T(8,128)(2,1)S(1)}, bf16[512,128]{1,0:T(8,128)(2,1)S(1)}, u32[]{:S(2)}, u32[]{:S(2)}) collective-permute-start(bf16[512,128]{1,0:T(8,128)(2,1)S(1)} %collective-permute-done.17.rest_9_), channel_id=1, source_target_pairs={{0,2},{1,3},{4,0},{5,1},{8,4},{9,5},{12,8},{13,9},{14,12},{15,13},... | collective-permute-start | bytes 393224 | tf_op jit(solution)/shard_map/ppermute | solution.py:267
  48.8 2.3 %collective-permute-done.11.rest_7_ = bf16[512,128]{1,0:T(8,128)(2,1)S(1)} collective-permute-done((bf16[512,128]{1,0:T(8,128)(2,1)S(1)}, bf16[512,128]{1,0:T(8,128)(2,1)S(1)}, u32[]{:S(2)}, u32[]{:S(2)}) %collective-permute-start.11) | collective-permute-done | bytes 131104 | tf_op jit(solution)/shard_map/ppermute | solution.py:267
  51.1 0.3 collective-permute-start.12
  51.4 1.7 %collective-permute-start.15 = (bf16[512,128]{1,0:T(8,128)(2,1)S(1)}, bf16[512,128]{1,0:T(8,128)(2,1)S(1)}, u32[]{:S(2)}, u32[]{:S(2)}) collective-permute-start(bf16[512,128]{1,0:T(8,128)(2,1)S(1)} %collective-permute-done.14.rest_8_), channel_id=1, source_target_pairs={{0,4},{1,5},{4,8},{5,9},{8,12},{9,13},{12,14},{13,15},{14,10},{15,... | collective-permute-start | bytes 393224 | tf_op jit(solution)/shard_map/ppermute | solution.py:266
  53.1 0.0 collective-permute-done.9.rest_0_
  53.1 1.0 %collective-permute-start.20 = (bf16[512,128]{1,0:T(8,128)(2,1)S(1)}, bf16[512,128]{1,0:T(8,128)(2,1)S(1)}, u32[]{:S(2)}, u32[]{:S(2)}) collective-permute-start(bf16[512,128]{1,0:T(8,128)(2,1)S(1)} %collective-permute-done.9.rest_0_), channel_id=1, source_target_pairs={{0,4},{1,5},{4,8},{5,9},{8,12},{9,13},{12,14},{13,15},{14,10},{15,... | collective-permute-start | bytes 393224 | tf_op jit(solution)/shard_map/ppermute | solution.py:266
  54.2 1.0 %collective-permute-start.21 = (bf16[512,128]{1,0:T(8,128)(2,1)S(1)}, bf16[512,128]{1,0:T(8,128)(2,1)S(1)}, u32[]{:S(2)}, u32[]{:S(2)}) collective-permute-start(bf16[512,128]{1,0:T(8,128)(2,1)S(1)} %collective-permute-done.18.rest_3_), channel_id=1, source_target_pairs={{0,2},{1,3},{4,0},{5,1},{8,4},{9,5},{12,8},{13,9},{14,12},{15,13},... | collective-permute-start | bytes 393224 | tf_op jit(solution)/shard_map/ppermute | solution.py:267
  55.2 1.6 %early_scores.2.rest_4_ = f32[2,2,256,128]{3,2,1,0:T(8,128)S(1)} custom-call(bf16[256,4096]{1,0:T(8,128)(2,1)S(1)} %copy-done, bf16[256,4096]{1,0:T(8,128)(2,1)S(1)} %collective-permute-done.other_ref, bf16[512,128]{1,0:T(8,128)(2,1)S(1)} %get-tuple-element.17.rest_0_, bf16[512,128]{1,0:T(8,128)(2,1)S(1)} %get-tuple-element.18.rest_1_, ...), custom_call_target="tpu_custom_call" | custom-call | tf_op jit(solution)/shard_map/early_scores/pallas_call | solution.py:180
  56.8 0.9 %early_scores.3 = (f32[256,256]{1,0:T(8,128)S(1)}, f32[256,256]{1,0:T(8,128)S(1)}) custom-call(bf16[256,4096]{1,0:T(8,128)(2,1)S(1)} %copy-done, bf16[256,4096]{1,0:T(8,128)(2,1)S(1)} %collective-permute-done.other_ref, bf16[512,128]{1,0:T(8,128)(2,1)S(1)} %collective-permute-done.9.rest_0_, bf16[512,128]{1,0:T(8,128)(2,1)S(1)} %collective-permute-done.12.rest_1_, ...), custom_call_target="tpu_custom_call" | custom-call | tf_op jit(solution)/shard_map/early_scores/pallas_call | solution.py:180
  57.7 0.1 collective-permute-start.19
  57.8 0.3 collective-permute-done.20.rest_0_
  58.1 0.2 collective-permute-start.22
  58.3 0.8 %collective-permute-done.21.rest_1_ = bf16[512,128]{1,0:T(8,128)(2,1)S(1)} collective-permute-done((bf16[512,128]{1,0:T(8,128)(2,1)S(1)}, bf16[512,128]{1,0:T(8,128)(2,1)S(1)}, u32[]{:S(2)}, u32[]{:S(2)}) %collective-permute-start.21) | collective-permute-done | bytes 131104 | tf_op jit(solution)/shard_map/ppermute | solution.py:267
  59.2 0.4 collective-permute-done.22.rest_2_
  59.5 1.0 %collective-permute-done.23.rest_3_ = bf16[512,128]{1,0:T(8,128)(2,1)S(1)} collective-permute-done((bf16[512,128]{1,0:T(8,128)(2,1)S(1)}, bf16[512,128]{1,0:T(8,128)(2,1)S(1)}, u32[]{:S(2)}, u32[]{:S(2)}) %collective-permute-start.23) | collective-permute-done | bytes 131104 | tf_op jit(solution)/shard_map/ppermute | solution.py:284
  60.5 1.3 %final_scores.1 = f32[512,256]{1,0:T(8,128)} custom-call(bf16[256,4096]{1,0:T(8,128)(2,1)S(1)} %copy-done, f32[256,256]{1,0:T(8,128)S(1)} %get-tuple-element.19.keep_ref, f32[256,256]{1,0:T(8,128)S(1)} %collective-permute-done.19.got_ref, bf16[512,128]{1,0:T(8,128)(2,1)S(1)} %collective-permute-done.20.rest_0_, ...), custom_call_target="tpu_custom_call" | custom-call | tf_op jit(solution)/shard_map/final_scores/pallas_call | solution.py:212
  (15 shorter events, 0.0 us)
Async XLA Ops:
  0.0 55.2 %collective-permute-start = (bf16[256,4096]{1,0:T(8,128)(2,1)}, bf16[256,4096]{1,0:T(8,128)(2,1)S(1)}, u32[]{:S(2)}, u32[]{:S(2)}) collective-permute-start(bf16[256,4096]{1,0:T(8,128)(2,1)} %stored_ref.1), channel_id=1, source_target_pairs={{0,1},{1,0},{2,3},{3,2},{4,5},{5,4},{6,7},{7,6},{8,9},{9,8},{10,11... | collective-permute-start | bytes 6291464 | tf_op jit(solution)/shard_map/ppermute | solution.py:259
  0.5 11.9 %copy-start.2 = (s32[1,1024]{1,0:T(1,128)S(1)}, s32[1,1024]{1,0:T(1,128)}, u32[]{:S(2)}) copy-start(s32[1,1024]{1,0:T(1,128)} %param.9) | copy-start | bytes 12292
  5.8 7.8 %collective-permute-start.1 = (bf16[256,128]{1,0:T(8,128)(2,1)}, bf16[256,128]{1,0:T(8,128)(2,1)S(1)}, u32[]{:S(2)}, u32[]{:S(2)}) collective-permute-start(bf16[256,128]{1,0:T(8,128)(2,1)} %get-tuple-element.14), channel_id=1, source_target_pairs={{0,4},{4,8},{8,12},{12,0},{1,5},{5,9},{9,13},{13,1},{2,6},{6,10},{... | collective-permute-start | bytes 196616 | tf_op jit(solution)/shard_map/ppermute | solution.py:235
  8.4 7.9 %collective-permute-start.2 = (bf16[256,128]{1,0:T(8,128)(2,1)}, bf16[256,128]{1,0:T(8,128)(2,1)S(1)}, u32[]{:S(2)}, u32[]{:S(2)}) collective-permute-start(bf16[256,128]{1,0:T(8,128)(2,1)} %get-tuple-element.15), channel_id=1, source_target_pairs={{0,8},{4,12},{8,0},{12,4},{1,9},{5,13},{9,1},{13,5},{2,10},{6,14},... | collective-permute-start | bytes 196616 | tf_op jit(solution)/shard_map/ppermute | solution.py:235
  11.0 5.6 %collective-permute-start.3 = (bf16[256,128]{1,0:T(8,128)(2,1)}, bf16[256,128]{1,0:T(8,128)(2,1)S(1)}, u32[]{:S(2)}, u32[]{:S(2)}) collective-permute-start(bf16[256,128]{1,0:T(8,128)(2,1)} %get-tuple-element.16), channel_id=1, source_target_pairs={{0,12},{4,0},{8,4},{12,8},{1,13},{5,1},{9,5},{13,9},{2,14},{6,2},{... | collective-permute-start | bytes 196616 | tf_op jit(solution)/shard_map/ppermute | solution.py:235
  17.5 6.5 %collective-permute-start.4 = (bf16[256,128]{1,0:T(8,128)(2,1)S(1)}, bf16[256,128]{1,0:T(8,128)(2,1)S(1)}, u32[]{:S(2)}, u32[]{:S(2)}) collective-permute-start(bf16[256,128]{1,0:T(8,128)(2,1)S(1)} %add_convert_fusion.rest_0_), channel_id=1, source_target_pairs={{0,4},{4,8},{8,12},{12,0},{1,5},{5,9},{9,13},{13,1},{2,6},{6,10},{... | collective-permute-start | bytes 196616 | tf_op jit(solution)/shard_map/ppermute | solution.py:237
  19.2 6.8 %collective-permute-start.5 = (bf16[256,128]{1,0:T(8,128)(2,1)S(1)}, bf16[256,128]{1,0:T(8,128)(2,1)S(1)}, u32[]{:S(2)}, u32[]{:S(2)}) collective-permute-start(bf16[256,128]{1,0:T(8,128)(2,1)S(1)} %add_convert_fusion.rest_0_), channel_id=1, source_target_pairs={{0,8},{4,12},{8,0},{12,4},{1,9},{5,13},{9,1},{13,5},{2,10},{6,14},... | collective-permute-start | bytes 196616 | tf_op jit(solution)/shard_map/ppermute | solution.py:237
  20.8 5.3 %collective-permute-start.6 = (bf16[256,128]{1,0:T(8,128)(2,1)S(1)}, bf16[256,128]{1,0:T(8,128)(2,1)S(1)}, u32[]{:S(2)}, u32[]{:S(2)}) collective-permute-start(bf16[256,128]{1,0:T(8,128)(2,1)S(1)} %add_convert_fusion.rest_0_), channel_id=1, source_target_pairs={{0,12},{4,0},{8,4},{12,8},{1,13},{5,1},{9,5},{13,9},{2,14},{6,2},{... | collective-permute-start | bytes 196616 | tf_op jit(solution)/shard_map/ppermute | solution.py:237
  26.1 3.4 %copy-start.1 = (bf16[1024,4096]{1,0:T(8,128)(2,1)S(1)}, bf16[1024,4096]{1,0:T(8,128)(2,1)}, u32[]{:S(2)}) copy-start(bf16[1024,4096]{1,0:T(8,128)(2,1)} %rest_4_.1) | copy-start | bytes 25165828
  29.5 25.7 %copy-start = (bf16[256,4096]{1,0:T(8,128)(2,1)S(1)}, bf16[256,4096]{1,0:T(8,128)(2,1)}, u32[]{:S(2)}) copy-start(bf16[256,4096]{1,0:T(8,128)(2,1)} %stored_ref.1) | copy-start | bytes 6291460
  34.0 5.7 %collective-permute-start.7 = (bf16[512,128]{1,0:T(8,128)(2,1)S(1)}, bf16[512,128]{1,0:T(8,128)(2,1)S(1)}, u32[]{:S(2)}, u32[]{:S(2)}) collective-permute-start(bf16[512,128]{1,0:T(8,128)(2,1)S(1)} %get-tuple-element.17.rest_0_), channel_id=1, source_target_pairs={{0,4},{1,5},{4,8},{5,9},{8,12},{9,13},{12,14},{13,15},{14,10},{15,... | collective-permute-start | bytes 393224 | tf_op jit(solution)/shard_map/ppermute | solution.py:266
  35.8 6.4 %collective-permute-start.16 = (bf16[512,128]{1,0:T(8,128)(2,1)S(1)}, bf16[512,128]{1,0:T(8,128)(2,1)S(1)}, u32[]{:S(2)}, u32[]{:S(2)}) collective-permute-start(bf16[512,128]{1,0:T(8,128)(2,1)S(1)} %get-tuple-element.18.rest_1_), channel_id=1, source_target_pairs={{0,2},{1,3},{4,0},{5,1},{8,4},{9,5},{12,8},{13,9},{14,12},{15,13},... | collective-permute-start | bytes 393224 | tf_op jit(solution)/shard_map/ppermute | solution.py:267
  36.1 8.6 %collective-permute-start.10 = (bf16[512,128]{1,0:T(8,128)(2,1)S(1)}, bf16[512,128]{1,0:T(8,128)(2,1)S(1)}, u32[]{:S(2)}, u32[]{:S(2)}) collective-permute-start(bf16[512,128]{1,0:T(8,128)(2,1)S(1)} %get-tuple-element.17.rest_0_), channel_id=1, source_target_pairs={{0,2},{1,3},{4,0},{5,1},{8,4},{9,5},{12,8},{13,9},{14,12},{15,13},... | collective-permute-start | bytes 393224 | tf_op jit(solution)/shard_map/ppermute | solution.py:267
  37.6 7.4 %collective-permute-start.13 = (bf16[512,128]{1,0:T(8,128)(2,1)S(1)}, bf16[512,128]{1,0:T(8,128)(2,1)S(1)}, u32[]{:S(2)}, u32[]{:S(2)}) collective-permute-start(bf16[512,128]{1,0:T(8,128)(2,1)S(1)} %get-tuple-element.18.rest_1_), channel_id=1, source_target_pairs={{0,4},{1,5},{4,8},{5,9},{8,12},{9,13},{12,14},{13,15},{14,10},{15,... | collective-permute-start | bytes 393224 | tf_op jit(solution)/shard_map/ppermute | solution.py:266
  39.7 7.1 %collective-permute-start.8 = (bf16[512,128]{1,0:T(8,128)(2,1)S(1)}, bf16[512,128]{1,0:T(8,128)(2,1)S(1)}, u32[]{:S(2)}, u32[]{:S(2)}) collective-permute-start(bf16[512,128]{1,0:T(8,128)(2,1)S(1)} %collective-permute-done.7.rest_2_), channel_id=1, source_target_pairs={{0,4},{1,5},{4,8},{5,9},{8,12},{9,13},{12,14},{13,15},{14,10},{15,... | collective-permute-start | bytes 393224 | tf_op jit(solution)/shard_map/ppermute | solution.py:266
  42.2 5.9 %collective-permute-start.17 = (bf16[512,128]{1,0:T(8,128)(2,1)S(1)}, bf16[512,128]{1,0:T(8,128)(2,1)S(1)}, u32[]{:S(2)}, u32[]{:S(2)}) collective-permute-start(bf16[512,128]{1,0:T(8,128)(2,1)S(1)} %collective-permute-done.16.rest_5_), channel_id=1, source_target_pairs={{0,2},{1,3},{4,0},{5,1},{8,4},{9,5},{12,8},{13,9},{14,12},{15,13},... | collective-permute-start | bytes 393224 | tf_op jit(solution)/shard_map/ppermute | solution.py:267
  44.7 6.4 %collective-permute-start.11 = (bf16[512,128]{1,0:T(8,128)(2,1)S(1)}, bf16[512,128]{1,0:T(8,128)(2,1)S(1)}, u32[]{:S(2)}, u32[]{:S(2)}) collective-permute-start(bf16[512,128]{1,0:T(8,128)(2,1)S(1)} %collective-permute-done.10.rest_3_), channel_id=1, source_target_pairs={{0,2},{1,3},{4,0},{5,1},{8,4},{9,5},{12,8},{13,9},{14,12},{15,13},... | collective-permute-start | bytes 393224 | tf_op jit(solution)/shard_map/ppermute | solution.py:267
  45.0 6.4 %collective-permute-start.14 = (bf16[512,128]{1,0:T(8,128)(2,1)S(1)}, bf16[512,128]{1,0:T(8,128)(2,1)S(1)}, u32[]{:S(2)}, u32[]{:S(2)}) collective-permute-start(bf16[512,128]{1,0:T(8,128)(2,1)S(1)} %collective-permute-done.13.rest_4_), channel_id=1, source_target_pairs={{0,4},{1,5},{4,8},{5,9},{8,12},{9,13},{12,14},{13,15},{14,10},{15,... | collective-permute-start | bytes 393224 | tf_op jit(solution)/shard_map/ppermute | solution.py:266
  46.8 6.4 %collective-permute-start.9 = (bf16[512,128]{1,0:T(8,128)(2,1)S(1)}, bf16[512,128]{1,0:T(8,128)(2,1)S(1)}, u32[]{:S(2)}, u32[]{:S(2)}) collective-permute-start(bf16[512,128]{1,0:T(8,128)(2,1)S(1)} %collective-permute-done.8.rest_6_), channel_id=1, source_target_pairs={{0,4},{1,5},{4,8},{5,9},{8,12},{9,13},{12,14},{13,15},{14,10},{15,... | collective-permute-start | bytes 393224 | tf_op jit(solution)/shard_map/ppermute | solution.py:266
  48.2 6.0 %collective-permute-start.18 = (bf16[512,128]{1,0:T(8,128)(2,1)S(1)}, bf16[512,128]{1,0:T(8,128)(2,1)S(1)}, u32[]{:S(2)}, u32[]{:S(2)}) collective-permute-start(bf16[512,128]{1,0:T(8,128)(2,1)S(1)} %collective-permute-done.17.rest_9_), channel_id=1, source_target_pairs={{0,2},{1,3},{4,0},{5,1},{8,4},{9,5},{12,8},{13,9},{14,12},{15,13},... | collective-permute-start | bytes 393224 | tf_op jit(solution)/shard_map/ppermute | solution.py:267
  51.1 5.7 %collective-permute-start.12 = (bf16[512,128]{1,0:T(8,128)(2,1)S(1)}, bf16[512,128]{1,0:T(8,128)(2,1)S(1)}, u32[]{:S(2)}, u32[]{:S(2)}) collective-permute-start(bf16[512,128]{1,0:T(8,128)(2,1)S(1)} %collective-permute-done.11.rest_7_), channel_id=1, source_target_pairs={{0,2},{1,3},{4,0},{5,1},{8,4},{9,5},{12,8},{13,9},{14,12},{15,13},... | collective-permute-start | bytes 393224 | tf_op jit(solution)/shard_map/ppermute | solution.py:267
  51.4 5.4 %collective-permute-start.15 = (bf16[512,128]{1,0:T(8,128)(2,1)S(1)}, bf16[512,128]{1,0:T(8,128)(2,1)S(1)}, u32[]{:S(2)}, u32[]{:S(2)}) collective-permute-start(bf16[512,128]{1,0:T(8,128)(2,1)S(1)} %collective-permute-done.14.rest_8_), channel_id=1, source_target_pairs={{0,4},{1,5},{4,8},{5,9},{8,12},{9,13},{12,14},{13,15},{14,10},{15,... | collective-permute-start | bytes 393224 | tf_op jit(solution)/shard_map/ppermute | solution.py:266
  53.1 5.0 %collective-permute-start.20 = (bf16[512,128]{1,0:T(8,128)(2,1)S(1)}, bf16[512,128]{1,0:T(8,128)(2,1)S(1)}, u32[]{:S(2)}, u32[]{:S(2)}) collective-permute-start(bf16[512,128]{1,0:T(8,128)(2,1)S(1)} %collective-permute-done.9.rest_0_), channel_id=1, source_target_pairs={{0,4},{1,5},{4,8},{5,9},{8,12},{9,13},{12,14},{13,15},{14,10},{15,... | collective-permute-start | bytes 393224 | tf_op jit(solution)/shard_map/ppermute | solution.py:266
  54.2 5.0 %collective-permute-start.21 = (bf16[512,128]{1,0:T(8,128)(2,1)S(1)}, bf16[512,128]{1,0:T(8,128)(2,1)S(1)}, u32[]{:S(2)}, u32[]{:S(2)}) collective-permute-start(bf16[512,128]{1,0:T(8,128)(2,1)S(1)} %collective-permute-done.18.rest_3_), channel_id=1, source_target_pairs={{0,2},{1,3},{4,0},{5,1},{8,4},{9,5},{12,8},{13,9},{14,12},{15,13},... | collective-permute-start | bytes 393224 | tf_op jit(solution)/shard_map/ppermute | solution.py:267
  57.7 2.8 %collective-permute-start.19 = (f32[256,256]{1,0:T(8,128)S(1)}, f32[256,256]{1,0:T(8,128)S(1)}, u32[]{:S(2)}, u32[]{:S(2)}) collective-permute-start(f32[256,256]{1,0:T(8,128)S(1)} %get-tuple-element.20), channel_id=1, source_target_pairs={{0,1},{1,0},{2,3},{3,2},{4,5},{5,4},{6,7},{7,6},{8,9},{9,8},{10,11... | collective-permute-start | bytes 786440 | tf_op jit(solution)/shard_map/ppermute | solution.py:283
  58.1 1.4 %collective-permute-start.22 = (bf16[512,128]{1,0:T(8,128)(2,1)S(1)}, bf16[512,128]{1,0:T(8,128)(2,1)S(1)}, u32[]{:S(2)}, u32[]{:S(2)}) collective-permute-start(bf16[512,128]{1,0:T(8,128)(2,1)S(1)} %collective-permute-done.20.rest_0_), channel_id=1, source_target_pairs={{0,1},{1,0},{2,3},{3,2},{4,5},{5,4},{6,7},{7,6},{8,9},{9,8},{10,11... | collective-permute-start | bytes 393224 | tf_op jit(solution)/shard_map/ppermute | solution.py:284
  59.2 1.3 %collective-permute-start.23 = (bf16[512,128]{1,0:T(8,128)(2,1)S(1)}, bf16[512,128]{1,0:T(8,128)(2,1)S(1)}, u32[]{:S(2)}, u32[]{:S(2)}) collective-permute-start(bf16[512,128]{1,0:T(8,128)(2,1)S(1)} %collective-permute-done.21.rest_1_), channel_id=1, source_target_pairs={{0,1},{1,0},{2,3},{3,2},{4,5},{5,4},{6,7},{7,6},{8,9},{9,8},{10,11... | collective-permute-start | bytes 393224 | tf_op jit(solution)/shard_map/ppermute | solution.py:284

commit v3 on v2

--- a/solution.py
+++ b/solution.py
@@ -14,6 +14,7 @@
 F32, BF16 = jnp.float32, jnp.bfloat16
 NT = (((1,), (1,)), ((), ()))
 MIB = 2**20
+in_hbm = lambda x: pltpu.with_memory_space_constraint(x, pltpu.HBM)
 
 
 def project_kernel(planes, act_hbm, grad_hbm, pin_hbm, pout_hbm, *rest):
@@ -62,7 +63,7 @@
         functools.partial(project_kernel, planes),
         in_specs=[pl.BlockSpec(memory_space=pltpu.HBM)] * 4,
         out_specs=[pl.BlockSpec(memory_space=pltpu.VMEM)] * planes,
-        out_shape=[jax.ShapeDtypeStruct((quarter, 2 * rank), BF16 if d else F32) for d in range(planes)],
+        out_shape=[pltpu.VMEM((quarter, 2 * rank), BF16 if d else F32) for d in range(planes)],
         scratch_shapes=[
             pltpu.VMEM((tokens, depth), BF16),
             pltpu.VMEM((tokens, depth), BF16),
@@ -71,9 +72,28 @@
             pltpu.VMEM((2, depth, 2 * rank), BF16),
             pltpu.SemaphoreType.DMA((2 + 2 * planes,)),
         ],
-        compiler_params=pltpu.CompilerParams(vmem_limit_bytes=60 * MIB),
+        compiler_params=pltpu.CompilerParams(vmem_limit_bytes=24 * MIB),
         name="project",
-    )(activations, out_grads, proj_in.T, proj_out.T)
+    )(*(in_hbm(x) for x in (activations, out_grads, proj_in.T, proj_out.T)))
+
+
+def load_kernel(hbm_ref, out_ref, sem):
+    copy = pltpu.make_async_copy(hbm_ref, out_ref, sem)
+    copy.start()
+    copy.wait()
+
+
+def load(x):
+    return pl.pallas_call(
+        load_kernel,
+        in_specs=[pl.BlockSpec(memory_space=pltpu.HBM)],
+        out_specs=pl.BlockSpec(memory_space=pltpu.VMEM),
+        out_shape=pltpu.VMEM(x.shape, x.dtype),
+        scratch_shapes=[pltpu.SemaphoreType.DMA],
+        compiler_params=pltpu.CompilerParams(vmem_limit_bytes=20 * MIB),
+        cost_estimate=pl.CostEstimate(flops=0, bytes_accessed=4 * x.size * x.dtype.itemsize, transcendentals=0),
+        name="load",
+    )(in_hbm(x))
 
 
 def query_kernel(pieces, start_ref, ids_ref, *rest):
@@ -228,13 +248,8 @@
     return pairs
 
 
-def sum_over_width(parts, planes):
-    total = parts[0]
-    turn = lambda d: [(i, (i + d) % planes) for i in range(planes)]
-    for d in range(1, planes):
-        total = total + lax.ppermute(parts[d], "width", turn(d)).astype(F32)
-    total = total.astype(BF16)
-    return [total] + [lax.ppermute(total, "width", turn(d)) for d in range(1, planes)]
+def turn(x, d, planes):
+    return lax.ppermute(x, "width", [(i, (i + d) % planes) for i in range(planes)])
 
 
 def body(activations, out_grads, example_of, proj_in, proj_out, inverse_curvature, stored):
@@ -255,10 +270,17 @@
         scores = jnp.einsum("wsfe,rwf->ser", blocks, stored_blocks, preferred_element_type=F32)
         return scores.reshape(stores * EX_DEV, stored.shape[0])
 
+    parts = project(activations, out_grads, proj_in, proj_out, planes)
+    own = parts[0]
+    for d in range(1, planes):
+        own = own + turn(parts[d], d, planes).astype(F32)
+    own = own.astype(BF16)
+    factors = [own] + [turn(own, d, planes) for d in range(1, planes)]
+    _, inverse_curvature, stored = lax.optimization_barrier((own, inverse_curvature, stored))
+    inverse_curvature = load(inverse_curvature)
     swap = [(i, i ^ 1) for i in range(stores)]
     others = lax.ppermute(stored, "store", swap)
-    parts = project(activations, out_grads, proj_in, proj_out, planes)
-    factors = sum_over_width(parts, planes)
+
     streams = 2
     query = query_transposed(factors, example_of, inverse_curvature, streams)
 

time: 62 us -> 57.3 us (0.924)
  local copies, waits for them, and re-layouts: 3.39 us -> 0.01 us
  waiting for transfers between devices: 18 us -> 14.9 us
  Pallas kernels: 13.7 us -> 16.5 us
  other arithmetic: 1.14 us -> 0.24 us
    pallas_call x0 -> x1, Pallas kernels: none -> 3.39 us  [load(): pl.pallas_call(load_kernel, in_specs=[pl.BlockSpec(memory_space=pltpu.HBM...]
    ppermute x6, waiting for transfers between devices: 8.48 us -> 5.1 us  [turn(): lax.ppermute(x, 'width', [(i, (i + d) % planes) for i in range(planes)])]
    unnamed x6 -> x4, local copies, waits for them, and re-layouts: 3.39 us -> 0.01 us
    convert_element_type x1, other arithmetic: 0.94 us -> 0.04 us  [body(): own = own.astype(BF16)]
  transfers between devices with their start and end apart: 24 -> 24, of which waited for: 14 -> 12; matrix products, arithmetic and copies ran while one was open for 2% -> 0% of each run, Pallas kernels for 20% -> 18%
where the time goes in v3:
time: 57.3 us; the launch traced here: 57.1 us
  starting transfers between devices  25.3 us (44%)
  Pallas kernels  16.5 us (29%)
  waiting for transfers between devices  14.9 us (26%)
    ppermute x6, starting transfers between devices, turn(): lax.ppermute(x, 'width', [(i, (i + d) % planes) for i in range(planes)])  11.1 us
    ppermute x7, starting transfers between devices, body(): lax.ppermute(x, ('width', 'store'), ring_pairs(planes, stores, 1))  9.83 us
    ppermute x7, waiting for transfers between devices, body(): lax.ppermute(x, ('width', 'store'), ring_pairs(planes, stores, -1))  6.47 us
    ppermute x6, waiting for transfers between devices, turn(): lax.ppermute(x, 'width', [(i, (i + d) % planes) for i in range(planes)])  5.1 us
    pallas_call x1, Pallas kernels, project(): pl.pallas_call(functools.partial(project_kernel, planes), in_specs=[pl.Bl...  4.77 us
    pallas_call x1, Pallas kernels, query_transposed(): pl.pallas_call(functools.partial(query_kernel, len(factors)), in_specs=[p...  4.51 us
    ppermute x7, starting transfers between devices, body(): lax.ppermute(x, ('width', 'store'), ring_pairs(planes, stores, -1))  4.06 us
    pallas_call x1, Pallas kernels, load(): pl.pallas_call(load_kernel, in_specs=[pl.BlockSpec(memory_space=pltpu.HBM...  3.39 us
  transfers between devices with their start and end apart: 24, of which 12 were waited for; matrix products, arithmetic and copies ran while one was open for 0% of the time, Pallas kernels for 18%

profile of v3, /device:TPU:0, one launch (start us, length us, event | category | flops | bytes accessed | tf_op | source)
XLA Modules:
  0.0 57.1 jit_solution(9168767135353769042)
XLA Ops:
  0.0 4.8 %project.1 = (f32[256,128]{1,0:T(8,128)S(1)}, bf16[256,128]{1,0:T(8,128)(2,1)S(1)}, bf16[256,128]{1,0:T(8,128)(2,1)S(1)}, bf16[256,128]{1,0:T(8,128)(2,1)S(1)}) custom-call(bf16[1024,2048]{1,0:T(8,128)(2,1)} %act_hbm.1, bf16[1024,2048]{1,0:T(8,128)(2,1)} %grad_hbm.1, bf16[64,2048]{1,0:T(8,128)(2,1)} %bitcast.6, bf16[64,2048]{1,0:T(8,128)(2,1)} %bitcast.7), custom_call_target="tpu_custom_call" | custom-call | tf_op jit(solution)/shard_map/project/pallas_call | solution.py:62
  4.8 3.1 %collective-permute-start = (bf16[256,128]{1,0:T(8,128)(2,1)S(1)}, bf16[256,128]{1,0:T(8,128)(2,1)S(1)}, u32[]{:S(2)}, u32[]{:S(2)}) collective-permute-start(bf16[256,128]{1,0:T(8,128)(2,1)S(1)} %get-tuple-element.16), channel_id=1, source_target_pairs={{0,4},{4,8},{8,12},{12,0},{1,5},{5,9},{9,13},{13,1},{2,6},{6,10},{... | collective-permute-start | bytes 196616 | tf_op jit(solution)/shard_map/ppermute | solution.py:252
  7.9 2.6 %collective-permute-start.1 = (bf16[256,128]{1,0:T(8,128)(2,1)S(1)}, bf16[256,128]{1,0:T(8,128)(2,1)S(1)}, u32[]{:S(2)}, u32[]{:S(2)}) collective-permute-start(bf16[256,128]{1,0:T(8,128)(2,1)S(1)} %get-tuple-element.17), channel_id=1, source_target_pairs={{0,8},{4,12},{8,0},{12,4},{1,9},{5,13},{9,1},{13,5},{2,10},{6,14},... | collective-permute-start | bytes 196616 | tf_op jit(solution)/shard_map/ppermute | solution.py:252
  10.4 1.3 %collective-permute-start.2 = (bf16[256,128]{1,0:T(8,128)(2,1)S(1)}, bf16[256,128]{1,0:T(8,128)(2,1)S(1)}, u32[]{:S(2)}, u32[]{:S(2)}) collective-permute-start(bf16[256,128]{1,0:T(8,128)(2,1)S(1)} %get-tuple-element.18), channel_id=1, source_target_pairs={{0,12},{4,0},{8,4},{12,8},{1,13},{5,1},{9,5},{13,9},{2,14},{6,2},{... | collective-permute-start | bytes 196616 | tf_op jit(solution)/shard_map/ppermute | solution.py:252
  11.8 0.6 %collective-permute-done = bf16[256,128]{1,0:T(8,128)(2,1)S(1)} collective-permute-done((bf16[256,128]{1,0:T(8,128)(2,1)S(1)}, bf16[256,128]{1,0:T(8,128)(2,1)S(1)}, u32[]{:S(2)}, u32[]{:S(2)}) %collective-permute-start) | collective-permute-done | bytes 65568 | tf_op jit(solution)/shard_map/ppermute | solution.py:252
  12.4 2.5 %collective-permute-done.1 = bf16[256,128]{1,0:T(8,128)(2,1)S(1)} collective-permute-done((bf16[256,128]{1,0:T(8,128)(2,1)S(1)}, bf16[256,128]{1,0:T(8,128)(2,1)S(1)}, u32[]{:S(2)}, u32[]{:S(2)}) %collective-permute-start.1) | collective-permute-done | bytes 65568 | tf_op jit(solution)/shard_map/ppermute | solution.py:252
  14.9 0.2 collective-permute-done.2
  15.2 0.1 collective-permute-start.3
  15.3 0.2 convert_reduce_fusion
  15.5 1.6 %collective-permute-start.4 = (bf16[256,128]{1,0:T(8,128)(2,1)S(1)}, bf16[256,128]{1,0:T(8,128)(2,1)S(1)}, u32[]{:S(2)}, u32[]{:S(2)}) collective-permute-start(bf16[256,128]{1,0:T(8,128)(2,1)S(1)} %add_convert_fusion.rest_0_), channel_id=1, source_target_pairs={{0,4},{4,8},{8,12},{12,0},{1,5},{5,9},{9,13},{13,1},{2,6},{6,10},{... | collective-permute-start | bytes 196616 | tf_op jit(solution)/shard_map/ppermute | solution.py:252
  17.1 2.0 %collective-permute-start.5 = (bf16[256,128]{1,0:T(8,128)(2,1)S(1)}, bf16[256,128]{1,0:T(8,128)(2,1)S(1)}, u32[]{:S(2)}, u32[]{:S(2)}) collective-permute-start(bf16[256,128]{1,0:T(8,128)(2,1)S(1)} %add_convert_fusion.rest_0_), channel_id=1, source_target_pairs={{0,8},{4,12},{8,0},{12,4},{1,9},{5,13},{9,1},{13,5},{2,10},{6,14},... | collective-permute-start | bytes 196616 | tf_op jit(solution)/shard_map/ppermute | solution.py:252
  19.2 0.4 collective-permute-start.6
  19.6 3.4 %load.1.rest_4_ = bf16[1024,4096]{1,0:T(8,128)(2,1)S(1)} custom-call(bf16[1024,4096]{1,0:T(8,128)(2,1)} %hbm_ref), custom_call_target="tpu_custom_call" | custom-call | bytes 33554432 | tf_op jit(solution)/shard_map/load/pallas_call | solution.py:87
  23.0 1.7 %collective-permute-done.5.rest_2_ = bf16[256,128]{1,0:T(8,128)(2,1)S(1)} collective-permute-done((bf16[256,128]{1,0:T(8,128)(2,1)S(1)}, bf16[256,128]{1,0:T(8,128)(2,1)S(1)}, u32[]{:S(2)}, u32[]{:S(2)}) %collective-permute-start.5) | collective-permute-done | bytes 65568 | tf_op jit(solution)/shard_map/ppermute | solution.py:252
  24.7 0.0 collective-permute-done.6.rest_3_
  24.7 4.5 %query.1 = (bf16[512,128]{1,0:T(8,128)(2,1)S(1)}, bf16[512,128]{1,0:T(8,128)(2,1)S(1)}) custom-call(s32[16]{0:T(128)S(1)} %fusion.start_ref, s32[8,128]{1,0:T(8,128)S(1)} %bitcast.5, bf16[256,128]{1,0:T(8,128)(2,1)S(1)} %add_convert_fusion.rest_0_, bf16[256,128]{1,0:T(8,128)(2,1)S(1)} %collective-permute-done.4.rest_1_, ...), custom_call_target="tpu_custom_call" | custom-call | tf_op jit(solution)/shard_map/query/pallas_call | solution.py:153
  29.3 1.9 %collective-permute-start.7 = (bf16[512,128]{1,0:T(8,128)(2,1)S(1)}, bf16[512,128]{1,0:T(8,128)(2,1)S(1)}, u32[]{:S(2)}, u32[]{:S(2)}) collective-permute-start(bf16[512,128]{1,0:T(8,128)(2,1)S(1)} %get-tuple-element.21.rest_0_), channel_id=1, source_target_pairs={{0,4},{1,5},{4,8},{5,9},{8,12},{9,13},{12,14},{13,15},{14,10},{15,... | collective-permute-start | bytes 393224 | tf_op jit(solution)/shard_map/ppermute | solution.py:288
  31.2 0.2 collective-permute-start.16
  31.3 1.5 %collective-permute-start.10 = (bf16[512,128]{1,0:T(8,128)(2,1)S(1)}, bf16[512,128]{1,0:T(8,128)(2,1)S(1)}, u32[]{:S(2)}, u32[]{:S(2)}) collective-permute-start(bf16[512,128]{1,0:T(8,128)(2,1)S(1)} %get-tuple-element.21.rest_0_), channel_id=1, source_target_pairs={{0,2},{1,3},{4,0},{5,1},{8,4},{9,5},{12,8},{13,9},{14,12},{15,13},... | collective-permute-start | bytes 393224 | tf_op jit(solution)/shard_map/ppermute | solution.py:289
  32.8 0.5 collective-permute-start.13
  33.4 1.7 %collective-permute-done.7.rest_2_ = bf16[512,128]{1,0:T(8,128)(2,1)S(1)} collective-permute-done((bf16[512,128]{1,0:T(8,128)(2,1)S(1)}, bf16[512,128]{1,0:T(8,128)(2,1)S(1)}, u32[]{:S(2)}, u32[]{:S(2)}) %collective-permute-start.7) | collective-permute-done | bytes 131104 | tf_op jit(solution)/shard_map/ppermute | solution.py:288
  35.1 2.5 %collective-permute-start.8 = (bf16[512,128]{1,0:T(8,128)(2,1)S(1)}, bf16[512,128]{1,0:T(8,128)(2,1)S(1)}, u32[]{:S(2)}, u32[]{:S(2)}) collective-permute-start(bf16[512,128]{1,0:T(8,128)(2,1)S(1)} %collective-permute-done.7.rest_2_), channel_id=1, source_target_pairs={{0,4},{1,5},{4,8},{5,9},{8,12},{9,13},{12,14},{13,15},{14,10},{15,... | collective-permute-start | bytes 393224 | tf_op jit(solution)/shard_map/ppermute | solution.py:288
  37.5 0.0 collective-permute-done.16.rest_5_
  37.6 0.1 collective-permute-start.17
  37.7 2.4 %collective-permute-done.10.rest_3_ = bf16[512,128]{1,0:T(8,128)(2,1)S(1)} collective-permute-done((bf16[512,128]{1,0:T(8,128)(2,1)S(1)}, bf16[512,128]{1,0:T(8,128)(2,1)S(1)}, u32[]{:S(2)}, u32[]{:S(2)}) %collective-permute-start.10) | collective-permute-done | bytes 131104 | tf_op jit(solution)/shard_map/ppermute | solution.py:289
  40.1 0.3 collective-permute-start.11
  40.4 1.7 %collective-permute-start.14 = (bf16[512,128]{1,0:T(8,128)(2,1)S(1)}, bf16[512,128]{1,0:T(8,128)(2,1)S(1)}, u32[]{:S(2)}, u32[]{:S(2)}) collective-permute-start(bf16[512,128]{1,0:T(8,128)(2,1)S(1)} %collective-permute-done.13.rest_4_), channel_id=1, source_target_pairs={{0,4},{1,5},{4,8},{5,9},{8,12},{9,13},{12,14},{13,15},{14,10},{15,... | collective-permute-start | bytes 393224 | tf_op jit(solution)/shard_map/ppermute | solution.py:288
  42.1 0.0 collective-permute-done.8.rest_6_
  42.1 0.5 collective-permute-start.9
  42.6 0.9 %collective-permute-done.17.rest_9_ = bf16[512,128]{1,0:T(8,128)(2,1)S(1)} collective-permute-done((bf16[512,128]{1,0:T(8,128)(2,1)S(1)}, bf16[512,128]{1,0:T(8,128)(2,1)S(1)}, u32[]{:S(2)}, u32[]{:S(2)}) %collective-permute-start.17) | collective-permute-done | bytes 131104 | tf_op jit(solution)/shard_map/ppermute | solution.py:289
  43.5 0.6 %collective-permute-start.18 = (bf16[512,128]{1,0:T(8,128)(2,1)S(1)}, bf16[512,128]{1,0:T(8,128)(2,1)S(1)}, u32[]{:S(2)}, u32[]{:S(2)}) collective-permute-start(bf16[512,128]{1,0:T(8,128)(2,1)S(1)} %collective-permute-done.17.rest_9_), channel_id=1, source_target_pairs={{0,2},{1,3},{4,0},{5,1},{8,4},{9,5},{12,8},{13,9},{14,12},{15,13},... | collective-permute-start | bytes 393224 | tf_op jit(solution)/shard_map/ppermute | solution.py:289
  44.2 2.3 %collective-permute-done.11.rest_7_ = bf16[512,128]{1,0:T(8,128)(2,1)S(1)} collective-permute-done((bf16[512,128]{1,0:T(8,128)(2,1)S(1)}, bf16[512,128]{1,0:T(8,128)(2,1)S(1)}, u32[]{:S(2)}, u32[]{:S(2)}) %collective-permute-start.11) | collective-permute-done | bytes 131104 | tf_op jit(solution)/shard_map/ppermute | solution.py:289
  46.5 0.3 collective-permute-start.12
  46.8 0.0 collective-permute-done.14.rest_8_
  46.8 1.7 %collective-permute-start.15 = (bf16[512,128]{1,0:T(8,128)(2,1)S(1)}, bf16[512,128]{1,0:T(8,128)(2,1)S(1)}, u32[]{:S(2)}, u32[]{:S(2)}) collective-permute-start(bf16[512,128]{1,0:T(8,128)(2,1)S(1)} %collective-permute-done.14.rest_8_), channel_id=1, source_target_pairs={{0,4},{1,5},{4,8},{5,9},{8,12},{9,13},{12,14},{13,15},{14,10},{15,... | collective-permute-start | bytes 393224 | tf_op jit(solution)/shard_map/ppermute | solution.py:288
  48.5 0.0 collective-permute-done.9.rest_0_
  48.5 1.0 %collective-permute-start.20 = (bf16[512,128]{1,0:T(8,128)(2,1)S(1)}, bf16[512,128]{1,0:T(8,128)(2,1)S(1)}, u32[]{:S(2)}, u32[]{:S(2)}) collective-permute-start(bf16[512,128]{1,0:T(8,128)(2,1)S(1)} %collective-permute-done.9.rest_0_), channel_id=1, source_target_pairs={{0,4},{1,5},{4,8},{5,9},{8,12},{9,13},{12,14},{13,15},{14,10},{15,... | collective-permute-start | bytes 393224 | tf_op jit(solution)/shard_map/ppermute | solution.py:288
  49.5 1.0 %collective-permute-start.21 = (bf16[512,128]{1,0:T(8,128)(2,1)S(1)}, bf16[512,128]{1,0:T(8,128)(2,1)S(1)}, u32[]{:S(2)}, u32[]{:S(2)}) collective-permute-start(bf16[512,128]{1,0:T(8,128)(2,1)S(1)} %collective-permute-done.18.rest_3_), channel_id=1, source_target_pairs={{0,2},{1,3},{4,0},{5,1},{8,4},{9,5},{12,8},{13,9},{14,12},{15,13},... | collective-permute-start | bytes 393224 | tf_op jit(solution)/shard_map/ppermute | solution.py:289
  50.5 1.6 %early_scores.2.rest_4_ = f32[2,2,256,128]{3,2,1,0:T(8,128)S(1)} custom-call(bf16[256,4096]{1,0:T(8,128)(2,1)S(1)} %copy-done, bf16[256,4096]{1,0:T(8,128)(2,1)S(1)} %collective-permute-done.3.other_ref, bf16[512,128]{1,0:T(8,128)(2,1)S(1)} %get-tuple-element.21.rest_0_, bf16[512,128]{1,0:T(8,128)(2,1)S(1)} %get-tuple-element.22.rest_1_, ...), custom_call_target="tpu_custom_call" | custom-call | tf_op jit(solution)/shard_map/early_scores/pallas_call | solution.py:200
  52.1 0.0 collective-permute-done.15.rest_2_
  52.1 0.9 %early_scores.3 = (f32[256,256]{1,0:T(8,128)S(1)}, f32[256,256]{1,0:T(8,128)S(1)}) custom-call(bf16[256,4096]{1,0:T(8,128)(2,1)S(1)} %copy-done, bf16[256,4096]{1,0:T(8,128)(2,1)S(1)} %collective-permute-done.3.other_ref, bf16[512,128]{1,0:T(8,128)(2,1)S(1)} %collective-permute-done.9.rest_0_, bf16[512,128]{1,0:T(8,128)(2,1)S(1)} %collective-permute-done.12.rest_1_, ...), custom_call_target="tpu_custom_call" | custom-call | tf_op jit(solution)/shard_map/early_scores/pallas_call | solution.py:200
  53.1 0.1 collective-permute-start.19
  53.2 0.3 collective-permute-done.20.rest_0_
  53.5 0.2 collective-permute-start.22
  53.7 0.8 %collective-permute-done.21.rest_1_ = bf16[512,128]{1,0:T(8,128)(2,1)S(1)} collective-permute-done((bf16[512,128]{1,0:T(8,128)(2,1)S(1)}, bf16[512,128]{1,0:T(8,128)(2,1)S(1)}, u32[]{:S(2)}, u32[]{:S(2)}) %collective-permute-start.21) | collective-permute-done | bytes 131104 | tf_op jit(solution)/shard_map/ppermute | solution.py:289
  54.5 0.4 collective-permute-done.22.rest_2_
  54.9 0.9 %collective-permute-done.23.rest_3_ = bf16[512,128]{1,0:T(8,128)(2,1)S(1)} collective-permute-done((bf16[512,128]{1,0:T(8,128)(2,1)S(1)}, bf16[512,128]{1,0:T(8,128)(2,1)S(1)}, u32[]{:S(2)}, u32[]{:S(2)}) %collective-permute-start.23) | collective-permute-done | bytes 131104 | tf_op jit(solution)/shard_map/ppermute | solution.py:306
  55.8 1.3 %final_scores.1 = f32[512,256]{1,0:T(8,128)} custom-call(bf16[256,4096]{1,0:T(8,128)(2,1)S(1)} %copy-done, f32[256,256]{1,0:T(8,128)S(1)} %get-tuple-element.23.keep_ref, f32[256,256]{1,0:T(8,128)S(1)} %collective-permute-done.19.got_ref, bf16[512,128]{1,0:T(8,128)(2,1)S(1)} %collective-permute-done.20.rest_0_, ...), custom_call_target="tpu_custom_call" | custom-call | tf_op jit(solution)/shard_map/final_scores/pallas_call | solution.py:232
  (14 shorter events, 0.1 us)
Async XLA Ops:
  0.0 15.2 %copy-start = (bf16[256,4096]{1,0:T(8,128)(2,1)S(1)}, bf16[256,4096]{1,0:T(8,128)(2,1)}, u32[]{:S(2)}) copy-start(bf16[256,4096]{1,0:T(8,128)(2,1)} %stored_ref) | copy-start | bytes 6291460
  0.0 15.3 %copy-start.1 = (s32[1,1024]{1,0:T(1,128)S(1)}, s32[1,1024]{1,0:T(1,128)}, u32[]{:S(2)}) copy-start(s32[1,1024]{1,0:T(1,128)} %param.9) | copy-start | bytes 12292
  4.8 7.6 %collective-permute-start = (bf16[256,128]{1,0:T(8,128)(2,1)S(1)}, bf16[256,128]{1,0:T(8,128)(2,1)S(1)}, u32[]{:S(2)}, u32[]{:S(2)}) collective-permute-start(bf16[256,128]{1,0:T(8,128)(2,1)S(1)} %get-tuple-element.16), channel_id=1, source_target_pairs={{0,4},{4,8},{8,12},{12,0},{1,5},{5,9},{9,13},{13,1},{2,6},{6,10},{... | collective-permute-start | bytes 196616 | tf_op jit(solution)/shard_map/ppermute | solution.py:252
  7.9 7.1 %collective-permute-start.1 = (bf16[256,128]{1,0:T(8,128)(2,1)S(1)}, bf16[256,128]{1,0:T(8,128)(2,1)S(1)}, u32[]{:S(2)}, u32[]{:S(2)}) collective-permute-start(bf16[256,128]{1,0:T(8,128)(2,1)S(1)} %get-tuple-element.17), channel_id=1, source_target_pairs={{0,8},{4,12},{8,0},{12,4},{1,9},{5,13},{9,1},{13,5},{2,10},{6,14},... | collective-permute-start | bytes 196616 | tf_op jit(solution)/shard_map/ppermute | solution.py:252
  10.4 4.7 %collective-permute-start.2 = (bf16[256,128]{1,0:T(8,128)(2,1)S(1)}, bf16[256,128]{1,0:T(8,128)(2,1)S(1)}, u32[]{:S(2)}, u32[]{:S(2)}) collective-permute-start(bf16[256,128]{1,0:T(8,128)(2,1)S(1)} %get-tuple-element.18), channel_id=1, source_target_pairs={{0,12},{4,0},{8,4},{12,8},{1,13},{5,1},{9,5},{13,9},{2,14},{6,2},{... | collective-permute-start | bytes 196616 | tf_op jit(solution)/shard_map/ppermute | solution.py:252
  15.2 35.3 %collective-permute-start.3 = (bf16[256,4096]{1,0:T(8,128)(2,1)S(1)}, bf16[256,4096]{1,0:T(8,128)(2,1)S(1)}, u32[]{:S(2)}, u32[]{:S(2)}) collective-permute-start(bf16[256,4096]{1,0:T(8,128)(2,1)S(1)} %copy-done), channel_id=1, source_target_pairs={{0,1},{1,0},{2,3},{3,2},{4,5},{5,4},{6,7},{7,6},{8,9},{9,8},{10,11... | collective-permute-start | bytes 6291464 | tf_op jit(solution)/shard_map/ppermute | solution.py:282
  15.5 7.5 %collective-permute-start.4 = (bf16[256,128]{1,0:T(8,128)(2,1)S(1)}, bf16[256,128]{1,0:T(8,128)(2,1)S(1)}, u32[]{:S(2)}, u32[]{:S(2)}) collective-permute-start(bf16[256,128]{1,0:T(8,128)(2,1)S(1)} %add_convert_fusion.rest_0_), channel_id=1, source_target_pairs={{0,4},{4,8},{8,12},{12,0},{1,5},{5,9},{9,13},{13,1},{2,6},{6,10},{... | collective-permute-start | bytes 196616 | tf_op jit(solution)/shard_map/ppermute | solution.py:252
  17.1 7.6 %collective-permute-start.5 = (bf16[256,128]{1,0:T(8,128)(2,1)S(1)}, bf16[256,128]{1,0:T(8,128)(2,1)S(1)}, u32[]{:S(2)}, u32[]{:S(2)}) collective-permute-start(bf16[256,128]{1,0:T(8,128)(2,1)S(1)} %add_convert_fusion.rest_0_), channel_id=1, source_target_pairs={{0,8},{4,12},{8,0},{12,4},{1,9},{5,13},{9,1},{13,5},{2,10},{6,14},... | collective-permute-start | bytes 196616 | tf_op jit(solution)/shard_map/ppermute | solution.py:252
  19.2 5.6 %collective-permute-start.6 = (bf16[256,128]{1,0:T(8,128)(2,1)S(1)}, bf16[256,128]{1,0:T(8,128)(2,1)S(1)}, u32[]{:S(2)}, u32[]{:S(2)}) collective-permute-start(bf16[256,128]{1,0:T(8,128)(2,1)S(1)} %add_convert_fusion.rest_0_), channel_id=1, source_target_pairs={{0,12},{4,0},{8,4},{12,8},{1,13},{5,1},{9,5},{13,9},{2,14},{6,2},{... | collective-permute-start | bytes 196616 | tf_op jit(solution)/shard_map/ppermute | solution.py:252
  29.3 5.8 %collective-permute-start.7 = (bf16[512,128]{1,0:T(8,128)(2,1)S(1)}, bf16[512,128]{1,0:T(8,128)(2,1)S(1)}, u32[]{:S(2)}, u32[]{:S(2)}) collective-permute-start(bf16[512,128]{1,0:T(8,128)(2,1)S(1)} %get-tuple-element.21.rest_0_), channel_id=1, source_target_pairs={{0,4},{1,5},{4,8},{5,9},{8,12},{9,13},{12,14},{13,15},{14,10},{15,... | collective-permute-start | bytes 393224 | tf_op jit(solution)/shard_map/ppermute | solution.py:288
  31.2 6.4 %collective-permute-start.16 = (bf16[512,128]{1,0:T(8,128)(2,1)S(1)}, bf16[512,128]{1,0:T(8,128)(2,1)S(1)}, u32[]{:S(2)}, u32[]{:S(2)}) collective-permute-start(bf16[512,128]{1,0:T(8,128)(2,1)S(1)} %get-tuple-element.22.rest_1_), channel_id=1, source_target_pairs={{0,2},{1,3},{4,0},{5,1},{8,4},{9,5},{12,8},{13,9},{14,12},{15,13},... | collective-permute-start | bytes 393224 | tf_op jit(solution)/shard_map/ppermute | solution.py:289
  31.3 8.8 %collective-permute-start.10 = (bf16[512,128]{1,0:T(8,128)(2,1)S(1)}, bf16[512,128]{1,0:T(8,128)(2,1)S(1)}, u32[]{:S(2)}, u32[]{:S(2)}) collective-permute-start(bf16[512,128]{1,0:T(8,128)(2,1)S(1)} %get-tuple-element.21.rest_0_), channel_id=1, source_target_pairs={{0,2},{1,3},{4,0},{5,1},{8,4},{9,5},{12,8},{13,9},{14,12},{15,13},... | collective-permute-start | bytes 393224 | tf_op jit(solution)/shard_map/ppermute | solution.py:289
  32.8 7.5 %collective-permute-start.13 = (bf16[512,128]{1,0:T(8,128)(2,1)S(1)}, bf16[512,128]{1,0:T(8,128)(2,1)S(1)}, u32[]{:S(2)}, u32[]{:S(2)}) collective-permute-start(bf16[512,128]{1,0:T(8,128)(2,1)S(1)} %get-tuple-element.22.rest_1_), channel_id=1, source_target_pairs={{0,4},{1,5},{4,8},{5,9},{8,12},{9,13},{12,14},{13,15},{14,10},{15,... | collective-permute-start | bytes 393224 | tf_op jit(solution)/shard_map/ppermute | solution.py:288
  35.1 7.1 %collective-permute-start.8 = (bf16[512,128]{1,0:T(8,128)(2,1)S(1)}, bf16[512,128]{1,0:T(8,128)(2,1)S(1)}, u32[]{:S(2)}, u32[]{:S(2)}) collective-permute-start(bf16[512,128]{1,0:T(8,128)(2,1)S(1)} %collective-permute-done.7.rest_2_), channel_id=1, source_target_pairs={{0,4},{1,5},{4,8},{5,9},{8,12},{9,13},{12,14},{13,15},{14,10},{15,... | collective-permute-start | bytes 393224 | tf_op jit(solution)/shard_map/ppermute | solution.py:288
  37.6 6.0 %collective-permute-start.17 = (bf16[512,128]{1,0:T(8,128)(2,1)S(1)}, bf16[512,128]{1,0:T(8,128)(2,1)S(1)}, u32[]{:S(2)}, u32[]{:S(2)}) collective-permute-start(bf16[512,128]{1,0:T(8,128)(2,1)S(1)} %collective-permute-done.16.rest_5_), channel_id=1, source_target_pairs={{0,2},{1,3},{4,0},{5,1},{8,4},{9,5},{12,8},{13,9},{14,12},{15,13},... | collective-permute-start | bytes 393224 | tf_op jit(solution)/shard_map/ppermute | solution.py:289
  40.1 6.4 %collective-permute-start.11 = (bf16[512,128]{1,0:T(8,128)(2,1)S(1)}, bf16[512,128]{1,0:T(8,128)(2,1)S(1)}, u32[]{:S(2)}, u32[]{:S(2)}) collective-permute-start(bf16[512,128]{1,0:T(8,128)(2,1)S(1)} %collective-permute-done.10.rest_3_), channel_id=1, source_target_pairs={{0,2},{1,3},{4,0},{5,1},{8,4},{9,5},{12,8},{13,9},{14,12},{15,13},... | collective-permute-start | bytes 393224 | tf_op jit(solution)/shard_map/ppermute | solution.py:289
  40.4 6.4 %collective-permute-start.14 = (bf16[512,128]{1,0:T(8,128)(2,1)S(1)}, bf16[512,128]{1,0:T(8,128)(2,1)S(1)}, u32[]{:S(2)}, u32[]{:S(2)}) collective-permute-start(bf16[512,128]{1,0:T(8,128)(2,1)S(1)} %collective-permute-done.13.rest_4_), channel_id=1, source_target_pairs={{0,4},{1,5},{4,8},{5,9},{8,12},{9,13},{12,14},{13,15},{14,10},{15,... | collective-permute-start | bytes 393224 | tf_op jit(solution)/shard_map/ppermute | solution.py:288
  42.1 6.4 %collective-permute-start.9 = (bf16[512,128]{1,0:T(8,128)(2,1)S(1)}, bf16[512,128]{1,0:T(8,128)(2,1)S(1)}, u32[]{:S(2)}, u32[]{:S(2)}) collective-permute-start(bf16[512,128]{1,0:T(8,128)(2,1)S(1)} %collective-permute-done.8.rest_6_), channel_id=1, source_target_pairs={{0,4},{1,5},{4,8},{5,9},{8,12},{9,13},{12,14},{13,15},{14,10},{15,... | collective-permute-start | bytes 393224 | tf_op jit(solution)/shard_map/ppermute | solution.py:288
  43.5 5.9 %collective-permute-start.18 = (bf16[512,128]{1,0:T(8,128)(2,1)S(1)}, bf16[512,128]{1,0:T(8,128)(2,1)S(1)}, u32[]{:S(2)}, u32[]{:S(2)}) collective-permute-start(bf16[512,128]{1,0:T(8,128)(2,1)S(1)} %collective-permute-done.17.rest_9_), channel_id=1, source_target_pairs={{0,2},{1,3},{4,0},{5,1},{8,4},{9,5},{12,8},{13,9},{14,12},{15,13},... | collective-permute-start | bytes 393224 | tf_op jit(solution)/shard_map/ppermute | solution.py:289
  46.5 5.7 %collective-permute-start.12 = (bf16[512,128]{1,0:T(8,128)(2,1)S(1)}, bf16[512,128]{1,0:T(8,128)(2,1)S(1)}, u32[]{:S(2)}, u32[]{:S(2)}) collective-permute-start(bf16[512,128]{1,0:T(8,128)(2,1)S(1)} %collective-permute-done.11.rest_7_), channel_id=1, source_target_pairs={{0,2},{1,3},{4,0},{5,1},{8,4},{9,5},{12,8},{13,9},{14,12},{15,13},... | collective-permute-start | bytes 393224 | tf_op jit(solution)/shard_map/ppermute | solution.py:289
  46.8 5.4 %collective-permute-start.15 = (bf16[512,128]{1,0:T(8,128)(2,1)S(1)}, bf16[512,128]{1,0:T(8,128)(2,1)S(1)}, u32[]{:S(2)}, u32[]{:S(2)}) collective-permute-start(bf16[512,128]{1,0:T(8,128)(2,1)S(1)} %collective-permute-done.14.rest_8_), channel_id=1, source_target_pairs={{0,4},{1,5},{4,8},{5,9},{8,12},{9,13},{12,14},{13,15},{14,10},{15,... | collective-permute-start | bytes 393224 | tf_op jit(solution)/shard_map/ppermute | solution.py:288
  48.5 5.0 %collective-permute-start.20 = (bf16[512,128]{1,0:T(8,128)(2,1)S(1)}, bf16[512,128]{1,0:T(8,128)(2,1)S(1)}, u32[]{:S(2)}, u32[]{:S(2)}) collective-permute-start(bf16[512,128]{1,0:T(8,128)(2,1)S(1)} %collective-permute-done.9.rest_0_), channel_id=1, source_target_pairs={{0,4},{1,5},{4,8},{5,9},{8,12},{9,13},{12,14},{13,15},{14,10},{15,... | collective-permute-start | bytes 393224 | tf_op jit(solution)/shard_map/ppermute | solution.py:288
  49.5 5.0 %collective-permute-start.21 = (bf16[512,128]{1,0:T(8,128)(2,1)S(1)}, bf16[512,128]{1,0:T(8,128)(2,1)S(1)}, u32[]{:S(2)}, u32[]{:S(2)}) collective-permute-start(bf16[512,128]{1,0:T(8,128)(2,1)S(1)} %collective-permute-done.18.rest_3_), channel_id=1, source_target_pairs={{0,2},{1,3},{4,0},{5,1},{8,4},{9,5},{12,8},{13,9},{14,12},{15,13},... | collective-permute-start | bytes 393224 | tf_op jit(solution)/shard_map/ppermute | solution.py:289
  53.1 2.7 %collective-permute-start.19 = (f32[256,256]{1,0:T(8,128)S(1)}, f32[256,256]{1,0:T(8,128)S(1)}, u32[]{:S(2)}, u32[]{:S(2)}) collective-permute-start(f32[256,256]{1,0:T(8,128)S(1)} %get-tuple-element.24), channel_id=1, source_target_pairs={{0,1},{1,0},{2,3},{3,2},{4,5},{5,4},{6,7},{7,6},{8,9},{9,8},{10,11... | collective-permute-start | bytes 786440 | tf_op jit(solution)/shard_map/ppermute | solution.py:305
  53.5 1.4 %collective-permute-start.22 = (bf16[512,128]{1,0:T(8,128)(2,1)S(1)}, bf16[512,128]{1,0:T(8,128)(2,1)S(1)}, u32[]{:S(2)}, u32[]{:S(2)}) collective-permute-start(bf16[512,128]{1,0:T(8,128)(2,1)S(1)} %collective-permute-done.20.rest_0_), channel_id=1, source_target_pairs={{0,1},{1,0},{2,3},{3,2},{4,5},{5,4},{6,7},{7,6},{8,9},{9,8},{10,11... | collective-permute-start | bytes 393224 | tf_op jit(solution)/shard_map/ppermute | solution.py:306
  54.5 1.3 %collective-permute-start.23 = (bf16[512,128]{1,0:T(8,128)(2,1)S(1)}, bf16[512,128]{1,0:T(8,128)(2,1)S(1)}, u32[]{:S(2)}, u32[]{:S(2)}) collective-permute-start(bf16[512,128]{1,0:T(8,128)(2,1)S(1)} %collective-permute-done.21.rest_1_), channel_id=1, source_target_pairs={{0,1},{1,0},{2,3},{3,2},{4,5},{5,4},{6,7},{7,6},{8,9},{9,8},{10,11... | collective-permute-start | bytes 393224 | tf_op jit(solution)/shard_map/ppermute | solution.py:306

commit v4 on v3

--- a/solution.py
+++ b/solution.py
@@ -17,87 +17,94 @@
 in_hbm = lambda x: pltpu.with_memory_space_constraint(x, pltpu.HBM)
 
 
-def project_kernel(planes, act_hbm, grad_hbm, pin_hbm, pout_hbm, *rest):
-    outs, (act, grad, win, wout, weight, sems) = rest[:planes], rest[planes:]
-    rank = pin_hbm.shape[0]
-    rows = act.shape[0] // planes
+def project_kernel(planes, turns, act_hbm, grad_hbm, pin_hbm, pout_hbm, *rest):
+    outs, (act, grad, win, wout, weight, sems) = rest[: len(turns)], rest[len(turns) :]
+    rank, depth = pin_hbm.shape
+    rows = act.shape[1]
+    me = lax.axis_index("width")
     loads = [
         pltpu.make_async_copy(pin_hbm, win.at[pl.ds(0, rank)], sems.at[0]),
         pltpu.make_async_copy(pout_hbm, wout.at[pl.ds(rank, rank)], sems.at[1]),
     ]
-    copies = [
-        [
-            pltpu.make_async_copy(hbm.at[pl.ds(i * rows, rows)], ref.at[pl.ds(i * rows, rows)], sems.at[2 + 2 * i + n])
-            for n, (hbm, ref) in enumerate(((act_hbm, act), (grad_hbm, grad)))
-        ]
-        for i in range(planes)
-    ]
+    copies = []
+    for n, d in enumerate(turns):
+        at = pl.ds(pl.multiple_of(lax.rem(me + d, planes) * rows, rows), rows)
+        copies.append(
+            [
+                pltpu.make_async_copy(act_hbm.at[at], act.at[n], sems.at[2 + 2 * n]),
+                pltpu.make_async_copy(grad_hbm.at[at], grad.at[n], sems.at[3 + 2 * n]),
+            ]
+        )
     for copy in sum(copies, loads):
         copy.start()
-    win[rank:, :] = jnp.zeros(win[rank:, :].shape, BF16)
-    wout[:rank, :] = jnp.zeros(wout[:rank, :].shape, BF16)
+    win[rank:, :] = jnp.zeros((rank, depth), BF16)
+    wout[:rank, :] = jnp.zeros((rank, depth), BF16)
     for copy in loads:
         copy.wait()
     weight[0] = win[...].T
     weight[1] = wout[...].T
-    me = lax.axis_index("width")
-    for i, pair in enumerate(copies):
-        away = lax.rem(i - me + planes, planes)
-        at = pl.ds(i * rows, rows)
+    for n, (pair, out) in enumerate(zip(copies, outs)):
         for copy in pair:
             copy.wait()
-        part = jnp.dot(act[at, :], weight[0], preferred_element_type=F32)
-        part += jnp.dot(grad[at, :], weight[1], preferred_element_type=F32)
-        for d, out in enumerate(outs):
-
-            @pl.when(away == d)
-            def _(out=out, part=part):
-                out[...] = part.astype(out.dtype)
-
-
-def project(activations, out_grads, proj_in, proj_out, planes):
+        part = jnp.dot(act[n], weight[0], preferred_element_type=F32)
+        part += jnp.dot(grad[n], weight[1], preferred_element_type=F32)
+        out[...] = part.astype(out.dtype)
+
+
+def project(activations, out_grads, proj_in, proj_out, planes, turns):
     tokens, depth = activations.shape
     rank = proj_in.shape[1]
     quarter = tokens // planes
+    operands = (activations, out_grads, proj_in.T, proj_out.T)
     return pl.pallas_call(
-        functools.partial(project_kernel, planes),
+        functools.partial(project_kernel, planes, turns),
         in_specs=[pl.BlockSpec(memory_space=pltpu.HBM)] * 4,
-        out_specs=[pl.BlockSpec(memory_space=pltpu.VMEM)] * planes,
-        out_shape=[pltpu.VMEM((quarter, 2 * rank), BF16 if d else F32) for d in range(planes)],
+        out_specs=[pl.BlockSpec(memory_space=pltpu.VMEM)] * len(turns),
+        out_shape=[pltpu.VMEM((quarter, 2 * rank), BF16 if d else F32) for d in turns],
         scratch_shapes=[
-            pltpu.VMEM((tokens, depth), BF16),
-            pltpu.VMEM((tokens, depth), BF16),
+            pltpu.VMEM((len(turns), quarter, depth), BF16),
+            pltpu.VMEM((len(turns), quarter, depth), BF16),
             pltpu.VMEM((2 * rank, depth), BF16),
             pltpu.VMEM((2 * rank, depth), BF16),
             pltpu.VMEM((2, depth, 2 * rank), BF16),
-            pltpu.SemaphoreType.DMA((2 + 2 * planes,)),
+            pltpu.SemaphoreType.DMA((2 + 2 * len(turns),)),
         ],
         compiler_params=pltpu.CompilerParams(vmem_limit_bytes=24 * MIB),
+        cost_estimate=pl.CostEstimate(
+            flops=4 * len(turns) * quarter * depth * rank,
+            bytes_accessed=8 * len(turns) * quarter * depth,
+            transcendentals=0,
+        ),
         name="project",
-    )(*(in_hbm(x) for x in (activations, out_grads, proj_in.T, proj_out.T)))
-
-
-def load_kernel(hbm_ref, out_ref, sem):
+    )(*(in_hbm(x) for x in operands))
+
+
+def load_kernel(ids_ref, hbm_ref, out_ref, start_ref, sem):
     copy = pltpu.make_async_copy(hbm_ref, out_ref, sem)
     copy.start()
+    chunks = ids_ref.shape[0]
+    for block in range(start_ref.shape[0]):
+        before = jnp.sum((ids_ref[...] < block * EX_BLOCK).astype(jnp.int32))
+        start_ref[block] = jnp.minimum(before // LANES, chunks - 2)
     copy.wait()
 
 
-def load(x):
+def load(ids, x):
+    vmem = pl.BlockSpec(memory_space=pltpu.VMEM)
     return pl.pallas_call(
         load_kernel,
-        in_specs=[pl.BlockSpec(memory_space=pltpu.HBM)],
-        out_specs=pl.BlockSpec(memory_space=pltpu.VMEM),
-        out_shape=pltpu.VMEM(x.shape, x.dtype),
+        in_specs=[vmem, pl.BlockSpec(memory_space=pltpu.HBM)],
+        out_specs=[vmem, pl.BlockSpec(memory_space=pltpu.SMEM)],
+        out_shape=[pltpu.VMEM(x.shape, x.dtype), pltpu.SMEM((EX_DEV // EX_BLOCK,), jnp.int32)],
         scratch_shapes=[pltpu.SemaphoreType.DMA],
         compiler_params=pltpu.CompilerParams(vmem_limit_bytes=20 * MIB),
         cost_estimate=pl.CostEstimate(flops=0, bytes_accessed=4 * x.size * x.dtype.itemsize, transcendentals=0),
         name="load",
-    )(in_hbm(x))
+    )(ids, in_hbm(x))
 
 
 def query_kernel(pieces, start_ref, ids_ref, *rest):
-    factor_refs, (ic_ref, *outs), (tok, spread, twice, pe) = rest[:pieces], rest[pieces:-4], rest[-4:]
+    factor_refs, (ic_ref, out_ref, pe, tok, spread, twice) = rest[:pieces], rest[pieces:]
     tokens, rank = tok.shape[0], tok.shape[1] // 2
     piece = tokens // pieces
     me = lax.axis_index("width") if pieces > 1 else 0
@@ -134,36 +141,48 @@
         for i in range(rank // 2):
             pe[pl.ds(pair * 2 * EX_BLOCK, 2 * EX_BLOCK), pl.ds(i * 2 * rank, 2 * rank)] = both[i]
 
-    rows = ic_ref.shape[0] // len(outs)
-    for j, out in enumerate(outs):
-        out[...] = lax.dot_general(
-            ic_ref[pl.ds(j * rows, rows), :], pe[...], NT, preferred_element_type=F32
-        ).astype(BF16)
-
-
-def query_transposed(factors, example_of, inverse_curvature, cuts):
-    tokens = example_of.shape[1]
-    chunks = tokens // LANES
-    firsts = jnp.arange(0, EX_DEV, EX_BLOCK, dtype=jnp.int32)
-    before = jnp.sum((example_of < firsts[:, None]).astype(jnp.int32), axis=1)
-    start = jnp.minimum(before // LANES, chunks - 2)
+    curve_kernel(0, pe, ic_ref, out_ref)
+
+
+def curve_kernel(cut, pe_ref, ic_ref, out_ref, parts=2):
+    rows = out_ref.shape[0]
+    step = rows // parts
+    for i in range(parts):
+        mine = ic_ref[pl.ds(cut * rows + i * step, step), :]
+        out_ref[pl.ds(i * step, step), :] = lax.dot_general(mine, pe_ref[...], NT, preferred_element_type=F32).astype(BF16)
+
+
+def query_transposed(factors, ids, start, inverse_curvature, cuts):
+    tokens = ids.shape[0] * LANES
     rank = factors[0].shape[1] // 2
     feats, width = inverse_curvature.shape
     vmem = pl.BlockSpec(memory_space=pltpu.VMEM)
-    return pl.pallas_call(
+    piece = pltpu.VMEM((feats // cuts, EX_DEV), BF16)
+    first, grads = pl.pallas_call(
         functools.partial(query_kernel, len(factors)),
         in_specs=[pl.BlockSpec(memory_space=pltpu.SMEM)] + [vmem] * (2 + len(factors)),
-        out_specs=[vmem] * cuts,
-        out_shape=[jax.ShapeDtypeStruct((feats // cuts, EX_DEV), BF16)] * cuts,
+        out_specs=[vmem] * 2,
+        out_shape=[piece, pltpu.VMEM((EX_DEV, width), BF16)],
         scratch_shapes=[
             pltpu.VMEM((tokens, 2 * rank), BF16),
             pltpu.VMEM((EX_BLOCK * rank, tokens), BF16),
             pltpu.VMEM((tokens, 2 * rank), BF16),
-            pltpu.VMEM((EX_DEV, width), BF16),
         ],
         compiler_params=pltpu.CompilerParams(vmem_limit_bytes=20 * MIB),
         name="query",
-    )(start, example_of.reshape(chunks, LANES), *factors, inverse_curvature)
+    )(start, ids, *factors, inverse_curvature)
+    return [first] + [
+        pl.pallas_call(
+            functools.partial(curve_kernel, cut),
+            in_specs=[vmem] * 2,
+            out_specs=vmem,
+            out_shape=piece,
+            compiler_params=pltpu.CompilerParams(vmem_limit_bytes=20 * MIB),
+            cost_estimate=pl.CostEstimate(flops=100 * feats // cuts * EX_DEV * width, bytes_accessed=2 * feats * width // cuts, transcendentals=0),
+            name="curve",
+        )(grads, inverse_curvature)
+        for cut in range(1, cuts)
+    ]
 
 
 def place_of(offset, places, planes):
@@ -254,6 +273,7 @@
 
 def body(activations, out_grads, example_of, proj_in, proj_out, inverse_curvature, stored):
     planes, stores = lax.axis_size("width"), lax.axis_size("store")
+    ids = example_of.reshape(-1, LANES)
     if planes * stores > 32 or stores % 2:
         partial_value = jnp.concatenate(
             [
@@ -263,26 +283,30 @@
             axis=1,
         )
         factors = lax.psum(partial_value, "width").astype(BF16)
-        (query,) = query_transposed([factors], example_of, inverse_curvature, 1)
+        curvature, start = load(ids, inverse_curvature)
+        (query,) = query_transposed([factors], ids, start, curvature, 1)
         gathered = lax.all_gather(query, ("width", "store"), axis=0)
         blocks = gathered.reshape(planes, stores, query.shape[0], EX_DEV)
         stored_blocks = stored.reshape(stored.shape[0], planes, query.shape[0])
         scores = jnp.einsum("wsfe,rwf->ser", blocks, stored_blocks, preferred_element_type=F32)
         return scores.reshape(stores * EX_DEV, stored.shape[0])
 
-    parts = project(activations, out_grads, proj_in, proj_out, planes)
-    own = parts[0]
-    for d in range(1, planes):
-        own = own + turn(parts[d], d, planes).astype(F32)
+    away = [*range(1, planes)]
+    operands = (activations, out_grads, proj_in, proj_out)
+    parts = project(*operands, planes, away)
+    sent = [turn(part, d, planes) for d, part in zip(away, parts)]
+    (own,) = project(*operands, planes, [0])
+    for part in sent:
+        own = own + part.astype(F32)
     own = own.astype(BF16)
     factors = [own] + [turn(own, d, planes) for d in range(1, planes)]
     _, inverse_curvature, stored = lax.optimization_barrier((own, inverse_curvature, stored))
-    inverse_curvature = load(inverse_curvature)
+    curvature, start = load(ids, inverse_curvature)
     swap = [(i, i ^ 1) for i in range(stores)]
     others = lax.ppermute(stored, "store", swap)
 
     streams = 2
-    query = query_transposed(factors, example_of, inverse_curvature, streams)
+    query = query_transposed(factors, ids, start, curvature, streams)
 
     places = planes * stores // 2
     on = lambda x: lax.ppermute(x, ("width", "store"), ring_pairs(planes, stores, 1))

time: 57.3 us -> 55 us (0.960)
  waiting for transfers between devices: 14.9 us -> 10.1 us
  Pallas kernels: 16.5 us -> 17.9 us
  starting transfers between devices: 25.3 us -> 26.5 us
    ppermute x7, starting transfers between devices: 4.06 us -> 9.35 us  [body(): lax.ppermute(x, ('width', 'store'), ring_pairs(planes, stores, -1))]
    ppermute x7, waiting for transfers between devices: 6.47 us -> 1.57 us  [body(): lax.ppermute(x, ('width', 'store'), ring_pairs(planes, stores, -1))]
    ppermute x7, starting transfers between devices: 9.83 us -> 5.78 us  [body(): lax.ppermute(x, ('width', 'store'), ring_pairs(planes, stores, 1))]
    ppermute x7, waiting for transfers between devices: 2.02 us -> 5.35 us  [body(): lax.ppermute(x, ('width', 'store'), ring_pairs(planes, stores, 1))]
    ppermute x6, waiting for transfers between devices: 5.1 us -> 1.88 us  [turn(): lax.ppermute(x, 'width', [(i, (i + d) % planes) for i in range(planes)])]
    pallas_call x2 -> x4, Pallas kernels: 8.16 us -> 11.2 us  [the longest x2 6.32 us: project(): pl.pallas_call(functools.partial(project_kernel, planes, turns), in_specs...]
    pallas_call x1, Pallas kernels: 4.51 us -> 2.89 us  [query_transposed(): pl.pallas_call(functools.partial(query_kernel, len(factors)), in_specs=[p...]
  transfers between devices with their start and end apart: 24 -> 24, of which waited for: 12 -> 12; matrix products, arithmetic and copies ran while one was open for 0% -> 0% of each run, Pallas kernels for 18% -> 23%
where the time goes in v4:
time: 55 us; the launch traced here: 54.8 us
  starting transfers between devices  26.5 us (48%)
  Pallas kernels  17.9 us (33%)
  waiting for transfers between devices  10.1 us (18%)
    ppermute x6, starting transfers between devices, turn(): lax.ppermute(x, 'width', [(i, (i + d) % planes) for i in range(planes)])  11.1 us
    ppermute x7, starting transfers between devices, body(): lax.ppermute(x, ('width', 'store'), ring_pairs(planes, stores, -1))  9.35 us
    pallas_call x2, Pallas kernels, project(): pl.pallas_call(functools.partial(project_kernel, planes, turns), in_specs...  6.32 us
    ppermute x7, starting transfers between devices, body(): lax.ppermute(x, ('width', 'store'), ring_pairs(planes, stores, 1))  5.78 us
    ppermute x7, waiting for transfers between devices, body(): lax.ppermute(x, ('width', 'store'), ring_pairs(planes, stores, 1))  5.35 us
    pallas_call x1, Pallas kernels, load(): pl.pallas_call(load_kernel, in_specs=[vmem, pl.BlockSpec(memory_space=plt...  3.61 us
    pallas_call x1, Pallas kernels, query_transposed(): pl.pallas_call(functools.partial(query_kernel, len(factors)), in_specs=[p...  2.89 us
    pallas_call x2, Pallas kernels, early_scores(): pl.pallas_call(functools.partial(early_kernel, places, planes, spots, boo...  2.57 us
  transfers between devices with their start and end apart: 24, of which 12 were waited for; matrix products, arithmetic and copies ran while one was open for 0% of the time, Pallas kernels for 23%

profile of v4, /device:TPU:0, one launch (start us, length us, event | category | flops | bytes accessed | tf_op | source)
XLA Modules:
  0.0 54.8 jit_solution(6619917259365092632)
XLA Ops:
  0.0 3.9 %project.3 = (bf16[256,128]{1,0:T(8,128)(2,1)S(1)}, bf16[256,128]{1,0:T(8,128)(2,1)S(1)}, bf16[256,128]{1,0:T(8,128)(2,1)S(1)}) custom-call(bf16[1024,2048]{1,0:T(8,128)(2,1)} %act_hbm.3, bf16[1024,2048]{1,0:T(8,128)(2,1)} %grad_hbm.3, bf16[64,2048]{1,0:T(8,128)(2,1)} %bitcast.5, bf16[64,2048]{1,0:T(8,128)(2,1)} %bitcast.7), custom_call_target="tpu_custom_call" | custom-call | flops 402653184 | bytes 12582912 | tf_op jit(solution)/shard_map/project/pallas_call | solution.py:59
  3.9 3.1 %collective-permute-start = (bf16[256,128]{1,0:T(8,128)(2,1)S(1)}, bf16[256,128]{1,0:T(8,128)(2,1)S(1)}, u32[]{:S(2)}, u32[]{:S(2)}) collective-permute-start(bf16[256,128]{1,0:T(8,128)(2,1)S(1)} %get-tuple-element.16), channel_id=1, source_target_pairs={{0,4},{4,8},{8,12},{12,0},{1,5},{5,9},{9,13},{13,1},{2,6},{6,10},{... | collective-permute-start | bytes 196616 | tf_op jit(solution)/shard_map/ppermute | solution.py:271
  7.0 2.6 %collective-permute-start.1 = (bf16[256,128]{1,0:T(8,128)(2,1)S(1)}, bf16[256,128]{1,0:T(8,128)(2,1)S(1)}, u32[]{:S(2)}, u32[]{:S(2)}) collective-permute-start(bf16[256,128]{1,0:T(8,128)(2,1)S(1)} %get-tuple-element.17), channel_id=1, source_target_pairs={{0,8},{4,12},{8,0},{12,4},{1,9},{5,13},{9,1},{13,5},{2,10},{6,14},... | collective-permute-start | bytes 196616 | tf_op jit(solution)/shard_map/ppermute | solution.py:271
  9.6 1.3 %collective-permute-start.2 = (bf16[256,128]{1,0:T(8,128)(2,1)S(1)}, bf16[256,128]{1,0:T(8,128)(2,1)S(1)}, u32[]{:S(2)}, u32[]{:S(2)}) collective-permute-start(bf16[256,128]{1,0:T(8,128)(2,1)S(1)} %get-tuple-element.18), channel_id=1, source_target_pairs={{0,12},{4,0},{8,4},{12,8},{1,13},{5,1},{9,5},{13,9},{2,14},{6,2},{... | collective-permute-start | bytes 196616 | tf_op jit(solution)/shard_map/ppermute | solution.py:271
  10.9 2.4 %project.2 = f32[256,128]{1,0:T(8,128)S(1)} custom-call(bf16[1024,2048]{1,0:T(8,128)(2,1)} %act_hbm.3, bf16[1024,2048]{1,0:T(8,128)(2,1)} %grad_hbm.3, bf16[64,2048]{1,0:T(8,128)(2,1)} %bitcast.6, bf16[64,2048]{1,0:T(8,128)(2,1)} %bitcast.8), custom_call_target="tpu_custom_call" | custom-call | flops 134217728 | bytes 4194304 | tf_op jit(solution)/shard_map/project/pallas_call | solution.py:59
  13.4 0.7 %collective-permute-done.1 = bf16[256,128]{1,0:T(8,128)(2,1)S(1)} collective-permute-done((bf16[256,128]{1,0:T(8,128)(2,1)S(1)}, bf16[256,128]{1,0:T(8,128)(2,1)S(1)}, u32[]{:S(2)}, u32[]{:S(2)}) %collective-permute-start.1) | collective-permute-done | bytes 65568 | tf_op jit(solution)/shard_map/ppermute | solution.py:271
  14.0 0.2 collective-permute-done.2
  14.3 1.6 %collective-permute-start.4 = (bf16[256,128]{1,0:T(8,128)(2,1)S(1)}, bf16[256,128]{1,0:T(8,128)(2,1)S(1)}, u32[]{:S(2)}, u32[]{:S(2)}) collective-permute-start(bf16[256,128]{1,0:T(8,128)(2,1)S(1)} %add_convert_fusion.rest_0_), channel_id=1, source_target_pairs={{0,4},{4,8},{8,12},{12,0},{1,5},{5,9},{9,13},{13,1},{2,6},{6,10},{... | collective-permute-start | bytes 196616 | tf_op jit(solution)/shard_map/ppermute | solution.py:271
  16.0 2.0 %collective-permute-start.5 = (bf16[256,128]{1,0:T(8,128)(2,1)S(1)}, bf16[256,128]{1,0:T(8,128)(2,1)S(1)}, u32[]{:S(2)}, u32[]{:S(2)}) collective-permute-start(bf16[256,128]{1,0:T(8,128)(2,1)S(1)} %add_convert_fusion.rest_0_), channel_id=1, source_target_pairs={{0,8},{4,12},{8,0},{12,4},{1,9},{5,13},{9,1},{13,5},{2,10},{6,14},... | collective-permute-start | bytes 196616 | tf_op jit(solution)/shard_map/ppermute | solution.py:271
  18.0 0.4 collective-permute-start.6
  18.4 3.6 %load.1 = (bf16[1024,4096]{1,0:T(8,128)(2,1)S(1)}, s32[16]{0:T(128)S(4)}) custom-call(s32[8,128]{1,0:T(8,128)S(1)} %bitcast.3, bf16[1024,4096]{1,0:T(8,128)(2,1)} %hbm_ref), custom_call_target="tpu_custom_call" | custom-call | bytes 33554432 | tf_op jit(solution)/shard_map/load/pallas_call | solution.py:94
  22.0 0.0 collective-permute-done.4.rest_1_
  22.0 0.6 %collective-permute-done.5.rest_2_ = bf16[256,128]{1,0:T(8,128)(2,1)S(1)} collective-permute-done((bf16[256,128]{1,0:T(8,128)(2,1)S(1)}, bf16[256,128]{1,0:T(8,128)(2,1)S(1)}, u32[]{:S(2)}, u32[]{:S(2)}) %collective-permute-start.5) | collective-permute-done | bytes 65568 | tf_op jit(solution)/shard_map/ppermute | solution.py:271
  22.6 0.4 collective-permute-done.6.rest_3_
  23.0 2.9 %query.1 = (bf16[512,128]{1,0:T(8,128)(2,1)S(1)}, bf16[128,4096]{1,0:T(8,128)(2,1)S(1)}) custom-call(s32[16]{0:T(128)S(4)} %get-tuple-element.21.start_ref, s32[8,128]{1,0:T(8,128)S(1)} %bitcast.4, bf16[256,128]{1,0:T(8,128)(2,1)S(1)} %add_convert_fusion.rest_0_, bf16[256,128]{1,0:T(8,128)(2,1)S(1)} %collective-permute-done.4.rest_1_, ...), custom_call_target="tpu_custom_call" | custom-call | tf_op jit(solution)/shard_map/query/pallas_call | solution.py:161
  25.9 1.2 %curve.1.rest_1_ = bf16[512,128]{1,0:T(8,128)(2,1)S(1)} custom-call(bf16[128,4096]{1,0:T(8,128)(2,1)S(1)} %get-tuple-element.24.pe_ref, bf16[1024,4096]{1,0:T(8,128)(2,1)S(1)} %get-tuple-element.22.rest_4_.ic_ref), custom_call_target="tpu_custom_call" | custom-call | flops 26843545600 | bytes 4194304 | tf_op jit(solution)/shard_map/curve/pallas_call | solution.py:175
  27.1 1.4 %collective-permute-start.16 = (bf16[512,128]{1,0:T(8,128)(2,1)S(1)}, bf16[512,128]{1,0:T(8,128)(2,1)S(1)}, u32[]{:S(2)}, u32[]{:S(2)}) collective-permute-start(bf16[512,128]{1,0:T(8,128)(2,1)S(1)} %curve.1.rest_1_), channel_id=1, source_target_pairs={{0,2},{1,3},{4,0},{5,1},{8,4},{9,5},{12,8},{13,9},{14,12},{15,13},... | collective-permute-start | bytes 393224 | tf_op jit(solution)/shard_map/ppermute | solution.py:313
  28.5 0.7 %collective-permute-start.7 = (bf16[512,128]{1,0:T(8,128)(2,1)S(1)}, bf16[512,128]{1,0:T(8,128)(2,1)S(1)}, u32[]{:S(2)}, u32[]{:S(2)}) collective-permute-start(bf16[512,128]{1,0:T(8,128)(2,1)S(1)} %get-tuple-element.23.rest_0_), channel_id=1, source_target_pairs={{0,4},{1,5},{4,8},{5,9},{8,12},{9,13},{12,14},{13,15},{14,10},{15,... | collective-permute-start | bytes 393224 | tf_op jit(solution)/shard_map/ppermute | solution.py:312
  29.2 1.5 %collective-permute-start.13 = (bf16[512,128]{1,0:T(8,128)(2,1)S(1)}, bf16[512,128]{1,0:T(8,128)(2,1)S(1)}, u32[]{:S(2)}, u32[]{:S(2)}) collective-permute-start(bf16[512,128]{1,0:T(8,128)(2,1)S(1)} %curve.1.rest_1_), channel_id=1, source_target_pairs={{0,4},{1,5},{4,8},{5,9},{8,12},{9,13},{12,14},{13,15},{14,10},{15,... | collective-permute-start | bytes 393224 | tf_op jit(solution)/shard_map/ppermute | solution.py:312
  30.7 0.5 collective-permute-start.10
  31.2 1.1 %collective-permute-done.16.rest_5_ = bf16[512,128]{1,0:T(8,128)(2,1)S(1)} collective-permute-done((bf16[512,128]{1,0:T(8,128)(2,1)S(1)}, bf16[512,128]{1,0:T(8,128)(2,1)S(1)}, u32[]{:S(2)}, u32[]{:S(2)}) %collective-permute-start.16) | collective-permute-done | bytes 131104 | tf_op jit(solution)/shard_map/ppermute | solution.py:313
  32.4 2.1 %collective-permute-start.17 = (bf16[512,128]{1,0:T(8,128)(2,1)S(1)}, bf16[512,128]{1,0:T(8,128)(2,1)S(1)}, u32[]{:S(2)}, u32[]{:S(2)}) collective-permute-start(bf16[512,128]{1,0:T(8,128)(2,1)S(1)} %collective-permute-done.16.rest_5_), channel_id=1, source_target_pairs={{0,2},{1,3},{4,0},{5,1},{8,4},{9,5},{12,8},{13,9},{14,12},{15,13},... | collective-permute-start | bytes 393224 | tf_op jit(solution)/shard_map/ppermute | solution.py:313
  34.5 0.3 collective-permute-done.7.rest_2_
  34.8 0.8 %collective-permute-start.8 = (bf16[512,128]{1,0:T(8,128)(2,1)S(1)}, bf16[512,128]{1,0:T(8,128)(2,1)S(1)}, u32[]{:S(2)}, u32[]{:S(2)}) collective-permute-start(bf16[512,128]{1,0:T(8,128)(2,1)S(1)} %collective-permute-done.7.rest_2_), channel_id=1, source_target_pairs={{0,4},{1,5},{4,8},{5,9},{8,12},{9,13},{12,14},{13,15},{14,10},{15,... | collective-permute-start | bytes 393224 | tf_op jit(solution)/shard_map/ppermute | solution.py:312
  35.6 1.7 %collective-permute-done.13.rest_4_ = bf16[512,128]{1,0:T(8,128)(2,1)S(1)} collective-permute-done((bf16[512,128]{1,0:T(8,128)(2,1)S(1)}, bf16[512,128]{1,0:T(8,128)(2,1)S(1)}, u32[]{:S(2)}, u32[]{:S(2)}) %collective-permute-start.13) | collective-permute-done | bytes 131104 | tf_op jit(solution)/shard_map/ppermute | solution.py:312
  37.3 0.8 %collective-permute-start.14 = (bf16[512,128]{1,0:T(8,128)(2,1)S(1)}, bf16[512,128]{1,0:T(8,128)(2,1)S(1)}, u32[]{:S(2)}, u32[]{:S(2)}) collective-permute-start(bf16[512,128]{1,0:T(8,128)(2,1)S(1)} %collective-permute-done.13.rest_4_), channel_id=1, source_target_pairs={{0,4},{1,5},{4,8},{5,9},{8,12},{9,13},{12,14},{13,15},{14,10},{15,... | collective-permute-start | bytes 393224 | tf_op jit(solution)/shard_map/ppermute | solution.py:312
  38.0 0.0 collective-permute-done.10.rest_3_
  38.0 1.2 %collective-permute-start.11 = (bf16[512,128]{1,0:T(8,128)(2,1)S(1)}, bf16[512,128]{1,0:T(8,128)(2,1)S(1)}, u32[]{:S(2)}, u32[]{:S(2)}) collective-permute-start(bf16[512,128]{1,0:T(8,128)(2,1)S(1)} %collective-permute-done.10.rest_3_), channel_id=1, source_target_pairs={{0,2},{1,3},{4,0},{5,1},{8,4},{9,5},{12,8},{13,9},{14,12},{15,13},... | collective-permute-start | bytes 393224 | tf_op jit(solution)/shard_map/ppermute | solution.py:313
  39.3 0.0 collective-permute-done.17.rest_9_
  39.3 1.5 %collective-permute-start.18 = (bf16[512,128]{1,0:T(8,128)(2,1)S(1)}, bf16[512,128]{1,0:T(8,128)(2,1)S(1)}, u32[]{:S(2)}, u32[]{:S(2)}) collective-permute-start(bf16[512,128]{1,0:T(8,128)(2,1)S(1)} %collective-permute-done.17.rest_9_), channel_id=1, source_target_pairs={{0,2},{1,3},{4,0},{5,1},{8,4},{9,5},{12,8},{13,9},{14,12},{15,13},... | collective-permute-start | bytes 393224 | tf_op jit(solution)/shard_map/ppermute | solution.py:313
  40.8 0.0 collective-permute-done.8.rest_6_
  40.8 0.6 %collective-permute-start.9 = (bf16[512,128]{1,0:T(8,128)(2,1)S(1)}, bf16[512,128]{1,0:T(8,128)(2,1)S(1)}, u32[]{:S(2)}, u32[]{:S(2)}) collective-permute-start(bf16[512,128]{1,0:T(8,128)(2,1)S(1)} %collective-permute-done.8.rest_6_), channel_id=1, source_target_pairs={{0,4},{1,5},{4,8},{5,9},{8,12},{9,13},{12,14},{13,15},{14,10},{15,... | collective-permute-start | bytes 393224 | tf_op jit(solution)/shard_map/ppermute | solution.py:312
  41.3 2.2 %collective-permute-done.14.rest_8_ = bf16[512,128]{1,0:T(8,128)(2,1)S(1)} collective-permute-done((bf16[512,128]{1,0:T(8,128)(2,1)S(1)}, bf16[512,128]{1,0:T(8,128)(2,1)S(1)}, u32[]{:S(2)}, u32[]{:S(2)}) %collective-permute-start.14) | collective-permute-done | bytes 131104 | tf_op jit(solution)/shard_map/ppermute | solution.py:312
  43.5 0.8 %collective-permute-start.15 = (bf16[512,128]{1,0:T(8,128)(2,1)S(1)}, bf16[512,128]{1,0:T(8,128)(2,1)S(1)}, u32[]{:S(2)}, u32[]{:S(2)}) collective-permute-start(bf16[512,128]{1,0:T(8,128)(2,1)S(1)} %collective-permute-done.14.rest_8_), channel_id=1, source_target_pairs={{0,4},{1,5},{4,8},{5,9},{8,12},{9,13},{12,14},{13,15},{14,10},{15,... | collective-permute-start | bytes 393224 | tf_op jit(solution)/shard_map/ppermute | solution.py:312
  44.3 1.2 %collective-permute-start.12 = (bf16[512,128]{1,0:T(8,128)(2,1)S(1)}, bf16[512,128]{1,0:T(8,128)(2,1)S(1)}, u32[]{:S(2)}, u32[]{:S(2)}) collective-permute-start(bf16[512,128]{1,0:T(8,128)(2,1)S(1)} %collective-permute-done.11.rest_7_), channel_id=1, source_target_pairs={{0,2},{1,3},{4,0},{5,1},{8,4},{9,5},{12,8},{13,9},{14,12},{15,13},... | collective-permute-start | bytes 393224 | tf_op jit(solution)/shard_map/ppermute | solution.py:313
  45.6 0.1 collective-permute-done.18.rest_3_
  45.7 1.4 %collective-permute-start.21 = (bf16[512,128]{1,0:T(8,128)(2,1)S(1)}, bf16[512,128]{1,0:T(8,128)(2,1)S(1)}, u32[]{:S(2)}, u32[]{:S(2)}) collective-permute-start(bf16[512,128]{1,0:T(8,128)(2,1)S(1)} %collective-permute-done.18.rest_3_), channel_id=1, source_target_pairs={{0,2},{1,3},{4,0},{5,1},{8,4},{9,5},{12,8},{13,9},{14,12},{15,13},... | collective-permute-start | bytes 393224 | tf_op jit(solution)/shard_map/ppermute | solution.py:313
  47.1 0.0 collective-permute-done.9.rest_0_
  47.1 0.6 %collective-permute-start.20 = (bf16[512,128]{1,0:T(8,128)(2,1)S(1)}, bf16[512,128]{1,0:T(8,128)(2,1)S(1)}, u32[]{:S(2)}, u32[]{:S(2)}) collective-permute-start(bf16[512,128]{1,0:T(8,128)(2,1)S(1)} %collective-permute-done.9.rest_0_), channel_id=1, source_target_pairs={{0,4},{1,5},{4,8},{5,9},{8,12},{9,13},{12,14},{13,15},{14,10},{15,... | collective-permute-start | bytes 393224 | tf_op jit(solution)/shard_map/ppermute | solution.py:312
  47.7 1.6 %early_scores.2.rest_4_ = f32[2,2,256,128]{3,2,1,0:T(8,128)S(1)} custom-call(bf16[256,4096]{1,0:T(8,128)(2,1)S(1)} %copy-done, bf16[256,4096]{1,0:T(8,128)(2,1)S(1)} %collective-permute-done.3.other_ref, bf16[512,128]{1,0:T(8,128)(2,1)S(1)} %get-tuple-element.23.rest_0_, bf16[512,128]{1,0:T(8,128)(2,1)S(1)} %curve.1.rest_1_, ...), custom_call_target="tpu_custom_call" | custom-call | tf_op jit(solution)/shard_map/early_scores/pallas_call | solution.py:219
  49.4 1.0 %early_scores.3 = (f32[256,256]{1,0:T(8,128)S(1)}, f32[256,256]{1,0:T(8,128)S(1)}) custom-call(bf16[256,4096]{1,0:T(8,128)(2,1)S(1)} %copy-done, bf16[256,4096]{1,0:T(8,128)(2,1)S(1)} %collective-permute-done.3.other_ref, bf16[512,128]{1,0:T(8,128)(2,1)S(1)} %collective-permute-done.9.rest_0_, bf16[512,128]{1,0:T(8,128)(2,1)S(1)} %collective-permute-done.12.rest_1_, ...), custom_call_target="tpu_custom_call" | custom-call | tf_op jit(solution)/shard_map/early_scores/pallas_call | solution.py:219
  50.3 0.1 collective-permute-start.19
  50.4 0.3 collective-permute-done.21.rest_1_
  50.7 0.2 collective-permute-start.23
  50.9 1.2 %collective-permute-done.20.rest_0_ = bf16[512,128]{1,0:T(8,128)(2,1)S(1)} collective-permute-done((bf16[512,128]{1,0:T(8,128)(2,1)S(1)}, bf16[512,128]{1,0:T(8,128)(2,1)S(1)}, u32[]{:S(2)}, u32[]{:S(2)}) %collective-permute-start.20) | collective-permute-done | bytes 131104 | tf_op jit(solution)/shard_map/ppermute | solution.py:312
  52.1 0.0 collective-permute-done.23.rest_3_
  52.1 1.3 %collective-permute-done.22.rest_2_ = bf16[512,128]{1,0:T(8,128)(2,1)S(1)} collective-permute-done((bf16[512,128]{1,0:T(8,128)(2,1)S(1)}, bf16[512,128]{1,0:T(8,128)(2,1)S(1)}, u32[]{:S(2)}, u32[]{:S(2)}) %collective-permute-start.22) | collective-permute-done | bytes 131104 | tf_op jit(solution)/shard_map/ppermute | solution.py:330
  53.5 1.3 %final_scores.1 = f32[512,256]{1,0:T(8,128)} custom-call(bf16[256,4096]{1,0:T(8,128)(2,1)S(1)} %copy-done, f32[256,256]{1,0:T(8,128)S(1)} %get-tuple-element.25.keep_ref, f32[256,256]{1,0:T(8,128)S(1)} %collective-permute-done.19.got_ref, bf16[512,128]{1,0:T(8,128)(2,1)S(1)} %collective-permute-done.20.rest_0_, ...), custom_call_target="tpu_custom_call" | custom-call | tf_op jit(solution)/shard_map/final_scores/pallas_call | solution.py:251
  (13 shorter events, 0.1 us)
Async XLA Ops:
  3.9 9.5 %collective-permute-start = (bf16[256,128]{1,0:T(8,128)(2,1)S(1)}, bf16[256,128]{1,0:T(8,128)(2,1)S(1)}, u32[]{:S(2)}, u32[]{:S(2)}) collective-permute-start(bf16[256,128]{1,0:T(8,128)(2,1)S(1)} %get-tuple-element.16), channel_id=1, source_target_pairs={{0,4},{4,8},{8,12},{12,0},{1,5},{5,9},{9,13},{13,1},{2,6},{6,10},{... | collective-permute-start | bytes 196616 | tf_op jit(solution)/shard_map/ppermute | solution.py:271
  7.0 7.1 %collective-permute-start.1 = (bf16[256,128]{1,0:T(8,128)(2,1)S(1)}, bf16[256,128]{1,0:T(8,128)(2,1)S(1)}, u32[]{:S(2)}, u32[]{:S(2)}) collective-permute-start(bf16[256,128]{1,0:T(8,128)(2,1)S(1)} %get-tuple-element.17), channel_id=1, source_target_pairs={{0,8},{4,12},{8,0},{12,4},{1,9},{5,13},{9,1},{13,5},{2,10},{6,14},... | collective-permute-start | bytes 196616 | tf_op jit(solution)/shard_map/ppermute | solution.py:271
  9.6 8.8 %copy-start = (bf16[256,4096]{1,0:T(8,128)(2,1)S(1)}, bf16[256,4096]{1,0:T(8,128)(2,1)}, u32[]{:S(2)}) copy-start(bf16[256,4096]{1,0:T(8,128)(2,1)} %stored_ref) | copy-start | bytes 6291460
  9.6 8.8 %copy-start.1 = (s32[1,1024]{1,0:T(1,128)S(1)}, s32[1,1024]{1,0:T(1,128)}, u32[]{:S(2)}) copy-start(s32[1,1024]{1,0:T(1,128)} %param.9) | copy-start | bytes 12292
  9.6 4.7 %collective-permute-start.2 = (bf16[256,128]{1,0:T(8,128)(2,1)S(1)}, bf16[256,128]{1,0:T(8,128)(2,1)S(1)}, u32[]{:S(2)}, u32[]{:S(2)}) collective-permute-start(bf16[256,128]{1,0:T(8,128)(2,1)S(1)} %get-tuple-element.18), channel_id=1, source_target_pairs={{0,12},{4,0},{8,4},{12,8},{1,13},{5,1},{9,5},{13,9},{2,14},{6,2},{... | collective-permute-start | bytes 196616 | tf_op jit(solution)/shard_map/ppermute | solution.py:271
  14.3 7.7 %collective-permute-start.4 = (bf16[256,128]{1,0:T(8,128)(2,1)S(1)}, bf16[256,128]{1,0:T(8,128)(2,1)S(1)}, u32[]{:S(2)}, u32[]{:S(2)}) collective-permute-start(bf16[256,128]{1,0:T(8,128)(2,1)S(1)} %add_convert_fusion.rest_0_), channel_id=1, source_target_pairs={{0,4},{4,8},{8,12},{12,0},{1,5},{5,9},{9,13},{13,1},{2,6},{6,10},{... | collective-permute-start | bytes 196616 | tf_op jit(solution)/shard_map/ppermute | solution.py:271
  16.0 6.7 %collective-permute-start.5 = (bf16[256,128]{1,0:T(8,128)(2,1)S(1)}, bf16[256,128]{1,0:T(8,128)(2,1)S(1)}, u32[]{:S(2)}, u32[]{:S(2)}) collective-permute-start(bf16[256,128]{1,0:T(8,128)(2,1)S(1)} %add_convert_fusion.rest_0_), channel_id=1, source_target_pairs={{0,8},{4,12},{8,0},{12,4},{1,9},{5,13},{9,1},{13,5},{2,10},{6,14},... | collective-permute-start | bytes 196616 | tf_op jit(solution)/shard_map/ppermute | solution.py:271
  18.0 5.0 %collective-permute-start.6 = (bf16[256,128]{1,0:T(8,128)(2,1)S(1)}, bf16[256,128]{1,0:T(8,128)(2,1)S(1)}, u32[]{:S(2)}, u32[]{:S(2)}) collective-permute-start(bf16[256,128]{1,0:T(8,128)(2,1)S(1)} %add_convert_fusion.rest_0_), channel_id=1, source_target_pairs={{0,12},{4,0},{8,4},{12,8},{1,13},{5,1},{9,5},{13,9},{2,14},{6,2},{... | collective-permute-start | bytes 196616 | tf_op jit(solution)/shard_map/ppermute | solution.py:271
  18.4 29.3 %collective-permute-start.3 = (bf16[256,4096]{1,0:T(8,128)(2,1)S(1)}, bf16[256,4096]{1,0:T(8,128)(2,1)S(1)}, u32[]{:S(2)}, u32[]{:S(2)}) collective-permute-start(bf16[256,4096]{1,0:T(8,128)(2,1)S(1)} %copy-done), channel_id=1, source_target_pairs={{0,1},{1,0},{2,3},{3,2},{4,5},{5,4},{6,7},{7,6},{8,9},{9,8},{10,11... | collective-permute-start | bytes 6291464 | tf_op jit(solution)/shard_map/ppermute | solution.py:306
  27.1 5.2 %collective-permute-start.16 = (bf16[512,128]{1,0:T(8,128)(2,1)S(1)}, bf16[512,128]{1,0:T(8,128)(2,1)S(1)}, u32[]{:S(2)}, u32[]{:S(2)}) collective-permute-start(bf16[512,128]{1,0:T(8,128)(2,1)S(1)} %curve.1.rest_1_), channel_id=1, source_target_pairs={{0,2},{1,3},{4,0},{5,1},{8,4},{9,5},{12,8},{13,9},{14,12},{15,13},... | collective-permute-start | bytes 393224 | tf_op jit(solution)/shard_map/ppermute | solution.py:313
  28.5 6.3 %collective-permute-start.7 = (bf16[512,128]{1,0:T(8,128)(2,1)S(1)}, bf16[512,128]{1,0:T(8,128)(2,1)S(1)}, u32[]{:S(2)}, u32[]{:S(2)}) collective-permute-start(bf16[512,128]{1,0:T(8,128)(2,1)S(1)} %get-tuple-element.23.rest_0_), channel_id=1, source_target_pairs={{0,4},{1,5},{4,8},{5,9},{8,12},{9,13},{12,14},{13,15},{14,10},{15,... | collective-permute-start | bytes 393224 | tf_op jit(solution)/shard_map/ppermute | solution.py:312
  29.2 8.0 %collective-permute-start.13 = (bf16[512,128]{1,0:T(8,128)(2,1)S(1)}, bf16[512,128]{1,0:T(8,128)(2,1)S(1)}, u32[]{:S(2)}, u32[]{:S(2)}) collective-permute-start(bf16[512,128]{1,0:T(8,128)(2,1)S(1)} %curve.1.rest_1_), channel_id=1, source_target_pairs={{0,4},{1,5},{4,8},{5,9},{8,12},{9,13},{12,14},{13,15},{14,10},{15,... | collective-permute-start | bytes 393224 | tf_op jit(solution)/shard_map/ppermute | solution.py:312
  30.7 7.3 %collective-permute-start.10 = (bf16[512,128]{1,0:T(8,128)(2,1)S(1)}, bf16[512,128]{1,0:T(8,128)(2,1)S(1)}, u32[]{:S(2)}, u32[]{:S(2)}) collective-permute-start(bf16[512,128]{1,0:T(8,128)(2,1)S(1)} %get-tuple-element.23.rest_0_), channel_id=1, source_target_pairs={{0,2},{1,3},{4,0},{5,1},{8,4},{9,5},{12,8},{13,9},{14,12},{15,13},... | collective-permute-start | bytes 393224 | tf_op jit(solution)/shard_map/ppermute | solution.py:313
  32.4 6.9 %collective-permute-start.17 = (bf16[512,128]{1,0:T(8,128)(2,1)S(1)}, bf16[512,128]{1,0:T(8,128)(2,1)S(1)}, u32[]{:S(2)}, u32[]{:S(2)}) collective-permute-start(bf16[512,128]{1,0:T(8,128)(2,1)S(1)} %collective-permute-done.16.rest_5_), channel_id=1, source_target_pairs={{0,2},{1,3},{4,0},{5,1},{8,4},{9,5},{12,8},{13,9},{14,12},{15,13},... | collective-permute-start | bytes 393224 | tf_op jit(solution)/shard_map/ppermute | solution.py:313
  34.8 6.0 %collective-permute-start.8 = (bf16[512,128]{1,0:T(8,128)(2,1)S(1)}, bf16[512,128]{1,0:T(8,128)(2,1)S(1)}, u32[]{:S(2)}, u32[]{:S(2)}) collective-permute-start(bf16[512,128]{1,0:T(8,128)(2,1)S(1)} %collective-permute-done.7.rest_2_), channel_id=1, source_target_pairs={{0,4},{1,5},{4,8},{5,9},{8,12},{9,13},{12,14},{13,15},{14,10},{15,... | collective-permute-start | bytes 393224 | tf_op jit(solution)/shard_map/ppermute | solution.py:312
  37.3 6.3 %collective-permute-start.14 = (bf16[512,128]{1,0:T(8,128)(2,1)S(1)}, bf16[512,128]{1,0:T(8,128)(2,1)S(1)}, u32[]{:S(2)}, u32[]{:S(2)}) collective-permute-start(bf16[512,128]{1,0:T(8,128)(2,1)S(1)} %collective-permute-done.13.rest_4_), channel_id=1, source_target_pairs={{0,4},{1,5},{4,8},{5,9},{8,12},{9,13},{12,14},{13,15},{14,10},{15,... | collective-permute-start | bytes 393224 | tf_op jit(solution)/shard_map/ppermute | solution.py:312
  38.0 6.3 %collective-permute-start.11 = (bf16[512,128]{1,0:T(8,128)(2,1)S(1)}, bf16[512,128]{1,0:T(8,128)(2,1)S(1)}, u32[]{:S(2)}, u32[]{:S(2)}) collective-permute-start(bf16[512,128]{1,0:T(8,128)(2,1)S(1)} %collective-permute-done.10.rest_3_), channel_id=1, source_target_pairs={{0,2},{1,3},{4,0},{5,1},{8,4},{9,5},{12,8},{13,9},{14,12},{15,13},... | collective-permute-start | bytes 393224 | tf_op jit(solution)/shard_map/ppermute | solution.py:313
  39.3 6.4 %collective-permute-start.18 = (bf16[512,128]{1,0:T(8,128)(2,1)S(1)}, bf16[512,128]{1,0:T(8,128)(2,1)S(1)}, u32[]{:S(2)}, u32[]{:S(2)}) collective-permute-start(bf16[512,128]{1,0:T(8,128)(2,1)S(1)} %collective-permute-done.17.rest_9_), channel_id=1, source_target_pairs={{0,2},{1,3},{4,0},{5,1},{8,4},{9,5},{12,8},{13,9},{14,12},{15,13},... | collective-permute-start | bytes 393224 | tf_op jit(solution)/shard_map/ppermute | solution.py:313
  40.8 6.4 %collective-permute-start.9 = (bf16[512,128]{1,0:T(8,128)(2,1)S(1)}, bf16[512,128]{1,0:T(8,128)(2,1)S(1)}, u32[]{:S(2)}, u32[]{:S(2)}) collective-permute-start(bf16[512,128]{1,0:T(8,128)(2,1)S(1)} %collective-permute-done.8.rest_6_), channel_id=1, source_target_pairs={{0,4},{1,5},{4,8},{5,9},{8,12},{9,13},{12,14},{13,15},{14,10},{15,... | collective-permute-start | bytes 393224 | tf_op jit(solution)/shard_map/ppermute | solution.py:312
  43.5 5.8 %collective-permute-start.15 = (bf16[512,128]{1,0:T(8,128)(2,1)S(1)}, bf16[512,128]{1,0:T(8,128)(2,1)S(1)}, u32[]{:S(2)}, u32[]{:S(2)}) collective-permute-start(bf16[512,128]{1,0:T(8,128)(2,1)S(1)} %collective-permute-done.14.rest_8_), channel_id=1, source_target_pairs={{0,4},{1,5},{4,8},{5,9},{8,12},{9,13},{12,14},{13,15},{14,10},{15,... | collective-permute-start | bytes 393224 | tf_op jit(solution)/shard_map/ppermute | solution.py:312
  44.3 5.0 %collective-permute-start.12 = (bf16[512,128]{1,0:T(8,128)(2,1)S(1)}, bf16[512,128]{1,0:T(8,128)(2,1)S(1)}, u32[]{:S(2)}, u32[]{:S(2)}) collective-permute-start(bf16[512,128]{1,0:T(8,128)(2,1)S(1)} %collective-permute-done.11.rest_7_), channel_id=1, source_target_pairs={{0,2},{1,3},{4,0},{5,1},{8,4},{9,5},{12,8},{13,9},{14,12},{15,13},... | collective-permute-start | bytes 393224 | tf_op jit(solution)/shard_map/ppermute | solution.py:313
  45.7 5.0 %collective-permute-start.21 = (bf16[512,128]{1,0:T(8,128)(2,1)S(1)}, bf16[512,128]{1,0:T(8,128)(2,1)S(1)}, u32[]{:S(2)}, u32[]{:S(2)}) collective-permute-start(bf16[512,128]{1,0:T(8,128)(2,1)S(1)} %collective-permute-done.18.rest_3_), channel_id=1, source_target_pairs={{0,2},{1,3},{4,0},{5,1},{8,4},{9,5},{12,8},{13,9},{14,12},{15,13},... | collective-permute-start | bytes 393224 | tf_op jit(solution)/shard_map/ppermute | solution.py:313
  47.1 5.0 %collective-permute-start.20 = (bf16[512,128]{1,0:T(8,128)(2,1)S(1)}, bf16[512,128]{1,0:T(8,128)(2,1)S(1)}, u32[]{:S(2)}, u32[]{:S(2)}) collective-permute-start(bf16[512,128]{1,0:T(8,128)(2,1)S(1)} %collective-permute-done.9.rest_0_), channel_id=1, source_target_pairs={{0,4},{1,5},{4,8},{5,9},{8,12},{9,13},{12,14},{13,15},{14,10},{15,... | collective-permute-start | bytes 393224 | tf_op jit(solution)/shard_map/ppermute | solution.py:312
  50.3 3.1 %collective-permute-start.19 = (f32[256,256]{1,0:T(8,128)S(1)}, f32[256,256]{1,0:T(8,128)S(1)}, u32[]{:S(2)}, u32[]{:S(2)}) collective-permute-start(f32[256,256]{1,0:T(8,128)S(1)} %get-tuple-element.26), channel_id=1, source_target_pairs={{0,1},{1,0},{2,3},{3,2},{4,5},{5,4},{6,7},{7,6},{8,9},{9,8},{10,11... | collective-permute-start | bytes 786440 | tf_op jit(solution)/shard_map/ppermute | solution.py:329
  50.7 1.4 %collective-permute-start.23 = (bf16[512,128]{1,0:T(8,128)(2,1)S(1)}, bf16[512,128]{1,0:T(8,128)(2,1)S(1)}, u32[]{:S(2)}, u32[]{:S(2)}) collective-permute-start(bf16[512,128]{1,0:T(8,128)(2,1)S(1)} %collective-permute-done.21.rest_1_), channel_id=1, source_target_pairs={{0,1},{1,0},{2,3},{3,2},{4,5},{5,4},{6,7},{7,6},{8,9},{9,8},{10,11... | collective-permute-start | bytes 393224 | tf_op jit(solution)/shard_map/ppermute | solution.py:330
  52.1 1.3 %collective-permute-start.22 = (bf16[512,128]{1,0:T(8,128)(2,1)S(1)}, bf16[512,128]{1,0:T(8,128)(2,1)S(1)}, u32[]{:S(2)}, u32[]{:S(2)}) collective-permute-start(bf16[512,128]{1,0:T(8,128)(2,1)S(1)} %collective-permute-done.20.rest_0_), channel_id=1, source_target_pairs={{0,1},{1,0},{2,3},{3,2},{4,5},{5,4},{6,7},{7,6},{8,9},{9,8},{10,11... | collective-permute-start | bytes 393224 | tf_op jit(solution)/shard_map/ppermute | solution.py:330

commit v5 on v4

--- a/solution.py
+++ b/solution.py
@@ -185,10 +185,11 @@
     ]
 
 
-def place_of(offset, places, planes):
-    plane, chip = lax.axis_index("width"), lax.axis_index("store") // 2
+def block_at(step, places, planes):
+    plane, index = lax.axis_index("width"), lax.axis_index("store")
+    chip, core = index // 2, lax.rem(index, 2)
     here = chip * planes + jnp.where(chip % 2 == 0, plane, planes - 1 - plane)
-    there = lax.rem(here + offset + places, places)
+    there = lax.rem(here + (2 * core - 1) * step + places, places)
     that_chip, left = there // planes, lax.rem(there, planes)
     return that_chip, jnp.where(that_chip % 2 == 0, left, planes - 1 - left)
 
@@ -198,72 +199,78 @@
     if has_total:
         total_ref, *rest = rest
     *outs, acc = rest if last else [*rest, rest[0]]
+    core = lax.rem(lax.axis_index("store"), 2)
     depth = mine_ref.shape[1] // planes
     acc[...] = total_ref[...] if has_total else jnp.zeros_like(acc)
-    for block, (offset, first) in zip(blocks, spots):
-        chip, plane = place_of(offset, places, planes)
-        columns = pl.ds(pl.multiple_of(plane * depth + first, LANES), block.shape[0])
-        for n, ref in enumerate((mine_ref, other_ref)):
-            acc[chip, n] += jnp.dot(ref[:, columns], block[...], preferred_element_type=F32)
+    for block, (step, segments) in zip(blocks, spots):
+        chip, plane = block_at(step, places, planes)
+        for mate, first, row, size in segments:
+            columns = pl.ds(pl.multiple_of(plane * depth + first, LANES), size)
+            index = 2 * chip + (1 - core if mate else core)
+            for n, ref in enumerate((mine_ref, other_ref) if step else (mine_ref,)):
+                acc[index, n] += jnp.dot(ref[:, columns], block[pl.ds(row, size), :], preferred_element_type=F32)
     if last:
-        for chip in range(places // planes):
-            for n, out in enumerate(outs):
-                out[pl.ds(chip * EX_DEV, EX_DEV), :] = acc[chip, n].T
+        keep_ref, *sends = outs
+        for index in range(acc.shape[0]):
+            keep_ref[pl.ds(index * EX_DEV, EX_DEV), :] = acc[index, 0].T
+            at, row = divmod(index * EX_DEV, sends[0].shape[0])
+            sends[at][pl.ds(row, EX_DEV), :] = acc[index, 1].T
 
 
 def early_scores(stored, others, blocks, spots, total, last, places, planes):
-    rows, chips = stored.shape[0], places // planes
-    sums = (chips, 2, rows, EX_DEV)
+    rows, stores = stored.shape[0], 2 * places // planes
+    sums = (stores, 2, rows, EX_DEV)
     vmem = pl.BlockSpec(memory_space=pltpu.VMEM)
     totals = [] if total is None else [total]
     return pl.pallas_call(
         functools.partial(early_kernel, places, planes, spots, bool(totals), last),
         in_specs=[vmem] * (2 + len(blocks) + len(totals)),
-        out_specs=[vmem] * 2 if last else vmem,
-        out_shape=[jax.ShapeDtypeStruct((chips * EX_DEV, rows), F32)] * 2 if last else jax.ShapeDtypeStruct(sums, F32),
+        out_specs=[vmem] * 3 if last else vmem,
+        out_shape=[pltpu.VMEM((stores * EX_DEV // n, rows), F32) for n in (1, 2, 2)] if last else pltpu.VMEM(sums, F32),
         scratch_shapes=[pltpu.VMEM(sums, F32)] if last else [],
         compiler_params=pltpu.CompilerParams(vmem_limit_bytes=20 * MIB),
         name="early_scores",
     )(stored, others, *blocks, *totals)
 
 
-def final_kernel(places, planes, spots, stored_ref, keep_ref, got_ref, *rest):
+def final_kernel(places, planes, spots, stored_ref, keep_ref, got_ref, more_ref, *rest):
     blocks, out_ref = rest[:-1], rest[-1]
     core = lax.rem(lax.axis_index("store"), 2)
     depth = stored_ref.shape[1] // planes
-    for n, ref in enumerate((keep_ref, got_ref)):
-        which = core if n == 0 else 1 - core
-        for chip in range(places // planes):
-            at = pl.multiple_of((2 * chip + which) * EX_DEV, EX_DEV)
-            out_ref[pl.ds(at, EX_DEV), :] = ref[pl.ds(chip * EX_DEV, EX_DEV), :]
+    chip, plane = block_at(places // 2, places, planes)
+    half = got_ref.shape[0]
+    out_ref[pl.ds(0, half), :] = keep_ref[pl.ds(0, half), :] + got_ref[...]
+    out_ref[pl.ds(half, half), :] = keep_ref[pl.ds(half, half), :] + more_ref[...]
+    for mate in range(2):
         part = None
-        for block, (offset, first) in zip(blocks[n * len(spots) : (n + 1) * len(spots)], spots):
-            chip, plane = place_of(offset, places, planes)
-            columns = pl.ds(pl.multiple_of(plane * depth + first, LANES), block.shape[0])
-            more = jnp.dot(stored_ref[:, columns], block[...], preferred_element_type=F32)
-            part = more if part is None else part + more
-        at = pl.multiple_of((2 * chip + which) * EX_DEV, EX_DEV)
-        out_ref[pl.ds(at, EX_DEV), :] += part.T
+        for block, (m, first) in zip(blocks, spots):
+            if m == mate:
+                columns = pl.ds(pl.multiple_of(plane * depth + first, LANES), block.shape[0])
+                more = jnp.dot(stored_ref[:, columns], block[...], preferred_element_type=F32)
+                part = more if part is None else part + more
+        index = 2 * chip + (1 - core if mate else core)
+        out_ref[pl.ds(pl.multiple_of(index * EX_DEV, EX_DEV), EX_DEV), :] += part.T
 
 
 def final_scores(stored, keep, got, blocks, spots, places, planes):
     vmem = pl.BlockSpec(memory_space=pltpu.VMEM)
     return pl.pallas_call(
         functools.partial(final_kernel, places, planes, spots),
-        in_specs=[vmem] * (3 + len(blocks)),
+        in_specs=[vmem] * (4 + len(blocks)),
         out_specs=vmem,
-        out_shape=jax.ShapeDtypeStruct((2 * keep.shape[0], keep.shape[1]), F32),
+        out_shape=jax.ShapeDtypeStruct(keep.shape, F32),
         compiler_params=pltpu.CompilerParams(vmem_limit_bytes=20 * MIB),
         name="final_scores",
-    )(stored, keep, got, *blocks)
-
-
-def ring_pairs(planes, stores, step):
+    )(stored, keep, *got, *blocks)
+
+
+def ring_pairs(planes, stores):
     walk = [(x, z if x % 2 == 0 else planes - 1 - z) for x in range(stores // 2) for z in range(planes)]
     pairs = []
     for at, (x, z) in enumerate(walk):
-        to_x, to_z = walk[(at + step) % len(walk)]
-        pairs += [(z * stores + 2 * x + core, to_z * stores + 2 * to_x + core) for core in range(2)]
+        for core, step in enumerate((1, -1)):
+            to_x, to_z = walk[(at + step) % len(walk)]
+            pairs.append((z * stores + 2 * x + core, to_z * stores + 2 * to_x + core))
     return pairs
 
 
@@ -274,7 +281,8 @@
 def body(activations, out_grads, example_of, proj_in, proj_out, inverse_curvature, stored):
     planes, stores = lax.axis_size("width"), lax.axis_size("store")
     ids = example_of.reshape(-1, LANES)
-    if planes * stores > 32 or stores % 2:
+    places = planes * stores // 2
+    if planes * stores > 32 or stores % 2 or places % 2 or inverse_curvature.shape[0] % (2 * LANES):
         partial_value = jnp.concatenate(
             [
                 jnp.dot(activations, proj_in, preferred_element_type=F32),
@@ -305,30 +313,28 @@
     swap = [(i, i ^ 1) for i in range(stores)]
     others = lax.ppermute(stored, "store", swap)
 
-    streams = 2
-    query = query_transposed(factors, ids, start, curvature, streams)
-
-    places = planes * stores // 2
-    on = lambda x: lax.ppermute(x, ("width", "store"), ring_pairs(planes, stores, 1))
-    back = lambda x: lax.ppermute(x, ("width", "store"), ring_pairs(planes, stores, -1))
-    firsts = [j * query[0].shape[0] for j in range(streams)]
-    ahead, behind = list(query), list(query)
-    early, spots = list(query), [(0, first) for first in firsts]
+    query = query_transposed(factors, ids, start, curvature, 2)
+    on = lambda x: lax.ppermute(x, ("width", "store"), ring_pairs(planes, stores))
+    mates = [lax.ppermute(x, "store", swap) for x in query]
+    half = query[0].shape[0]
+    streams = [query[0], mates[0], query[1], mates[1]]
+    marks = [((mate, i * half, 0, half),) for i in range(2) for mate in range(2)]
+    early = query + mates
+    spots = [(0, ((mate, i * half, 0, half),)) for mate in range(2) for i in range(2)]
     total = None
-    for k in range(1, places // 2):
-        if k == places // 2 - 1:
+    for step in range(1, places // 2):
+        if step == places // 2 - 1:
             total = early_scores(stored, others, early, spots, None, False, places, planes)
             early, spots = [], []
-        for j in range(streams):
-            ahead[j], behind[j] = on(ahead[j]), back(behind[j])
-            early += [ahead[j], behind[j]]
-            spots += [(-k, firsts[j]), (k, firsts[j])]
-    far = [on(ahead[0]), back(behind[1])]
-    spots_far = [(places // 2, first) for first in firsts]
-    keep, send = early_scores(stored, others, early, spots, total, True, places, planes)
-    got = lax.ppermute(send, "store", swap)
+        streams = [on(x) for x in streams]
+        early += streams
+        spots += [(step, mark) for mark in marks]
+    far = [on(x) for x in streams[::2]]
+    keep, *send = early_scores(stored, others, early, spots, total, True, places, planes)
+    got = [lax.ppermute(x, "store", swap) for x in send]
     far += [lax.ppermute(x, "store", swap) for x in far]
-    return final_scores(stored, keep, got, far, spots_far, places, planes)
+    spots = [(mate, i * half) for mate in range(2) for i in range(2)]
+    return final_scores(stored, keep, got, far, spots, places, planes)
 
 
 def solution(mesh):

time: 55 us -> 53.9 us (0.980)
  waiting for transfers between devices: 10.1 us -> 4.37 us
  starting transfers between devices: 26.5 us -> 31.1 us
    ppermute x15 -> x18, waiting for transfers between devices: 6.92 us -> 1.15 us  [the longest x14 1.14 us: body(): lax.ppermute(x, ('width', 'store'), ring_pairs(planes, stores))]
    ppermute x15 -> x18, starting transfers between devices: 15.2 us -> 19.9 us  [the longest x14 18.8 us: body(): lax.ppermute(x, ('width', 'store'), ring_pairs(planes, stores))]
  transfers between devices with their start and end apart: 24 -> 27, of which waited for: 12 -> 8; matrix products, arithmetic and copies ran while one was open for 0% -> 0% of each run, Pallas kernels for 23% -> 24%
where the time goes in v5:
time: 53.9 us; the launch traced here: 53.7 us
  starting transfers between devices  31.1 us (58%)
  Pallas kernels  18.1 us (34%)
  waiting for transfers between devices  4.37 us (8%)
    ppermute x14, starting transfers between devices, body(): lax.ppermute(x, ('width', 'store'), ring_pairs(planes, stores))  18.8 us
    ppermute x6, starting transfers between devices, turn(): lax.ppermute(x, 'width', [(i, (i + d) % planes) for i in range(planes)])  11.1 us
    pallas_call x2, Pallas kernels, project(): pl.pallas_call(functools.partial(project_kernel, planes, turns), in_specs...  6.32 us
    pallas_call x1, Pallas kernels, load(): pl.pallas_call(load_kernel, in_specs=[vmem, pl.BlockSpec(memory_space=plt...  3.61 us
    pallas_call x1, Pallas kernels, query_transposed(): pl.pallas_call(functools.partial(query_kernel, len(factors)), in_specs=[p...  2.89 us
    pallas_call x2, Pallas kernels, early_scores(): pl.pallas_call(functools.partial(early_kernel, places, planes, spots, boo...  2.73 us
    ppermute x6, waiting for transfers between devices, turn(): lax.ppermute(x, 'width', [(i, (i + d) % planes) for i in range(planes)])  1.87 us
    ppermute x2, waiting for transfers between devices, body(): far += [lax.ppermute(x, 'store', swap) for x in far]  1.34 us
  transfers between devices with their start and end apart: 27, of which 8 were waited for; matrix products, arithmetic and copies ran while one was open for 0% of the time, Pallas kernels for 24%

profile of v5, /device:TPU:0, one launch (start us, length us, event | category | flops | bytes accessed | tf_op | source)
XLA Modules:
  0.0 53.7 jit_solution(12805221193307199232)
XLA Ops:
  0.0 3.9 %project.3 = (bf16[256,128]{1,0:T(8,128)(2,1)S(1)}, bf16[256,128]{1,0:T(8,128)(2,1)S(1)}, bf16[256,128]{1,0:T(8,128)(2,1)S(1)}) custom-call(bf16[1024,2048]{1,0:T(8,128)(2,1)} %act_hbm.3, bf16[1024,2048]{1,0:T(8,128)(2,1)} %grad_hbm.3, bf16[64,2048]{1,0:T(8,128)(2,1)} %bitcast.5, bf16[64,2048]{1,0:T(8,128)(2,1)} %bitcast.7), custom_call_target="tpu_custom_call" | custom-call | flops 402653184 | bytes 12582912 | tf_op jit(solution)/shard_map/project/pallas_call | solution.py:59
  3.9 3.1 %collective-permute-start = (bf16[256,128]{1,0:T(8,128)(2,1)S(1)}, bf16[256,128]{1,0:T(8,128)(2,1)S(1)}, u32[]{:S(2)}, u32[]{:S(2)}) collective-permute-start(bf16[256,128]{1,0:T(8,128)(2,1)S(1)} %get-tuple-element.17), channel_id=1, source_target_pairs={{0,4},{4,8},{8,12},{12,0},{1,5},{5,9},{9,13},{13,1},{2,6},{6,10},{... | collective-permute-start | bytes 196616 | tf_op jit(solution)/shard_map/ppermute | solution.py:278
  7.0 2.6 %collective-permute-start.1 = (bf16[256,128]{1,0:T(8,128)(2,1)S(1)}, bf16[256,128]{1,0:T(8,128)(2,1)S(1)}, u32[]{:S(2)}, u32[]{:S(2)}) collective-permute-start(bf16[256,128]{1,0:T(8,128)(2,1)S(1)} %get-tuple-element.18), channel_id=1, source_target_pairs={{0,8},{4,12},{8,0},{12,4},{1,9},{5,13},{9,1},{13,5},{2,10},{6,14},... | collective-permute-start | bytes 196616 | tf_op jit(solution)/shard_map/ppermute | solution.py:278
  9.6 1.3 %collective-permute-start.2 = (bf16[256,128]{1,0:T(8,128)(2,1)S(1)}, bf16[256,128]{1,0:T(8,128)(2,1)S(1)}, u32[]{:S(2)}, u32[]{:S(2)}) collective-permute-start(bf16[256,128]{1,0:T(8,128)(2,1)S(1)} %get-tuple-element.19), channel_id=1, source_target_pairs={{0,12},{4,0},{8,4},{12,8},{1,13},{5,1},{9,5},{13,9},{2,14},{6,2},{... | collective-permute-start | bytes 196616 | tf_op jit(solution)/shard_map/ppermute | solution.py:278
  10.9 2.4 %project.2 = f32[256,128]{1,0:T(8,128)S(1)} custom-call(bf16[1024,2048]{1,0:T(8,128)(2,1)} %act_hbm.3, bf16[1024,2048]{1,0:T(8,128)(2,1)} %grad_hbm.3, bf16[64,2048]{1,0:T(8,128)(2,1)} %bitcast.6, bf16[64,2048]{1,0:T(8,128)(2,1)} %bitcast.8), custom_call_target="tpu_custom_call" | custom-call | flops 134217728 | bytes 4194304 | tf_op jit(solution)/shard_map/project/pallas_call | solution.py:59
  13.4 0.0 collective-permute-done
  13.4 0.7 %collective-permute-done.1 = bf16[256,128]{1,0:T(8,128)(2,1)S(1)} collective-permute-done((bf16[256,128]{1,0:T(8,128)(2,1)S(1)}, bf16[256,128]{1,0:T(8,128)(2,1)S(1)}, u32[]{:S(2)}, u32[]{:S(2)}) %collective-permute-start.1) | collective-permute-done | bytes 65568 | tf_op jit(solution)/shard_map/ppermute | solution.py:278
  14.0 0.2 collective-permute-done.2
  14.3 1.6 %collective-permute-start.4 = (bf16[256,128]{1,0:T(8,128)(2,1)S(1)}, bf16[256,128]{1,0:T(8,128)(2,1)S(1)}, u32[]{:S(2)}, u32[]{:S(2)}) collective-permute-start(bf16[256,128]{1,0:T(8,128)(2,1)S(1)} %add_convert_fusion.rest_0_), channel_id=1, source_target_pairs={{0,4},{4,8},{8,12},{12,0},{1,5},{5,9},{9,13},{13,1},{2,6},{6,10},{... | collective-permute-start | bytes 196616 | tf_op jit(solution)/shard_map/ppermute | solution.py:278
  16.0 2.0 %collective-permute-start.5 = (bf16[256,128]{1,0:T(8,128)(2,1)S(1)}, bf16[256,128]{1,0:T(8,128)(2,1)S(1)}, u32[]{:S(2)}, u32[]{:S(2)}) collective-permute-start(bf16[256,128]{1,0:T(8,128)(2,1)S(1)} %add_convert_fusion.rest_0_), channel_id=1, source_target_pairs={{0,8},{4,12},{8,0},{12,4},{1,9},{5,13},{9,1},{13,5},{2,10},{6,14},... | collective-permute-start | bytes 196616 | tf_op jit(solution)/shard_map/ppermute | solution.py:278
  18.0 0.4 collective-permute-start.6
  18.4 3.6 %load.1 = (bf16[1024,4096]{1,0:T(8,128)(2,1)S(1)}, s32[16]{0:T(128)S(4)}) custom-call(s32[8,128]{1,0:T(8,128)S(1)} %bitcast.3, bf16[1024,4096]{1,0:T(8,128)(2,1)} %hbm_ref), custom_call_target="tpu_custom_call" | custom-call | bytes 33554432 | tf_op jit(solution)/shard_map/load/pallas_call | solution.py:94
  22.0 0.0 collective-permute-done.4.rest_1_
  22.0 0.6 %collective-permute-done.5.rest_2_ = bf16[256,128]{1,0:T(8,128)(2,1)S(1)} collective-permute-done((bf16[256,128]{1,0:T(8,128)(2,1)S(1)}, bf16[256,128]{1,0:T(8,128)(2,1)S(1)}, u32[]{:S(2)}, u32[]{:S(2)}) %collective-permute-start.5) | collective-permute-done | bytes 65568 | tf_op jit(solution)/shard_map/ppermute | solution.py:278
  22.6 0.4 collective-permute-done.6.rest_3_
  23.0 2.9 %query.1 = (bf16[512,128]{1,0:T(8,128)(2,1)S(1)}, bf16[128,4096]{1,0:T(8,128)(2,1)S(1)}) custom-call(s32[16]{0:T(128)S(4)} %get-tuple-element.22.start_ref, s32[8,128]{1,0:T(8,128)S(1)} %bitcast.4, bf16[256,128]{1,0:T(8,128)(2,1)S(1)} %add_convert_fusion.rest_0_, bf16[256,128]{1,0:T(8,128)(2,1)S(1)} %collective-permute-done.4.rest_1_, ...), custom_call_target="tpu_custom_call" | custom-call | tf_op jit(solution)/shard_map/query/pallas_call | solution.py:161
  25.9 1.2 %curve.1.rest_1_ = bf16[512,128]{1,0:T(8,128)(2,1)S(1)} custom-call(bf16[128,4096]{1,0:T(8,128)(2,1)S(1)} %get-tuple-element.25.pe_ref, bf16[1024,4096]{1,0:T(8,128)(2,1)S(1)} %get-tuple-element.23.rest_4_.ic_ref), custom_call_target="tpu_custom_call" | custom-call | flops 26843545600 | bytes 4194304 | tf_op jit(solution)/shard_map/curve/pallas_call | solution.py:175
  27.1 0.1 collective-permute-start.17
  27.2 0.5 collective-permute-start.10
  27.7 1.5 %collective-permute-start.14 = (bf16[512,128]{1,0:T(8,128)(2,1)S(1)}, bf16[512,128]{1,0:T(8,128)(2,1)S(1)}, u32[]{:S(2)}, u32[]{:S(2)}) collective-permute-start(bf16[512,128]{1,0:T(8,128)(2,1)S(1)} %curve.1.rest_1_), channel_id=1, source_target_pairs={{0,4},{1,3},{4,8},{5,1},{8,12},{9,5},{12,14},{13,9},{14,10},{15,13... | collective-permute-start | bytes 393224 | tf_op jit(solution)/shard_map/ppermute | solution.py:317
  29.2 0.0 collective-permute-start.7
  29.3 1.9 %collective-permute-start.18 = (bf16[512,128]{1,0:T(8,128)(2,1)S(1)}, bf16[512,128]{1,0:T(8,128)(2,1)S(1)}, u32[]{:S(2)}, u32[]{:S(2)}) collective-permute-start(bf16[512,128]{1,0:T(8,128)(2,1)S(1)} %collective-permute-done.17.rest_3_), channel_id=1, source_target_pairs={{0,4},{1,3},{4,8},{5,1},{8,12},{9,5},{12,14},{13,9},{14,10},{15,13... | collective-permute-start | bytes 393224 | tf_op jit(solution)/shard_map/ppermute | solution.py:317
  31.1 1.2 %collective-permute-start.11 = (bf16[512,128]{1,0:T(8,128)(2,1)S(1)}, bf16[512,128]{1,0:T(8,128)(2,1)S(1)}, u32[]{:S(2)}, u32[]{:S(2)}) collective-permute-start(bf16[512,128]{1,0:T(8,128)(2,1)S(1)} %collective-permute-done.10.rest_2_), channel_id=1, source_target_pairs={{0,4},{1,3},{4,8},{5,1},{8,12},{9,5},{12,14},{13,9},{14,10},{15,13... | collective-permute-start | bytes 393224 | tf_op jit(solution)/shard_map/ppermute | solution.py:317
  32.4 0.3 collective-permute-done.14.rest_6_
  32.7 1.5 %collective-permute-start.15 = (bf16[512,128]{1,0:T(8,128)(2,1)S(1)}, bf16[512,128]{1,0:T(8,128)(2,1)S(1)}, u32[]{:S(2)}, u32[]{:S(2)}) collective-permute-start(bf16[512,128]{1,0:T(8,128)(2,1)S(1)} %collective-permute-done.14.rest_6_), channel_id=1, source_target_pairs={{0,4},{1,3},{4,8},{5,1},{8,12},{9,5},{12,14},{13,9},{14,10},{15,13... | collective-permute-start | bytes 393224 | tf_op jit(solution)/shard_map/ppermute | solution.py:317
  34.2 0.0 collective-permute-done.7.rest_4_
  34.2 1.4 %collective-permute-start.8 = (bf16[512,128]{1,0:T(8,128)(2,1)S(1)}, bf16[512,128]{1,0:T(8,128)(2,1)S(1)}, u32[]{:S(2)}, u32[]{:S(2)}) collective-permute-start(bf16[512,128]{1,0:T(8,128)(2,1)S(1)} %collective-permute-done.7.rest_4_), channel_id=1, source_target_pairs={{0,4},{1,3},{4,8},{5,1},{8,12},{9,5},{12,14},{13,9},{14,10},{15,13... | collective-permute-start | bytes 393224 | tf_op jit(solution)/shard_map/ppermute | solution.py:317
  35.6 0.0 collective-permute-done.18.rest_7_
  35.6 1.4 %collective-permute-start.19 = (bf16[512,128]{1,0:T(8,128)(2,1)S(1)}, bf16[512,128]{1,0:T(8,128)(2,1)S(1)}, u32[]{:S(2)}, u32[]{:S(2)}) collective-permute-start(bf16[512,128]{1,0:T(8,128)(2,1)S(1)} %collective-permute-done.18.rest_7_), channel_id=1, source_target_pairs={{0,4},{1,3},{4,8},{5,1},{8,12},{9,5},{12,14},{13,9},{14,10},{15,13... | collective-permute-start | bytes 393224 | tf_op jit(solution)/shard_map/ppermute | solution.py:317
  37.0 1.4 %collective-permute-start.12 = (bf16[512,128]{1,0:T(8,128)(2,1)S(1)}, bf16[512,128]{1,0:T(8,128)(2,1)S(1)}, u32[]{:S(2)}, u32[]{:S(2)}) collective-permute-start(bf16[512,128]{1,0:T(8,128)(2,1)S(1)} %collective-permute-done.11.rest_5_), channel_id=1, source_target_pairs={{0,4},{1,3},{4,8},{5,1},{8,12},{9,5},{12,14},{13,9},{14,10},{15,13... | collective-permute-start | bytes 393224 | tf_op jit(solution)/shard_map/ppermute | solution.py:317
  38.4 0.0 collective-permute-done.15.rest_10_
  38.4 1.4 %collective-permute-start.16 = (bf16[512,128]{1,0:T(8,128)(2,1)S(1)}, bf16[512,128]{1,0:T(8,128)(2,1)S(1)}, u32[]{:S(2)}, u32[]{:S(2)}) collective-permute-start(bf16[512,128]{1,0:T(8,128)(2,1)S(1)} %collective-permute-done.15.rest_10_), channel_id=1, source_target_pairs={{0,4},{1,3},{4,8},{5,1},{8,12},{9,5},{12,14},{13,9},{14,10},{15,13... | collective-permute-start | bytes 393224 | tf_op jit(solution)/shard_map/ppermute | solution.py:317
  39.8 0.0 collective-permute-done.8.rest_8_
  39.8 1.4 %collective-permute-start.9 = (bf16[512,128]{1,0:T(8,128)(2,1)S(1)}, bf16[512,128]{1,0:T(8,128)(2,1)S(1)}, u32[]{:S(2)}, u32[]{:S(2)}) collective-permute-start(bf16[512,128]{1,0:T(8,128)(2,1)S(1)} %collective-permute-done.8.rest_8_), channel_id=1, source_target_pairs={{0,4},{1,3},{4,8},{5,1},{8,12},{9,5},{12,14},{13,9},{14,10},{15,13... | collective-permute-start | bytes 393224 | tf_op jit(solution)/shard_map/ppermute | solution.py:317
  41.2 1.4 %collective-permute-start.20 = (bf16[512,128]{1,0:T(8,128)(2,1)S(1)}, bf16[512,128]{1,0:T(8,128)(2,1)S(1)}, u32[]{:S(2)}, u32[]{:S(2)}) collective-permute-start(bf16[512,128]{1,0:T(8,128)(2,1)S(1)} %collective-permute-done.19.rest_11_), channel_id=1, source_target_pairs={{0,4},{1,3},{4,8},{5,1},{8,12},{9,5},{12,14},{13,9},{14,10},{15,13... | collective-permute-start | bytes 393224 | tf_op jit(solution)/shard_map/ppermute | solution.py:317
  42.6 0.0 collective-permute-done.12.rest_9_
  42.6 1.4 %collective-permute-start.13 = (bf16[512,128]{1,0:T(8,128)(2,1)S(1)}, bf16[512,128]{1,0:T(8,128)(2,1)S(1)}, u32[]{:S(2)}, u32[]{:S(2)}) collective-permute-start(bf16[512,128]{1,0:T(8,128)(2,1)S(1)} %collective-permute-done.12.rest_9_), channel_id=1, source_target_pairs={{0,4},{1,3},{4,8},{5,1},{8,12},{9,5},{12,14},{13,9},{14,10},{15,13... | collective-permute-start | bytes 393224 | tf_op jit(solution)/shard_map/ppermute | solution.py:317
  44.0 1.4 %collective-permute-start.24 = (bf16[512,128]{1,0:T(8,128)(2,1)S(1)}, bf16[512,128]{1,0:T(8,128)(2,1)S(1)}, u32[]{:S(2)}, u32[]{:S(2)}) collective-permute-start(bf16[512,128]{1,0:T(8,128)(2,1)S(1)} %collective-permute-done.16.rest_2_), channel_id=1, source_target_pairs={{0,4},{1,3},{4,8},{5,1},{8,12},{9,5},{12,14},{13,9},{14,10},{15,13... | collective-permute-start | bytes 393224 | tf_op jit(solution)/shard_map/ppermute | solution.py:317
  45.4 1.4 %collective-permute-start.23 = (bf16[512,128]{1,0:T(8,128)(2,1)S(1)}, bf16[512,128]{1,0:T(8,128)(2,1)S(1)}, u32[]{:S(2)}, u32[]{:S(2)}) collective-permute-start(bf16[512,128]{1,0:T(8,128)(2,1)S(1)} %collective-permute-done.9.rest_0_), channel_id=1, source_target_pairs={{0,4},{1,3},{4,8},{5,1},{8,12},{9,5},{12,14},{13,9},{14,10},{15,13... | collective-permute-start | bytes 393224 | tf_op jit(solution)/shard_map/ppermute | solution.py:317
  46.8 1.6 %early_scores.2.rest_4_ = f32[4,2,256,128]{3,2,1,0:T(8,128)S(1)} custom-call(bf16[256,4096]{1,0:T(8,128)(2,1)S(1)} %copy-done, bf16[256,4096]{1,0:T(8,128)(2,1)S(1)} %collective-permute-done.3.other_ref, bf16[512,128]{1,0:T(8,128)(2,1)S(1)} %get-tuple-element.24.rest_0_, bf16[512,128]{1,0:T(8,128)(2,1)S(1)} %curve.1.rest_1_, ...), custom_call_target="tpu_custom_call" | custom-call | tf_op jit(solution)/shard_map/early_scores/pallas_call | solution.py:225
  48.5 1.1 %early_scores.3 = (f32[512,256]{1,0:T(8,128)S(1)}, f32[256,256]{1,0:T(8,128)S(1)}, f32[256,256]{1,0:T(8,128)S(1)}) custom-call(bf16[256,4096]{1,0:T(8,128)(2,1)S(1)} %copy-done, bf16[256,4096]{1,0:T(8,128)(2,1)S(1)} %collective-permute-done.3.other_ref, bf16[512,128]{1,0:T(8,128)(2,1)S(1)} %collective-permute-done.9.rest_0_, ...), custom_call_target="tpu_custom_call" | custom-call | tf_op jit(solution)/shard_map/early_scores/pallas_call | solution.py:225
  49.6 0.1 collective-permute-start.21
  49.7 0.5 collective-permute-start.22
  50.2 0.1 collective-permute-start.26
  50.3 0.8 %collective-permute-done.23.rest_0_ = bf16[512,128]{1,0:T(8,128)(2,1)S(1)} collective-permute-done((bf16[512,128]{1,0:T(8,128)(2,1)S(1)}, bf16[512,128]{1,0:T(8,128)(2,1)S(1)}, u32[]{:S(2)}, u32[]{:S(2)}) %collective-permute-start.23) | collective-permute-done | bytes 131104 | tf_op jit(solution)/shard_map/ppermute | solution.py:317
  51.1 0.7 %collective-permute-done.26.rest_3_ = bf16[512,128]{1,0:T(8,128)(2,1)S(1)} collective-permute-done((bf16[512,128]{1,0:T(8,128)(2,1)S(1)}, bf16[512,128]{1,0:T(8,128)(2,1)S(1)}, u32[]{:S(2)}, u32[]{:S(2)}) %collective-permute-start.26) | collective-permute-done | bytes 131104 | tf_op jit(solution)/shard_map/ppermute | solution.py:335
  51.8 0.6 %collective-permute-done.25.rest_2_ = bf16[512,128]{1,0:T(8,128)(2,1)S(1)} collective-permute-done((bf16[512,128]{1,0:T(8,128)(2,1)S(1)}, bf16[512,128]{1,0:T(8,128)(2,1)S(1)}, u32[]{:S(2)}, u32[]{:S(2)}) %collective-permute-start.25) | collective-permute-done | bytes 131104 | tf_op jit(solution)/shard_map/ppermute | solution.py:335
  52.4 1.3 %final_scores.1 = f32[512,256]{1,0:T(8,128)} custom-call(bf16[256,4096]{1,0:T(8,128)(2,1)S(1)} %copy-done, f32[512,256]{1,0:T(8,128)S(1)} %get-tuple-element.26.keep_ref, f32[256,256]{1,0:T(8,128)S(1)} %collective-permute-done.21.got_ref, f32[256,256]{1,0:T(8,128)S(1)} %collective-permute-done.22.more_ref, ...), custom_call_target="tpu_custom_call" | custom-call | tf_op jit(solution)/shard_map/final_scores/pallas_call | solution.py:257
  (19 shorter events, 0.1 us)
Async XLA Ops:
  3.9 9.5 %collective-permute-start = (bf16[256,128]{1,0:T(8,128)(2,1)S(1)}, bf16[256,128]{1,0:T(8,128)(2,1)S(1)}, u32[]{:S(2)}, u32[]{:S(2)}) collective-permute-start(bf16[256,128]{1,0:T(8,128)(2,1)S(1)} %get-tuple-element.17), channel_id=1, source_target_pairs={{0,4},{4,8},{8,12},{12,0},{1,5},{5,9},{9,13},{13,1},{2,6},{6,10},{... | collective-permute-start | bytes 196616 | tf_op jit(solution)/shard_map/ppermute | solution.py:278
  7.0 7.1 %collective-permute-start.1 = (bf16[256,128]{1,0:T(8,128)(2,1)S(1)}, bf16[256,128]{1,0:T(8,128)(2,1)S(1)}, u32[]{:S(2)}, u32[]{:S(2)}) collective-permute-start(bf16[256,128]{1,0:T(8,128)(2,1)S(1)} %get-tuple-element.18), channel_id=1, source_target_pairs={{0,8},{4,12},{8,0},{12,4},{1,9},{5,13},{9,1},{13,5},{2,10},{6,14},... | collective-permute-start | bytes 196616 | tf_op jit(solution)/shard_map/ppermute | solution.py:278
  9.6 8.8 %copy-start = (bf16[256,4096]{1,0:T(8,128)(2,1)S(1)}, bf16[256,4096]{1,0:T(8,128)(2,1)}, u32[]{:S(2)}) copy-start(bf16[256,4096]{1,0:T(8,128)(2,1)} %stored_ref) | copy-start | bytes 6291460
  9.6 8.8 %copy-start.1 = (s32[1,1024]{1,0:T(1,128)S(1)}, s32[1,1024]{1,0:T(1,128)}, u32[]{:S(2)}) copy-start(s32[1,1024]{1,0:T(1,128)} %param.9) | copy-start | bytes 12292
  9.6 4.7 %collective-permute-start.2 = (bf16[256,128]{1,0:T(8,128)(2,1)S(1)}, bf16[256,128]{1,0:T(8,128)(2,1)S(1)}, u32[]{:S(2)}, u32[]{:S(2)}) collective-permute-start(bf16[256,128]{1,0:T(8,128)(2,1)S(1)} %get-tuple-element.19), channel_id=1, source_target_pairs={{0,12},{4,0},{8,4},{12,8},{1,13},{5,1},{9,5},{13,9},{2,14},{6,2},{... | collective-permute-start | bytes 196616 | tf_op jit(solution)/shard_map/ppermute | solution.py:278
  14.3 7.7 %collective-permute-start.4 = (bf16[256,128]{1,0:T(8,128)(2,1)S(1)}, bf16[256,128]{1,0:T(8,128)(2,1)S(1)}, u32[]{:S(2)}, u32[]{:S(2)}) collective-permute-start(bf16[256,128]{1,0:T(8,128)(2,1)S(1)} %add_convert_fusion.rest_0_), channel_id=1, source_target_pairs={{0,4},{4,8},{8,12},{12,0},{1,5},{5,9},{9,13},{13,1},{2,6},{6,10},{... | collective-permute-start | bytes 196616 | tf_op jit(solution)/shard_map/ppermute | solution.py:278
  16.0 6.7 %collective-permute-start.5 = (bf16[256,128]{1,0:T(8,128)(2,1)S(1)}, bf16[256,128]{1,0:T(8,128)(2,1)S(1)}, u32[]{:S(2)}, u32[]{:S(2)}) collective-permute-start(bf16[256,128]{1,0:T(8,128)(2,1)S(1)} %add_convert_fusion.rest_0_), channel_id=1, source_target_pairs={{0,8},{4,12},{8,0},{12,4},{1,9},{5,13},{9,1},{13,5},{2,10},{6,14},... | collective-permute-start | bytes 196616 | tf_op jit(solution)/shard_map/ppermute | solution.py:278
  18.0 5.0 %collective-permute-start.6 = (bf16[256,128]{1,0:T(8,128)(2,1)S(1)}, bf16[256,128]{1,0:T(8,128)(2,1)S(1)}, u32[]{:S(2)}, u32[]{:S(2)}) collective-permute-start(bf16[256,128]{1,0:T(8,128)(2,1)S(1)} %add_convert_fusion.rest_0_), channel_id=1, source_target_pairs={{0,12},{4,0},{8,4},{12,8},{1,13},{5,1},{9,5},{13,9},{2,14},{6,2},{... | collective-permute-start | bytes 196616 | tf_op jit(solution)/shard_map/ppermute | solution.py:278
  18.4 28.4 %collective-permute-start.3 = (bf16[256,4096]{1,0:T(8,128)(2,1)S(1)}, bf16[256,4096]{1,0:T(8,128)(2,1)S(1)}, u32[]{:S(2)}, u32[]{:S(2)}) collective-permute-start(bf16[256,4096]{1,0:T(8,128)(2,1)S(1)} %copy-done), channel_id=1, source_target_pairs={{0,1},{1,0},{2,3},{3,2},{4,5},{5,4},{6,7},{7,6},{8,9},{9,8},{10,11... | collective-permute-start | bytes 6291464 | tf_op jit(solution)/shard_map/ppermute | solution.py:314
  27.1 2.1 %collective-permute-start.17 = (bf16[512,128]{1,0:T(8,128)(2,1)S(1)}, bf16[512,128]{1,0:T(8,128)(2,1)S(1)}, u32[]{:S(2)}, u32[]{:S(2)}) collective-permute-start(bf16[512,128]{1,0:T(8,128)(2,1)S(1)} %curve.1.rest_1_), channel_id=1, source_target_pairs={{0,1},{1,0},{2,3},{3,2},{4,5},{5,4},{6,7},{7,6},{8,9},{9,8},{10,11... | collective-permute-start | bytes 393224 | tf_op jit(solution)/shard_map/ppermute | solution.py:318
  27.2 3.9 %collective-permute-start.10 = (bf16[512,128]{1,0:T(8,128)(2,1)S(1)}, bf16[512,128]{1,0:T(8,128)(2,1)S(1)}, u32[]{:S(2)}, u32[]{:S(2)}) collective-permute-start(bf16[512,128]{1,0:T(8,128)(2,1)S(1)} %get-tuple-element.24.rest_0_), channel_id=1, source_target_pairs={{0,1},{1,0},{2,3},{3,2},{4,5},{5,4},{6,7},{7,6},{8,9},{9,8},{10,11... | collective-permute-start | bytes 393224 | tf_op jit(solution)/shard_map/ppermute | solution.py:318
  27.7 5.0 %collective-permute-start.14 = (bf16[512,128]{1,0:T(8,128)(2,1)S(1)}, bf16[512,128]{1,0:T(8,128)(2,1)S(1)}, u32[]{:S(2)}, u32[]{:S(2)}) collective-permute-start(bf16[512,128]{1,0:T(8,128)(2,1)S(1)} %curve.1.rest_1_), channel_id=1, source_target_pairs={{0,4},{1,3},{4,8},{5,1},{8,12},{9,5},{12,14},{13,9},{14,10},{15,13... | collective-permute-start | bytes 393224 | tf_op jit(solution)/shard_map/ppermute | solution.py:317
  29.2 5.0 %collective-permute-start.7 = (bf16[512,128]{1,0:T(8,128)(2,1)S(1)}, bf16[512,128]{1,0:T(8,128)(2,1)S(1)}, u32[]{:S(2)}, u32[]{:S(2)}) collective-permute-start(bf16[512,128]{1,0:T(8,128)(2,1)S(1)} %get-tuple-element.24.rest_0_), channel_id=1, source_target_pairs={{0,4},{1,3},{4,8},{5,1},{8,12},{9,5},{12,14},{13,9},{14,10},{15,13... | collective-permute-start | bytes 393224 | tf_op jit(solution)/shard_map/ppermute | solution.py:317
  29.3 6.3 %collective-permute-start.18 = (bf16[512,128]{1,0:T(8,128)(2,1)S(1)}, bf16[512,128]{1,0:T(8,128)(2,1)S(1)}, u32[]{:S(2)}, u32[]{:S(2)}) collective-permute-start(bf16[512,128]{1,0:T(8,128)(2,1)S(1)} %collective-permute-done.17.rest_3_), channel_id=1, source_target_pairs={{0,4},{1,3},{4,8},{5,1},{8,12},{9,5},{12,14},{13,9},{14,10},{15,13... | collective-permute-start | bytes 393224 | tf_op jit(solution)/shard_map/ppermute | solution.py:317
  31.1 5.9 %collective-permute-start.11 = (bf16[512,128]{1,0:T(8,128)(2,1)S(1)}, bf16[512,128]{1,0:T(8,128)(2,1)S(1)}, u32[]{:S(2)}, u32[]{:S(2)}) collective-permute-start(bf16[512,128]{1,0:T(8,128)(2,1)S(1)} %collective-permute-done.10.rest_2_), channel_id=1, source_target_pairs={{0,4},{1,3},{4,8},{5,1},{8,12},{9,5},{12,14},{13,9},{14,10},{15,13... | collective-permute-start | bytes 393224 | tf_op jit(solution)/shard_map/ppermute | solution.py:317
  32.7 5.7 %collective-permute-start.15 = (bf16[512,128]{1,0:T(8,128)(2,1)S(1)}, bf16[512,128]{1,0:T(8,128)(2,1)S(1)}, u32[]{:S(2)}, u32[]{:S(2)}) collective-permute-start(bf16[512,128]{1,0:T(8,128)(2,1)S(1)} %collective-permute-done.14.rest_6_), channel_id=1, source_target_pairs={{0,4},{1,3},{4,8},{5,1},{8,12},{9,5},{12,14},{13,9},{14,10},{15,13... | collective-permute-start | bytes 393224 | tf_op jit(solution)/shard_map/ppermute | solution.py:317
  34.2 5.6 %collective-permute-start.8 = (bf16[512,128]{1,0:T(8,128)(2,1)S(1)}, bf16[512,128]{1,0:T(8,128)(2,1)S(1)}, u32[]{:S(2)}, u32[]{:S(2)}) collective-permute-start(bf16[512,128]{1,0:T(8,128)(2,1)S(1)} %collective-permute-done.7.rest_4_), channel_id=1, source_target_pairs={{0,4},{1,3},{4,8},{5,1},{8,12},{9,5},{12,14},{13,9},{14,10},{15,13... | collective-permute-start | bytes 393224 | tf_op jit(solution)/shard_map/ppermute | solution.py:317
  35.6 5.6 %collective-permute-start.19 = (bf16[512,128]{1,0:T(8,128)(2,1)S(1)}, bf16[512,128]{1,0:T(8,128)(2,1)S(1)}, u32[]{:S(2)}, u32[]{:S(2)}) collective-permute-start(bf16[512,128]{1,0:T(8,128)(2,1)S(1)} %collective-permute-done.18.rest_7_), channel_id=1, source_target_pairs={{0,4},{1,3},{4,8},{5,1},{8,12},{9,5},{12,14},{13,9},{14,10},{15,13... | collective-permute-start | bytes 393224 | tf_op jit(solution)/shard_map/ppermute | solution.py:317
  37.0 5.6 %collective-permute-start.12 = (bf16[512,128]{1,0:T(8,128)(2,1)S(1)}, bf16[512,128]{1,0:T(8,128)(2,1)S(1)}, u32[]{:S(2)}, u32[]{:S(2)}) collective-permute-start(bf16[512,128]{1,0:T(8,128)(2,1)S(1)} %collective-permute-done.11.rest_5_), channel_id=1, source_target_pairs={{0,4},{1,3},{4,8},{5,1},{8,12},{9,5},{12,14},{13,9},{14,10},{15,13... | collective-permute-start | bytes 393224 | tf_op jit(solution)/shard_map/ppermute | solution.py:317
  38.4 5.6 %collective-permute-start.16 = (bf16[512,128]{1,0:T(8,128)(2,1)S(1)}, bf16[512,128]{1,0:T(8,128)(2,1)S(1)}, u32[]{:S(2)}, u32[]{:S(2)}) collective-permute-start(bf16[512,128]{1,0:T(8,128)(2,1)S(1)} %collective-permute-done.15.rest_10_), channel_id=1, source_target_pairs={{0,4},{1,3},{4,8},{5,1},{8,12},{9,5},{12,14},{13,9},{14,10},{15,13... | collective-permute-start | bytes 393224 | tf_op jit(solution)/shard_map/ppermute | solution.py:317
  39.8 5.6 %collective-permute-start.9 = (bf16[512,128]{1,0:T(8,128)(2,1)S(1)}, bf16[512,128]{1,0:T(8,128)(2,1)S(1)}, u32[]{:S(2)}, u32[]{:S(2)}) collective-permute-start(bf16[512,128]{1,0:T(8,128)(2,1)S(1)} %collective-permute-done.8.rest_8_), channel_id=1, source_target_pairs={{0,4},{1,3},{4,8},{5,1},{8,12},{9,5},{12,14},{13,9},{14,10},{15,13... | collective-permute-start | bytes 393224 | tf_op jit(solution)/shard_map/ppermute | solution.py:317
  41.2 7.2 %collective-permute-start.20 = (bf16[512,128]{1,0:T(8,128)(2,1)S(1)}, bf16[512,128]{1,0:T(8,128)(2,1)S(1)}, u32[]{:S(2)}, u32[]{:S(2)}) collective-permute-start(bf16[512,128]{1,0:T(8,128)(2,1)S(1)} %collective-permute-done.19.rest_11_), channel_id=1, source_target_pairs={{0,4},{1,3},{4,8},{5,1},{8,12},{9,5},{12,14},{13,9},{14,10},{15,13... | collective-permute-start | bytes 393224 | tf_op jit(solution)/shard_map/ppermute | solution.py:317
  42.6 5.9 %collective-permute-start.13 = (bf16[512,128]{1,0:T(8,128)(2,1)S(1)}, bf16[512,128]{1,0:T(8,128)(2,1)S(1)}, u32[]{:S(2)}, u32[]{:S(2)}) collective-permute-start(bf16[512,128]{1,0:T(8,128)(2,1)S(1)} %collective-permute-done.12.rest_9_), channel_id=1, source_target_pairs={{0,4},{1,3},{4,8},{5,1},{8,12},{9,5},{12,14},{13,9},{14,10},{15,13... | collective-permute-start | bytes 393224 | tf_op jit(solution)/shard_map/ppermute | solution.py:317
  44.0 6.2 %collective-permute-start.24 = (bf16[512,128]{1,0:T(8,128)(2,1)S(1)}, bf16[512,128]{1,0:T(8,128)(2,1)S(1)}, u32[]{:S(2)}, u32[]{:S(2)}) collective-permute-start(bf16[512,128]{1,0:T(8,128)(2,1)S(1)} %collective-permute-done.16.rest_2_), channel_id=1, source_target_pairs={{0,4},{1,3},{4,8},{5,1},{8,12},{9,5},{12,14},{13,9},{14,10},{15,13... | collective-permute-start | bytes 393224 | tf_op jit(solution)/shard_map/ppermute | solution.py:317
  45.4 5.6 %collective-permute-start.23 = (bf16[512,128]{1,0:T(8,128)(2,1)S(1)}, bf16[512,128]{1,0:T(8,128)(2,1)S(1)}, u32[]{:S(2)}, u32[]{:S(2)}) collective-permute-start(bf16[512,128]{1,0:T(8,128)(2,1)S(1)} %collective-permute-done.9.rest_0_), channel_id=1, source_target_pairs={{0,4},{1,3},{4,8},{5,1},{8,12},{9,5},{12,14},{13,9},{14,10},{15,13... | collective-permute-start | bytes 393224 | tf_op jit(solution)/shard_map/ppermute | solution.py:317
  49.6 2.8 %collective-permute-start.21 = (f32[256,256]{1,0:T(8,128)S(1)}, f32[256,256]{1,0:T(8,128)S(1)}, u32[]{:S(2)}, u32[]{:S(2)}) collective-permute-start(f32[256,256]{1,0:T(8,128)S(1)} %get-tuple-element.27), channel_id=1, source_target_pairs={{0,1},{1,0},{2,3},{3,2},{4,5},{5,4},{6,7},{7,6},{8,9},{9,8},{10,11... | collective-permute-start | bytes 786440 | tf_op jit(solution)/shard_map/ppermute | solution.py:334
  49.7 2.7 %collective-permute-start.22 = (f32[256,256]{1,0:T(8,128)S(1)}, f32[256,256]{1,0:T(8,128)S(1)}, u32[]{:S(2)}, u32[]{:S(2)}) collective-permute-start(f32[256,256]{1,0:T(8,128)S(1)} %get-tuple-element.28), channel_id=1, source_target_pairs={{0,1},{1,0},{2,3},{3,2},{4,5},{5,4},{6,7},{7,6},{8,9},{9,8},{10,11... | collective-permute-start | bytes 786440 | tf_op jit(solution)/shard_map/ppermute | solution.py:334
  50.2 1.6 %collective-permute-start.26 = (bf16[512,128]{1,0:T(8,128)(2,1)S(1)}, bf16[512,128]{1,0:T(8,128)(2,1)S(1)}, u32[]{:S(2)}, u32[]{:S(2)}) collective-permute-start(bf16[512,128]{1,0:T(8,128)(2,1)S(1)} %collective-permute-done.24.rest_1_), channel_id=1, source_target_pairs={{0,1},{1,0},{2,3},{3,2},{4,5},{5,4},{6,7},{7,6},{8,9},{9,8},{10,11... | collective-permute-start | bytes 393224 | tf_op jit(solution)/shard_map/ppermute | solution.py:335
  51.1 1.3 %collective-permute-start.25 = (bf16[512,128]{1,0:T(8,128)(2,1)S(1)}, bf16[512,128]{1,0:T(8,128)(2,1)S(1)}, u32[]{:S(2)}, u32[]{:S(2)}) collective-permute-start(bf16[512,128]{1,0:T(8,128)(2,1)S(1)} %collective-permute-done.23.rest_0_), channel_id=1, source_target_pairs={{0,1},{1,0},{2,3},{3,2},{4,5},{5,4},{6,7},{7,6},{8,9},{9,8},{10,11... | collective-permute-start | bytes 393224 | tf_op jit(solution)/shard_map/ppermute | solution.py:335

commit v6 on v5

--- a/solution.py
+++ b/solution.py
@@ -195,20 +195,21 @@
 
 
 def early_kernel(places, planes, spots, has_total, last, mine_ref, other_ref, *rest):
-    blocks, rest = rest[: len(spots)], rest[len(spots) :]
+    blocks, rest = rest[: 2 * len(spots)], rest[2 * len(spots) :]
     if has_total:
         total_ref, *rest = rest
     *outs, acc = rest if last else [*rest, rest[0]]
     core = lax.rem(lax.axis_index("store"), 2)
     depth = mine_ref.shape[1] // planes
     acc[...] = total_ref[...] if has_total else jnp.zeros_like(acc)
-    for block, (step, segments) in zip(blocks, spots):
+    for i, (step, first) in enumerate(spots):
         chip, plane = block_at(step, places, planes)
-        for mate, first, row, size in segments:
-            columns = pl.ds(pl.multiple_of(plane * depth + first, LANES), size)
-            index = 2 * chip + (1 - core if mate else core)
-            for n, ref in enumerate((mine_ref, other_ref) if step else (mine_ref,)):
-                acc[index, n] += jnp.dot(ref[:, columns], block[pl.ds(row, size), :], preferred_element_type=F32)
+        both = jnp.concatenate([blocks[2 * i][...], blocks[2 * i + 1][...]], axis=1)
+        columns = pl.ds(pl.multiple_of(plane * depth + first, LANES), both.shape[0])
+        for n, ref in enumerate((mine_ref, other_ref) if step else (mine_ref,)):
+            part = jnp.dot(ref[:, columns], both, preferred_element_type=F32)
+            acc[2 * chip + core, n] += part[:, :EX_DEV]
+            acc[2 * chip + 1 - core, n] += part[:, EX_DEV:]
     if last:
         keep_ref, *sends = outs
         for index in range(acc.shape[0]):
@@ -234,22 +235,37 @@
 
 
 def final_kernel(places, planes, spots, stored_ref, keep_ref, got_ref, more_ref, *rest):
-    blocks, out_ref = rest[:-1], rest[-1]
+    blocks, (out_hbm, stage, sems) = rest[:-3], rest[-3:]
     core = lax.rem(lax.axis_index("store"), 2)
-    depth = stored_ref.shape[1] // planes
-    chip, plane = block_at(places // 2, places, planes)
-    half = got_ref.shape[0]
-    out_ref[pl.ds(0, half), :] = keep_ref[pl.ds(0, half), :] + got_ref[...]
-    out_ref[pl.ds(half, half), :] = keep_ref[pl.ds(half, half), :] + more_ref[...]
+    depth, half, chips = stored_ref.shape[1] // planes, got_ref.shape[0], places // planes
+    far, plane = block_at(places // 2, places, planes)
+
+    stage[pl.ds(0, half), :] = keep_ref[pl.ds(0, half), :] + got_ref[...]
+    stage[pl.ds(half, half), :] = keep_ref[pl.ds(half, half), :] + more_ref[...]
+    copies = []
+
+    def send(index, count):
+        at = pl.ds(pl.multiple_of(index * EX_DEV, EX_DEV), count * EX_DEV)
+        copies.append(pltpu.make_async_copy(stage.at[at], out_hbm.at[at], sems.at[len(copies)]))
+        copies[-1].start()
+
+    for i in range(1, chips):
+        send(2 * lax.rem(far + i, chips), 2)
+    part, count = None, len(blocks) // 2
+    for n in range(count):
+        first = spots[n][1]
+        columns = pl.ds(pl.multiple_of(plane * depth + first, LANES), blocks[n].shape[0])
+        both = jnp.concatenate([blocks[n][...], blocks[count + n][...]], axis=1)
+        more = jnp.dot(stored_ref[:, columns], both, preferred_element_type=F32)
+        part = more if part is None else part + more
+    part = part.T
     for mate in range(2):
-        part = None
-        for block, (m, first) in zip(blocks, spots):
-            if m == mate:
-                columns = pl.ds(pl.multiple_of(plane * depth + first, LANES), block.shape[0])
-                more = jnp.dot(stored_ref[:, columns], block[...], preferred_element_type=F32)
-                part = more if part is None else part + more
-        index = 2 * chip + (1 - core if mate else core)
-        out_ref[pl.ds(pl.multiple_of(index * EX_DEV, EX_DEV), EX_DEV), :] += part.T
+        index = 2 * far + (1 - core if mate else core)
+        at = pl.ds(pl.multiple_of(index * EX_DEV, EX_DEV), EX_DEV)
+        stage[at, :] += part[mate * EX_DEV : (mate + 1) * EX_DEV]
+        send(index, 1)
+    for copy in copies:
+        copy.wait()
 
 
 def final_scores(stored, keep, got, blocks, spots, places, planes):
@@ -257,8 +273,9 @@
     return pl.pallas_call(
         functools.partial(final_kernel, places, planes, spots),
         in_specs=[vmem] * (4 + len(blocks)),
-        out_specs=vmem,
-        out_shape=jax.ShapeDtypeStruct(keep.shape, F32),
+        out_specs=pl.BlockSpec(memory_space=pltpu.HBM),
+        out_shape=pltpu.HBM(keep.shape, F32),
+        scratch_shapes=[pltpu.VMEM(keep.shape, F32), pltpu.SemaphoreType.DMA((places // planes + 1,))],
         compiler_params=pltpu.CompilerParams(vmem_limit_bytes=20 * MIB),
         name="final_scores",
     )(stored, keep, *got, *blocks)
@@ -318,9 +335,7 @@
     mates = [lax.ppermute(x, "store", swap) for x in query]
     half = query[0].shape[0]
     streams = [query[0], mates[0], query[1], mates[1]]
-    marks = [((mate, i * half, 0, half),) for i in range(2) for mate in range(2)]
-    early = query + mates
-    spots = [(0, ((mate, i * half, 0, half),)) for mate in range(2) for i in range(2)]
+    early, spots = list(streams), [(0, 0), (0, half)]
     total = None
     for step in range(1, places // 2):
         if step == places // 2 - 1:
@@ -328,7 +343,7 @@
             early, spots = [], []
         streams = [on(x) for x in streams]
         early += streams
-        spots += [(step, mark) for mark in marks]
+        spots += [(step, 0), (step, half)]
     far = [on(x) for x in streams[::2]]
     keep, *send = early_scores(stored, others, early, spots, total, True, places, planes)
     got = [lax.ppermute(x, "store", swap) for x in send]

time: 53.9 us -> 53.7 us (level)
  Pallas kernels: 18.1 us -> 17 us
  waiting for transfers between devices: 4.37 us -> 5.32 us
    ppermute x14, waiting for transfers between devices: 1.14 us -> 2.08 us  [body(): lax.ppermute(x, ('width', 'store'), ring_pairs(planes, stores))]
    pallas_call x2, Pallas kernels: 2.73 us -> 1.8 us  [early_scores(): pl.pallas_call(functools.partial(early_kernel, places, planes, spots, boo...]
  transfers between devices with their start and end apart: 27 -> 27, of which waited for: 8 -> 9; matrix products, arithmetic and copies ran while one was open for 0% -> 0% of each run, Pallas kernels for 24% -> 22%
where the time goes in v6:
time: 53.7 us; the launch traced here: 53.5 us
  starting transfers between devices  31.1 us (58%)
  Pallas kernels  17 us (32%)
  waiting for transfers between devices  5.32 us (10%)
    ppermute x14, starting transfers between devices, body(): lax.ppermute(x, ('width', 'store'), ring_pairs(planes, stores))  18.8 us
    ppermute x6, starting transfers between devices, turn(): lax.ppermute(x, 'width', [(i, (i + d) % planes) for i in range(planes)])  11.1 us
    pallas_call x2, Pallas kernels, project(): pl.pallas_call(functools.partial(project_kernel, planes, turns), in_specs...  6.32 us
    pallas_call x1, Pallas kernels, load(): pl.pallas_call(load_kernel, in_specs=[vmem, pl.BlockSpec(memory_space=plt...  3.61 us
    pallas_call x1, Pallas kernels, query_transposed(): pl.pallas_call(functools.partial(query_kernel, len(factors)), in_specs=[p...  2.89 us
    ppermute x14, waiting for transfers between devices, body(): lax.ppermute(x, ('width', 'store'), ring_pairs(planes, stores))  2.08 us
    ppermute x6, waiting for transfers between devices, turn(): lax.ppermute(x, 'width', [(i, (i + d) % planes) for i in range(planes)])  1.88 us
    pallas_call x2, Pallas kernels, early_scores(): pl.pallas_call(functools.partial(early_kernel, places, planes, spots, boo...  1.8 us
  transfers between devices with their start and end apart: 27, of which 9 were waited for; matrix products, arithmetic and copies ran while one was open for 0% of the time, Pallas kernels for 22%

profile of v6, /device:TPU:0, one launch (start us, length us, event | category | flops | bytes accessed | tf_op | source)
XLA Modules:
  0.0 53.5 jit_solution(18024246115683151905)
XLA Ops:
  0.0 3.9 %project.3 = (bf16[256,128]{1,0:T(8,128)(2,1)S(1)}, bf16[256,128]{1,0:T(8,128)(2,1)S(1)}, bf16[256,128]{1,0:T(8,128)(2,1)S(1)}) custom-call(bf16[1024,2048]{1,0:T(8,128)(2,1)} %act_hbm.3, bf16[1024,2048]{1,0:T(8,128)(2,1)} %grad_hbm.3, bf16[64,2048]{1,0:T(8,128)(2,1)} %bitcast.5, bf16[64,2048]{1,0:T(8,128)(2,1)} %bitcast.7), custom_call_target="tpu_custom_call" | custom-call | flops 402653184 | bytes 12582912 | tf_op jit(solution)/shard_map/project/pallas_call | solution.py:59
  3.9 3.1 %collective-permute-start = (bf16[256,128]{1,0:T(8,128)(2,1)S(1)}, bf16[256,128]{1,0:T(8,128)(2,1)S(1)}, u32[]{:S(2)}, u32[]{:S(2)}) collective-permute-start(bf16[256,128]{1,0:T(8,128)(2,1)S(1)} %get-tuple-element.17), channel_id=1, source_target_pairs={{0,4},{4,8},{8,12},{12,0},{1,5},{5,9},{9,13},{13,1},{2,6},{6,10},{... | collective-permute-start | bytes 196616 | tf_op jit(solution)/shard_map/ppermute | solution.py:295
  7.0 2.6 %collective-permute-start.1 = (bf16[256,128]{1,0:T(8,128)(2,1)S(1)}, bf16[256,128]{1,0:T(8,128)(2,1)S(1)}, u32[]{:S(2)}, u32[]{:S(2)}) collective-permute-start(bf16[256,128]{1,0:T(8,128)(2,1)S(1)} %get-tuple-element.18), channel_id=1, source_target_pairs={{0,8},{4,12},{8,0},{12,4},{1,9},{5,13},{9,1},{13,5},{2,10},{6,14},... | collective-permute-start | bytes 196616 | tf_op jit(solution)/shard_map/ppermute | solution.py:295
  9.6 1.3 %collective-permute-start.2 = (bf16[256,128]{1,0:T(8,128)(2,1)S(1)}, bf16[256,128]{1,0:T(8,128)(2,1)S(1)}, u32[]{:S(2)}, u32[]{:S(2)}) collective-permute-start(bf16[256,128]{1,0:T(8,128)(2,1)S(1)} %get-tuple-element.19), channel_id=1, source_target_pairs={{0,12},{4,0},{8,4},{12,8},{1,13},{5,1},{9,5},{13,9},{2,14},{6,2},{... | collective-permute-start | bytes 196616 | tf_op jit(solution)/shard_map/ppermute | solution.py:295
  10.9 2.4 %project.2 = f32[256,128]{1,0:T(8,128)S(1)} custom-call(bf16[1024,2048]{1,0:T(8,128)(2,1)} %act_hbm.3, bf16[1024,2048]{1,0:T(8,128)(2,1)} %grad_hbm.3, bf16[64,2048]{1,0:T(8,128)(2,1)} %bitcast.6, bf16[64,2048]{1,0:T(8,128)(2,1)} %bitcast.8), custom_call_target="tpu_custom_call" | custom-call | flops 134217728 | bytes 4194304 | tf_op jit(solution)/shard_map/project/pallas_call | solution.py:59
  13.4 0.7 %collective-permute-done.1 = bf16[256,128]{1,0:T(8,128)(2,1)S(1)} collective-permute-done((bf16[256,128]{1,0:T(8,128)(2,1)S(1)}, bf16[256,128]{1,0:T(8,128)(2,1)S(1)}, u32[]{:S(2)}, u32[]{:S(2)}) %collective-permute-start.1) | collective-permute-done | bytes 65568 | tf_op jit(solution)/shard_map/ppermute | solution.py:295
  14.0 0.2 collective-permute-done.2
  14.3 1.6 %collective-permute-start.4 = (bf16[256,128]{1,0:T(8,128)(2,1)S(1)}, bf16[256,128]{1,0:T(8,128)(2,1)S(1)}, u32[]{:S(2)}, u32[]{:S(2)}) collective-permute-start(bf16[256,128]{1,0:T(8,128)(2,1)S(1)} %add_convert_fusion.rest_0_), channel_id=1, source_target_pairs={{0,4},{4,8},{8,12},{12,0},{1,5},{5,9},{9,13},{13,1},{2,6},{6,10},{... | collective-permute-start | bytes 196616 | tf_op jit(solution)/shard_map/ppermute | solution.py:295
  16.0 2.0 %collective-permute-start.5 = (bf16[256,128]{1,0:T(8,128)(2,1)S(1)}, bf16[256,128]{1,0:T(8,128)(2,1)S(1)}, u32[]{:S(2)}, u32[]{:S(2)}) collective-permute-start(bf16[256,128]{1,0:T(8,128)(2,1)S(1)} %add_convert_fusion.rest_0_), channel_id=1, source_target_pairs={{0,8},{4,12},{8,0},{12,4},{1,9},{5,13},{9,1},{13,5},{2,10},{6,14},... | collective-permute-start | bytes 196616 | tf_op jit(solution)/shard_map/ppermute | solution.py:295
  18.0 0.4 collective-permute-start.6
  18.4 0.0 collective-permute-start.3
  18.4 3.6 %load.1 = (bf16[1024,4096]{1,0:T(8,128)(2,1)S(1)}, s32[16]{0:T(128)S(4)}) custom-call(s32[8,128]{1,0:T(8,128)S(1)} %bitcast.3, bf16[1024,4096]{1,0:T(8,128)(2,1)} %hbm_ref), custom_call_target="tpu_custom_call" | custom-call | bytes 33554432 | tf_op jit(solution)/shard_map/load/pallas_call | solution.py:94
  22.0 0.0 collective-permute-done.4.rest_1_
  22.0 0.6 %collective-permute-done.5.rest_2_ = bf16[256,128]{1,0:T(8,128)(2,1)S(1)} collective-permute-done((bf16[256,128]{1,0:T(8,128)(2,1)S(1)}, bf16[256,128]{1,0:T(8,128)(2,1)S(1)}, u32[]{:S(2)}, u32[]{:S(2)}) %collective-permute-start.5) | collective-permute-done | bytes 65568 | tf_op jit(solution)/shard_map/ppermute | solution.py:295
  22.6 0.4 collective-permute-done.6.rest_3_
  23.0 2.9 %query.1 = (bf16[512,128]{1,0:T(8,128)(2,1)S(1)}, bf16[128,4096]{1,0:T(8,128)(2,1)S(1)}) custom-call(s32[16]{0:T(128)S(4)} %get-tuple-element.22.start_ref, s32[8,128]{1,0:T(8,128)S(1)} %bitcast.4, bf16[256,128]{1,0:T(8,128)(2,1)S(1)} %add_convert_fusion.rest_0_, bf16[256,128]{1,0:T(8,128)(2,1)S(1)} %collective-permute-done.4.rest_1_, ...), custom_call_target="tpu_custom_call" | custom-call | tf_op jit(solution)/shard_map/query/pallas_call | solution.py:161
  25.9 1.2 %curve.1.rest_2_ = bf16[512,128]{1,0:T(8,128)(2,1)S(1)} custom-call(bf16[128,4096]{1,0:T(8,128)(2,1)S(1)} %get-tuple-element.25.pe_ref, bf16[1024,4096]{1,0:T(8,128)(2,1)S(1)} %get-tuple-element.23.rest_4_.ic_ref), custom_call_target="tpu_custom_call" | custom-call | flops 26843545600 | bytes 4194304 | tf_op jit(solution)/shard_map/curve/pallas_call | solution.py:175
  27.1 0.1 collective-permute-start.17
  27.2 0.5 collective-permute-start.10
  27.7 1.5 %collective-permute-start.14 = (bf16[512,128]{1,0:T(8,128)(2,1)S(1)}, bf16[512,128]{1,0:T(8,128)(2,1)S(1)}, u32[]{:S(2)}, u32[]{:S(2)}) collective-permute-start(bf16[512,128]{1,0:T(8,128)(2,1)S(1)} %curve.1.rest_2_), channel_id=1, source_target_pairs={{0,4},{1,3},{4,8},{5,1},{8,12},{9,5},{12,14},{13,9},{14,10},{15,13... | collective-permute-start | bytes 393224 | tf_op jit(solution)/shard_map/ppermute | solution.py:334
  29.2 0.0 collective-permute-start.7
  29.3 1.9 %collective-permute-start.18 = (bf16[512,128]{1,0:T(8,128)(2,1)S(1)}, bf16[512,128]{1,0:T(8,128)(2,1)S(1)}, u32[]{:S(2)}, u32[]{:S(2)}) collective-permute-start(bf16[512,128]{1,0:T(8,128)(2,1)S(1)} %collective-permute-done.17.rest_3_), channel_id=1, source_target_pairs={{0,4},{1,3},{4,8},{5,1},{8,12},{9,5},{12,14},{13,9},{14,10},{15,13... | collective-permute-start | bytes 393224 | tf_op jit(solution)/shard_map/ppermute | solution.py:334
  31.1 0.0 collective-permute-done.10.rest_1_
  31.1 1.2 %collective-permute-start.11 = (bf16[512,128]{1,0:T(8,128)(2,1)S(1)}, bf16[512,128]{1,0:T(8,128)(2,1)S(1)}, u32[]{:S(2)}, u32[]{:S(2)}) collective-permute-start(bf16[512,128]{1,0:T(8,128)(2,1)S(1)} %collective-permute-done.10.rest_1_), channel_id=1, source_target_pairs={{0,4},{1,3},{4,8},{5,1},{8,12},{9,5},{12,14},{13,9},{14,10},{15,13... | collective-permute-start | bytes 393224 | tf_op jit(solution)/shard_map/ppermute | solution.py:334
  32.4 0.3 collective-permute-done.14.rest_6_
  32.7 1.5 %collective-permute-start.15 = (bf16[512,128]{1,0:T(8,128)(2,1)S(1)}, bf16[512,128]{1,0:T(8,128)(2,1)S(1)}, u32[]{:S(2)}, u32[]{:S(2)}) collective-permute-start(bf16[512,128]{1,0:T(8,128)(2,1)S(1)} %collective-permute-done.14.rest_6_), channel_id=1, source_target_pairs={{0,4},{1,3},{4,8},{5,1},{8,12},{9,5},{12,14},{13,9},{14,10},{15,13... | collective-permute-start | bytes 393224 | tf_op jit(solution)/shard_map/ppermute | solution.py:334
  34.2 0.0 collective-permute-done.7.rest_4_
  34.2 1.4 %collective-permute-start.8 = (bf16[512,128]{1,0:T(8,128)(2,1)S(1)}, bf16[512,128]{1,0:T(8,128)(2,1)S(1)}, u32[]{:S(2)}, u32[]{:S(2)}) collective-permute-start(bf16[512,128]{1,0:T(8,128)(2,1)S(1)} %collective-permute-done.7.rest_4_), channel_id=1, source_target_pairs={{0,4},{1,3},{4,8},{5,1},{8,12},{9,5},{12,14},{13,9},{14,10},{15,13... | collective-permute-start | bytes 393224 | tf_op jit(solution)/shard_map/ppermute | solution.py:334
  35.6 0.0 collective-permute-done.18.rest_7_
  35.6 1.4 %collective-permute-start.19 = (bf16[512,128]{1,0:T(8,128)(2,1)S(1)}, bf16[512,128]{1,0:T(8,128)(2,1)S(1)}, u32[]{:S(2)}, u32[]{:S(2)}) collective-permute-start(bf16[512,128]{1,0:T(8,128)(2,1)S(1)} %collective-permute-done.18.rest_7_), channel_id=1, source_target_pairs={{0,4},{1,3},{4,8},{5,1},{8,12},{9,5},{12,14},{13,9},{14,10},{15,13... | collective-permute-start | bytes 393224 | tf_op jit(solution)/shard_map/ppermute | solution.py:334
  37.0 1.4 %collective-permute-start.12 = (bf16[512,128]{1,0:T(8,128)(2,1)S(1)}, bf16[512,128]{1,0:T(8,128)(2,1)S(1)}, u32[]{:S(2)}, u32[]{:S(2)}) collective-permute-start(bf16[512,128]{1,0:T(8,128)(2,1)S(1)} %collective-permute-done.11.rest_5_), channel_id=1, source_target_pairs={{0,4},{1,3},{4,8},{5,1},{8,12},{9,5},{12,14},{13,9},{14,10},{15,13... | collective-permute-start | bytes 393224 | tf_op jit(solution)/shard_map/ppermute | solution.py:334
  38.4 0.0 collective-permute-done.15.rest_10_
  38.4 1.4 %collective-permute-start.16 = (bf16[512,128]{1,0:T(8,128)(2,1)S(1)}, bf16[512,128]{1,0:T(8,128)(2,1)S(1)}, u32[]{:S(2)}, u32[]{:S(2)}) collective-permute-start(bf16[512,128]{1,0:T(8,128)(2,1)S(1)} %collective-permute-done.15.rest_10_), channel_id=1, source_target_pairs={{0,4},{1,3},{4,8},{5,1},{8,12},{9,5},{12,14},{13,9},{14,10},{15,13... | collective-permute-start | bytes 393224 | tf_op jit(solution)/shard_map/ppermute | solution.py:334
  39.8 1.4 %collective-permute-start.9 = (bf16[512,128]{1,0:T(8,128)(2,1)S(1)}, bf16[512,128]{1,0:T(8,128)(2,1)S(1)}, u32[]{:S(2)}, u32[]{:S(2)}) collective-permute-start(bf16[512,128]{1,0:T(8,128)(2,1)S(1)} %collective-permute-done.8.rest_8_), channel_id=1, source_target_pairs={{0,4},{1,3},{4,8},{5,1},{8,12},{9,5},{12,14},{13,9},{14,10},{15,13... | collective-permute-start | bytes 393224 | tf_op jit(solution)/shard_map/ppermute | solution.py:334
  41.2 1.4 %collective-permute-start.20 = (bf16[512,128]{1,0:T(8,128)(2,1)S(1)}, bf16[512,128]{1,0:T(8,128)(2,1)S(1)}, u32[]{:S(2)}, u32[]{:S(2)}) collective-permute-start(bf16[512,128]{1,0:T(8,128)(2,1)S(1)} %collective-permute-done.19.rest_11_), channel_id=1, source_target_pairs={{0,4},{1,3},{4,8},{5,1},{8,12},{9,5},{12,14},{13,9},{14,10},{15,13... | collective-permute-start | bytes 393224 | tf_op jit(solution)/shard_map/ppermute | solution.py:334
  42.6 1.4 %collective-permute-start.13 = (bf16[512,128]{1,0:T(8,128)(2,1)S(1)}, bf16[512,128]{1,0:T(8,128)(2,1)S(1)}, u32[]{:S(2)}, u32[]{:S(2)}) collective-permute-start(bf16[512,128]{1,0:T(8,128)(2,1)S(1)} %collective-permute-done.12.rest_9_), channel_id=1, source_target_pairs={{0,4},{1,3},{4,8},{5,1},{8,12},{9,5},{12,14},{13,9},{14,10},{15,13... | collective-permute-start | bytes 393224 | tf_op jit(solution)/shard_map/ppermute | solution.py:334
  44.0 1.4 %collective-permute-start.24 = (bf16[512,128]{1,0:T(8,128)(2,1)S(1)}, bf16[512,128]{1,0:T(8,128)(2,1)S(1)}, u32[]{:S(2)}, u32[]{:S(2)}) collective-permute-start(bf16[512,128]{1,0:T(8,128)(2,1)S(1)} %collective-permute-done.16.rest_2_), channel_id=1, source_target_pairs={{0,4},{1,3},{4,8},{5,1},{8,12},{9,5},{12,14},{13,9},{14,10},{15,13... | collective-permute-start | bytes 393224 | tf_op jit(solution)/shard_map/ppermute | solution.py:334
  45.4 1.4 %collective-permute-start.23 = (bf16[512,128]{1,0:T(8,128)(2,1)S(1)}, bf16[512,128]{1,0:T(8,128)(2,1)S(1)}, u32[]{:S(2)}, u32[]{:S(2)}) collective-permute-start(bf16[512,128]{1,0:T(8,128)(2,1)S(1)} %collective-permute-done.9.rest_0_), channel_id=1, source_target_pairs={{0,4},{1,3},{4,8},{5,1},{8,12},{9,5},{12,14},{13,9},{14,10},{15,13... | collective-permute-start | bytes 393224 | tf_op jit(solution)/shard_map/ppermute | solution.py:334
  46.8 1.0 %early_scores.2.rest_4_ = f32[4,2,256,128]{3,2,1,0:T(8,128)S(1)} custom-call(bf16[256,4096]{1,0:T(8,128)(2,1)S(1)} %copy-done, bf16[256,4096]{1,0:T(8,128)(2,1)S(1)} %collective-permute-done.3.other_ref, bf16[512,128]{1,0:T(8,128)(2,1)S(1)} %get-tuple-element.24.rest_0_, bf16[512,128]{1,0:T(8,128)(2,1)S(1)} %collective-permute-done.10.rest_1_, ...), custom_call_target="tpu_custom_call" | custom-call | tf_op jit(solution)/shard_map/early_scores/pallas_call | solution.py:226
  47.8 0.4 collective-permute-done.13.rest_1_
  48.3 0.8 %early_scores.3 = (f32[512,256]{1,0:T(8,128)S(1)}, f32[256,256]{1,0:T(8,128)S(1)}, f32[256,256]{1,0:T(8,128)S(1)}) custom-call(bf16[256,4096]{1,0:T(8,128)(2,1)S(1)} %copy-done, bf16[256,4096]{1,0:T(8,128)(2,1)S(1)} %collective-permute-done.3.other_ref, bf16[512,128]{1,0:T(8,128)(2,1)S(1)} %collective-permute-done.9.rest_0_, ...), custom_call_target="tpu_custom_call" | custom-call | tf_op jit(solution)/shard_map/early_scores/pallas_call | solution.py:226
  49.1 0.1 collective-permute-start.21
  49.2 0.5 collective-permute-start.22
  49.7 0.1 collective-permute-start.26
  49.7 1.3 %collective-permute-done.23.rest_0_ = bf16[512,128]{1,0:T(8,128)(2,1)S(1)} collective-permute-done((bf16[512,128]{1,0:T(8,128)(2,1)S(1)}, bf16[512,128]{1,0:T(8,128)(2,1)S(1)}, u32[]{:S(2)}, u32[]{:S(2)}) %collective-permute-start.23) | collective-permute-done | bytes 131104 | tf_op jit(solution)/shard_map/ppermute | solution.py:334
  51.1 0.2 collective-permute-done.26.rest_3_
  51.2 1.2 %collective-permute-done.25.rest_2_ = bf16[512,128]{1,0:T(8,128)(2,1)S(1)} collective-permute-done((bf16[512,128]{1,0:T(8,128)(2,1)S(1)}, bf16[512,128]{1,0:T(8,128)(2,1)S(1)}, u32[]{:S(2)}, u32[]{:S(2)}) %collective-permute-start.25) | collective-permute-done | bytes 131104 | tf_op jit(solution)/shard_map/ppermute | solution.py:350
  52.4 1.1 %final_scores.1 = f32[512,256]{1,0:T(8,128)} custom-call(bf16[256,4096]{1,0:T(8,128)(2,1)S(1)} %copy-done, f32[512,256]{1,0:T(8,128)S(1)} %get-tuple-element.26.keep_ref, f32[256,256]{1,0:T(8,128)S(1)} %collective-permute-done.21.got_ref, f32[256,256]{1,0:T(8,128)S(1)} %collective-permute-done.22.more_ref, ...), custom_call_target="tpu_custom_call" | custom-call | tf_op jit(solution)/shard_map/final_scores/pallas_call | solution.py:273
  (19 shorter events, 0.1 us)
Async XLA Ops:
  3.9 9.5 %collective-permute-start = (bf16[256,128]{1,0:T(8,128)(2,1)S(1)}, bf16[256,128]{1,0:T(8,128)(2,1)S(1)}, u32[]{:S(2)}, u32[]{:S(2)}) collective-permute-start(bf16[256,128]{1,0:T(8,128)(2,1)S(1)} %get-tuple-element.17), channel_id=1, source_target_pairs={{0,4},{4,8},{8,12},{12,0},{1,5},{5,9},{9,13},{13,1},{2,6},{6,10},{... | collective-permute-start | bytes 196616 | tf_op jit(solution)/shard_map/ppermute | solution.py:295
  7.0 7.1 %collective-permute-start.1 = (bf16[256,128]{1,0:T(8,128)(2,1)S(1)}, bf16[256,128]{1,0:T(8,128)(2,1)S(1)}, u32[]{:S(2)}, u32[]{:S(2)}) collective-permute-start(bf16[256,128]{1,0:T(8,128)(2,1)S(1)} %get-tuple-element.18), channel_id=1, source_target_pairs={{0,8},{4,12},{8,0},{12,4},{1,9},{5,13},{9,1},{13,5},{2,10},{6,14},... | collective-permute-start | bytes 196616 | tf_op jit(solution)/shard_map/ppermute | solution.py:295
  9.6 8.8 %copy-start = (bf16[256,4096]{1,0:T(8,128)(2,1)S(1)}, bf16[256,4096]{1,0:T(8,128)(2,1)}, u32[]{:S(2)}) copy-start(bf16[256,4096]{1,0:T(8,128)(2,1)} %stored_ref) | copy-start | bytes 6291460
  9.6 8.8 %copy-start.1 = (s32[1,1024]{1,0:T(1,128)S(1)}, s32[1,1024]{1,0:T(1,128)}, u32[]{:S(2)}) copy-start(s32[1,1024]{1,0:T(1,128)} %param.9) | copy-start | bytes 12292
  9.6 4.7 %collective-permute-start.2 = (bf16[256,128]{1,0:T(8,128)(2,1)S(1)}, bf16[256,128]{1,0:T(8,128)(2,1)S(1)}, u32[]{:S(2)}, u32[]{:S(2)}) collective-permute-start(bf16[256,128]{1,0:T(8,128)(2,1)S(1)} %get-tuple-element.19), channel_id=1, source_target_pairs={{0,12},{4,0},{8,4},{12,8},{1,13},{5,1},{9,5},{13,9},{2,14},{6,2},{... | collective-permute-start | bytes 196616 | tf_op jit(solution)/shard_map/ppermute | solution.py:295
  14.3 7.7 %collective-permute-start.4 = (bf16[256,128]{1,0:T(8,128)(2,1)S(1)}, bf16[256,128]{1,0:T(8,128)(2,1)S(1)}, u32[]{:S(2)}, u32[]{:S(2)}) collective-permute-start(bf16[256,128]{1,0:T(8,128)(2,1)S(1)} %add_convert_fusion.rest_0_), channel_id=1, source_target_pairs={{0,4},{4,8},{8,12},{12,0},{1,5},{5,9},{9,13},{13,1},{2,6},{6,10},{... | collective-permute-start | bytes 196616 | tf_op jit(solution)/shard_map/ppermute | solution.py:295
  16.0 6.7 %collective-permute-start.5 = (bf16[256,128]{1,0:T(8,128)(2,1)S(1)}, bf16[256,128]{1,0:T(8,128)(2,1)S(1)}, u32[]{:S(2)}, u32[]{:S(2)}) collective-permute-start(bf16[256,128]{1,0:T(8,128)(2,1)S(1)} %add_convert_fusion.rest_0_), channel_id=1, source_target_pairs={{0,8},{4,12},{8,0},{12,4},{1,9},{5,13},{9,1},{13,5},{2,10},{6,14},... | collective-permute-start | bytes 196616 | tf_op jit(solution)/shard_map/ppermute | solution.py:295
  18.0 5.0 %collective-permute-start.6 = (bf16[256,128]{1,0:T(8,128)(2,1)S(1)}, bf16[256,128]{1,0:T(8,128)(2,1)S(1)}, u32[]{:S(2)}, u32[]{:S(2)}) collective-permute-start(bf16[256,128]{1,0:T(8,128)(2,1)S(1)} %add_convert_fusion.rest_0_), channel_id=1, source_target_pairs={{0,12},{4,0},{8,4},{12,8},{1,13},{5,1},{9,5},{13,9},{2,14},{6,2},{... | collective-permute-start | bytes 196616 | tf_op jit(solution)/shard_map/ppermute | solution.py:295
  18.4 28.5 %collective-permute-start.3 = (bf16[256,4096]{1,0:T(8,128)(2,1)S(1)}, bf16[256,4096]{1,0:T(8,128)(2,1)S(1)}, u32[]{:S(2)}, u32[]{:S(2)}) collective-permute-start(bf16[256,4096]{1,0:T(8,128)(2,1)S(1)} %copy-done), channel_id=1, source_target_pairs={{0,1},{1,0},{2,3},{3,2},{4,5},{5,4},{6,7},{7,6},{8,9},{9,8},{10,11... | collective-permute-start | bytes 6291464 | tf_op jit(solution)/shard_map/ppermute | solution.py:331
  27.1 2.1 %collective-permute-start.17 = (bf16[512,128]{1,0:T(8,128)(2,1)S(1)}, bf16[512,128]{1,0:T(8,128)(2,1)S(1)}, u32[]{:S(2)}, u32[]{:S(2)}) collective-permute-start(bf16[512,128]{1,0:T(8,128)(2,1)S(1)} %curve.1.rest_2_), channel_id=1, source_target_pairs={{0,1},{1,0},{2,3},{3,2},{4,5},{5,4},{6,7},{7,6},{8,9},{9,8},{10,11... | collective-permute-start | bytes 393224 | tf_op jit(solution)/shard_map/ppermute | solution.py:335
  27.2 3.9 %collective-permute-start.10 = (bf16[512,128]{1,0:T(8,128)(2,1)S(1)}, bf16[512,128]{1,0:T(8,128)(2,1)S(1)}, u32[]{:S(2)}, u32[]{:S(2)}) collective-permute-start(bf16[512,128]{1,0:T(8,128)(2,1)S(1)} %get-tuple-element.24.rest_0_), channel_id=1, source_target_pairs={{0,1},{1,0},{2,3},{3,2},{4,5},{5,4},{6,7},{7,6},{8,9},{9,8},{10,11... | collective-permute-start | bytes 393224 | tf_op jit(solution)/shard_map/ppermute | solution.py:335
  27.7 5.0 %collective-permute-start.14 = (bf16[512,128]{1,0:T(8,128)(2,1)S(1)}, bf16[512,128]{1,0:T(8,128)(2,1)S(1)}, u32[]{:S(2)}, u32[]{:S(2)}) collective-permute-start(bf16[512,128]{1,0:T(8,128)(2,1)S(1)} %curve.1.rest_2_), channel_id=1, source_target_pairs={{0,4},{1,3},{4,8},{5,1},{8,12},{9,5},{12,14},{13,9},{14,10},{15,13... | collective-permute-start | bytes 393224 | tf_op jit(solution)/shard_map/ppermute | solution.py:334
  29.2 5.0 %collective-permute-start.7 = (bf16[512,128]{1,0:T(8,128)(2,1)S(1)}, bf16[512,128]{1,0:T(8,128)(2,1)S(1)}, u32[]{:S(2)}, u32[]{:S(2)}) collective-permute-start(bf16[512,128]{1,0:T(8,128)(2,1)S(1)} %get-tuple-element.24.rest_0_), channel_id=1, source_target_pairs={{0,4},{1,3},{4,8},{5,1},{8,12},{9,5},{12,14},{13,9},{14,10},{15,13... | collective-permute-start | bytes 393224 | tf_op jit(solution)/shard_map/ppermute | solution.py:334
  29.3 6.3 %collective-permute-start.18 = (bf16[512,128]{1,0:T(8,128)(2,1)S(1)}, bf16[512,128]{1,0:T(8,128)(2,1)S(1)}, u32[]{:S(2)}, u32[]{:S(2)}) collective-permute-start(bf16[512,128]{1,0:T(8,128)(2,1)S(1)} %collective-permute-done.17.rest_3_), channel_id=1, source_target_pairs={{0,4},{1,3},{4,8},{5,1},{8,12},{9,5},{12,14},{13,9},{14,10},{15,13... | collective-permute-start | bytes 393224 | tf_op jit(solution)/shard_map/ppermute | solution.py:334
  31.1 5.9 %collective-permute-start.11 = (bf16[512,128]{1,0:T(8,128)(2,1)S(1)}, bf16[512,128]{1,0:T(8,128)(2,1)S(1)}, u32[]{:S(2)}, u32[]{:S(2)}) collective-permute-start(bf16[512,128]{1,0:T(8,128)(2,1)S(1)} %collective-permute-done.10.rest_1_), channel_id=1, source_target_pairs={{0,4},{1,3},{4,8},{5,1},{8,12},{9,5},{12,14},{13,9},{14,10},{15,13... | collective-permute-start | bytes 393224 | tf_op jit(solution)/shard_map/ppermute | solution.py:334
  32.7 5.7 %collective-permute-start.15 = (bf16[512,128]{1,0:T(8,128)(2,1)S(1)}, bf16[512,128]{1,0:T(8,128)(2,1)S(1)}, u32[]{:S(2)}, u32[]{:S(2)}) collective-permute-start(bf16[512,128]{1,0:T(8,128)(2,1)S(1)} %collective-permute-done.14.rest_6_), channel_id=1, source_target_pairs={{0,4},{1,3},{4,8},{5,1},{8,12},{9,5},{12,14},{13,9},{14,10},{15,13... | collective-permute-start | bytes 393224 | tf_op jit(solution)/shard_map/ppermute | solution.py:334
  34.2 5.6 %collective-permute-start.8 = (bf16[512,128]{1,0:T(8,128)(2,1)S(1)}, bf16[512,128]{1,0:T(8,128)(2,1)S(1)}, u32[]{:S(2)}, u32[]{:S(2)}) collective-permute-start(bf16[512,128]{1,0:T(8,128)(2,1)S(1)} %collective-permute-done.7.rest_4_), channel_id=1, source_target_pairs={{0,4},{1,3},{4,8},{5,1},{8,12},{9,5},{12,14},{13,9},{14,10},{15,13... | collective-permute-start | bytes 393224 | tf_op jit(solution)/shard_map/ppermute | solution.py:334
  35.6 5.6 %collective-permute-start.19 = (bf16[512,128]{1,0:T(8,128)(2,1)S(1)}, bf16[512,128]{1,0:T(8,128)(2,1)S(1)}, u32[]{:S(2)}, u32[]{:S(2)}) collective-permute-start(bf16[512,128]{1,0:T(8,128)(2,1)S(1)} %collective-permute-done.18.rest_7_), channel_id=1, source_target_pairs={{0,4},{1,3},{4,8},{5,1},{8,12},{9,5},{12,14},{13,9},{14,10},{15,13... | collective-permute-start | bytes 393224 | tf_op jit(solution)/shard_map/ppermute | solution.py:334
  37.0 5.6 %collective-permute-start.12 = (bf16[512,128]{1,0:T(8,128)(2,1)S(1)}, bf16[512,128]{1,0:T(8,128)(2,1)S(1)}, u32[]{:S(2)}, u32[]{:S(2)}) collective-permute-start(bf16[512,128]{1,0:T(8,128)(2,1)S(1)} %collective-permute-done.11.rest_5_), channel_id=1, source_target_pairs={{0,4},{1,3},{4,8},{5,1},{8,12},{9,5},{12,14},{13,9},{14,10},{15,13... | collective-permute-start | bytes 393224 | tf_op jit(solution)/shard_map/ppermute | solution.py:334
  38.4 5.6 %collective-permute-start.16 = (bf16[512,128]{1,0:T(8,128)(2,1)S(1)}, bf16[512,128]{1,0:T(8,128)(2,1)S(1)}, u32[]{:S(2)}, u32[]{:S(2)}) collective-permute-start(bf16[512,128]{1,0:T(8,128)(2,1)S(1)} %collective-permute-done.15.rest_10_), channel_id=1, source_target_pairs={{0,4},{1,3},{4,8},{5,1},{8,12},{9,5},{12,14},{13,9},{14,10},{15,13... | collective-permute-start | bytes 393224 | tf_op jit(solution)/shard_map/ppermute | solution.py:334
  39.8 5.6 %collective-permute-start.9 = (bf16[512,128]{1,0:T(8,128)(2,1)S(1)}, bf16[512,128]{1,0:T(8,128)(2,1)S(1)}, u32[]{:S(2)}, u32[]{:S(2)}) collective-permute-start(bf16[512,128]{1,0:T(8,128)(2,1)S(1)} %collective-permute-done.8.rest_8_), channel_id=1, source_target_pairs={{0,4},{1,3},{4,8},{5,1},{8,12},{9,5},{12,14},{13,9},{14,10},{15,13... | collective-permute-start | bytes 393224 | tf_op jit(solution)/shard_map/ppermute | solution.py:334
  41.2 6.6 %collective-permute-start.20 = (bf16[512,128]{1,0:T(8,128)(2,1)S(1)}, bf16[512,128]{1,0:T(8,128)(2,1)S(1)}, u32[]{:S(2)}, u32[]{:S(2)}) collective-permute-start(bf16[512,128]{1,0:T(8,128)(2,1)S(1)} %collective-permute-done.19.rest_11_), channel_id=1, source_target_pairs={{0,4},{1,3},{4,8},{5,1},{8,12},{9,5},{12,14},{13,9},{14,10},{15,13... | collective-permute-start | bytes 393224 | tf_op jit(solution)/shard_map/ppermute | solution.py:334
  42.6 5.6 %collective-permute-start.13 = (bf16[512,128]{1,0:T(8,128)(2,1)S(1)}, bf16[512,128]{1,0:T(8,128)(2,1)S(1)}, u32[]{:S(2)}, u32[]{:S(2)}) collective-permute-start(bf16[512,128]{1,0:T(8,128)(2,1)S(1)} %collective-permute-done.12.rest_9_), channel_id=1, source_target_pairs={{0,4},{1,3},{4,8},{5,1},{8,12},{9,5},{12,14},{13,9},{14,10},{15,13... | collective-permute-start | bytes 393224 | tf_op jit(solution)/shard_map/ppermute | solution.py:334
  44.0 5.6 %collective-permute-start.24 = (bf16[512,128]{1,0:T(8,128)(2,1)S(1)}, bf16[512,128]{1,0:T(8,128)(2,1)S(1)}, u32[]{:S(2)}, u32[]{:S(2)}) collective-permute-start(bf16[512,128]{1,0:T(8,128)(2,1)S(1)} %collective-permute-done.16.rest_2_), channel_id=1, source_target_pairs={{0,4},{1,3},{4,8},{5,1},{8,12},{9,5},{12,14},{13,9},{14,10},{15,13... | collective-permute-start | bytes 393224 | tf_op jit(solution)/shard_map/ppermute | solution.py:334
  45.4 5.6 %collective-permute-start.23 = (bf16[512,128]{1,0:T(8,128)(2,1)S(1)}, bf16[512,128]{1,0:T(8,128)(2,1)S(1)}, u32[]{:S(2)}, u32[]{:S(2)}) collective-permute-start(bf16[512,128]{1,0:T(8,128)(2,1)S(1)} %collective-permute-done.9.rest_0_), channel_id=1, source_target_pairs={{0,4},{1,3},{4,8},{5,1},{8,12},{9,5},{12,14},{13,9},{14,10},{15,13... | collective-permute-start | bytes 393224 | tf_op jit(solution)/shard_map/ppermute | solution.py:334
  49.1 3.3 %collective-permute-start.21 = (f32[256,256]{1,0:T(8,128)S(1)}, f32[256,256]{1,0:T(8,128)S(1)}, u32[]{:S(2)}, u32[]{:S(2)}) collective-permute-start(f32[256,256]{1,0:T(8,128)S(1)} %get-tuple-element.27), channel_id=1, source_target_pairs={{0,1},{1,0},{2,3},{3,2},{4,5},{5,4},{6,7},{7,6},{8,9},{9,8},{10,11... | collective-permute-start | bytes 786440 | tf_op jit(solution)/shard_map/ppermute | solution.py:349
  49.2 3.2 %collective-permute-start.22 = (f32[256,256]{1,0:T(8,128)S(1)}, f32[256,256]{1,0:T(8,128)S(1)}, u32[]{:S(2)}, u32[]{:S(2)}) collective-permute-start(f32[256,256]{1,0:T(8,128)S(1)} %get-tuple-element.28), channel_id=1, source_target_pairs={{0,1},{1,0},{2,3},{3,2},{4,5},{5,4},{6,7},{7,6},{8,9},{9,8},{10,11... | collective-permute-start | bytes 786440 | tf_op jit(solution)/shard_map/ppermute | solution.py:349
  49.7 1.6 %collective-permute-start.26 = (bf16[512,128]{1,0:T(8,128)(2,1)S(1)}, bf16[512,128]{1,0:T(8,128)(2,1)S(1)}, u32[]{:S(2)}, u32[]{:S(2)}) collective-permute-start(bf16[512,128]{1,0:T(8,128)(2,1)S(1)} %collective-permute-done.24.rest_1_), channel_id=1, source_target_pairs={{0,1},{1,0},{2,3},{3,2},{4,5},{5,4},{6,7},{7,6},{8,9},{9,8},{10,11... | collective-permute-start | bytes 393224 | tf_op jit(solution)/shard_map/ppermute | solution.py:350
  51.1 1.3 %collective-permute-start.25 = (bf16[512,128]{1,0:T(8,128)(2,1)S(1)}, bf16[512,128]{1,0:T(8,128)(2,1)S(1)}, u32[]{:S(2)}, u32[]{:S(2)}) collective-permute-start(bf16[512,128]{1,0:T(8,128)(2,1)S(1)} %collective-permute-done.23.rest_0_), channel_id=1, source_target_pairs={{0,1},{1,0},{2,3},{3,2},{4,5},{5,4},{6,7},{7,6},{8,9},{9,8},{10,11... | collective-permute-start | bytes 393224 | tf_op jit(solution)/shard_map/ppermute | solution.py:350

commit v7 on v6

--- a/solution.py
+++ b/solution.py
@@ -79,23 +79,37 @@
     )(*(in_hbm(x) for x in operands))
 
 
-def load_kernel(ids_ref, hbm_ref, out_ref, start_ref, sem):
+def load_kernel(ids_ref, hbm_ref, out_ref, start_ref, pick_ref, double_ref, sem):
     copy = pltpu.make_async_copy(hbm_ref, out_ref, sem)
     copy.start()
     chunks = ids_ref.shape[0]
     for block in range(start_ref.shape[0]):
         before = jnp.sum((ids_ref[...] < block * EX_BLOCK).astype(jnp.int32))
         start_ref[block] = jnp.minimum(before // LANES, chunks - 2)
+    rank = double_ref.shape[0] // 2
+    entry = lax.broadcasted_iota(jnp.int32, (EX_BLOCK * rank, 2 * rank), 0) // EX_BLOCK + rank
+    column = lax.broadcasted_iota(jnp.int32, (EX_BLOCK * rank, 2 * rank), 1)
+    pick = (entry == column).astype(F32).astype(BF16)
+    source = lax.broadcasted_iota(jnp.int32, (2 * rank, 2 * rank), 0)
+    target = lax.broadcasted_iota(jnp.int32, (2 * rank, 2 * rank), 1) % rank
+    double = (source == target).astype(F32).astype(BF16)
+    pick_ref[...] = pick
+    double_ref[...] = double
     copy.wait()
 
 
-def load(ids, x):
+def load(ids, x, rank):
     vmem = pl.BlockSpec(memory_space=pltpu.VMEM)
     return pl.pallas_call(
         load_kernel,
         in_specs=[vmem, pl.BlockSpec(memory_space=pltpu.HBM)],
-        out_specs=[vmem, pl.BlockSpec(memory_space=pltpu.SMEM)],
-        out_shape=[pltpu.VMEM(x.shape, x.dtype), pltpu.SMEM((EX_DEV // EX_BLOCK,), jnp.int32)],
+        out_specs=[vmem, pl.BlockSpec(memory_space=pltpu.SMEM), vmem, vmem],
+        out_shape=[
+            pltpu.VMEM(x.shape, x.dtype),
+            pltpu.SMEM((EX_DEV // EX_BLOCK,), jnp.int32),
+            pltpu.VMEM((EX_BLOCK * rank, 2 * rank), BF16),
+            pltpu.VMEM((2 * rank, 2 * rank), BF16),
+        ],
         scratch_shapes=[pltpu.SemaphoreType.DMA],
         compiler_params=pltpu.CompilerParams(vmem_limit_bytes=20 * MIB),
         cost_estimate=pl.CostEstimate(flops=0, bytes_accessed=4 * x.size * x.dtype.itemsize, transcendentals=0),
@@ -103,7 +117,7 @@
     )(ids, in_hbm(x))
 
 
-def query_kernel(pieces, start_ref, ids_ref, *rest):
+def query_kernel(pieces, start_ref, pick_ref, double_ref, ids_ref, *rest):
     factor_refs, (ic_ref, out_ref, pe, tok, spread, twice) = rest[:pieces], rest[pieces:]
     tokens, rank = tok.shape[0], tok.shape[1] // 2
     piece = tokens // pieces
@@ -112,14 +126,8 @@
         at = lax.rem(me - d + pieces, pieces) if pieces > 1 else 0
         tok[pl.ds(pl.multiple_of(at * piece, piece), piece), :] = ref[...]
 
-    entry = lax.broadcasted_iota(jnp.int32, (EX_BLOCK * rank, 2 * rank), 0) // EX_BLOCK + rank
-    column = lax.broadcasted_iota(jnp.int32, (EX_BLOCK * rank, 2 * rank), 1)
-    pick = (entry == column).astype(F32).astype(BF16)
-    source = lax.broadcasted_iota(jnp.int32, (2 * rank, 2 * rank), 0)
-    target = lax.broadcasted_iota(jnp.int32, (2 * rank, 2 * rank), 1) % rank
-    double = (source == target).astype(F32).astype(BF16)
-    spread[...] = lax.dot_general(pick, tok[...], NT, preferred_element_type=F32).astype(BF16)
-    twice[...] = jnp.dot(tok[...], double, preferred_element_type=F32).astype(BF16)
+    spread[...] = lax.dot_general(pick_ref[...], tok[...], NT, preferred_element_type=F32).astype(BF16)
+    twice[...] = jnp.dot(tok[...], double_ref[...], preferred_element_type=F32).astype(BF16)
 
     slot = lax.broadcasted_iota(jnp.int32, (EX_BLOCK, 2 * LANES), 0)
     low = lax.broadcasted_iota(jnp.int32, (EX_BLOCK, 2 * rank), 1) < rank
@@ -160,7 +168,7 @@
     piece = pltpu.VMEM((feats // cuts, EX_DEV), BF16)
     first, grads = pl.pallas_call(
         functools.partial(query_kernel, len(factors)),
-        in_specs=[pl.BlockSpec(memory_space=pltpu.SMEM)] + [vmem] * (2 + len(factors)),
+        in_specs=[pl.BlockSpec(memory_space=pltpu.SMEM)] + [vmem] * (4 + len(factors)),
         out_specs=[vmem] * 2,
         out_shape=[piece, pltpu.VMEM((EX_DEV, width), BF16)],
         scratch_shapes=[
@@ -170,7 +178,7 @@
         ],
         compiler_params=pltpu.CompilerParams(vmem_limit_bytes=20 * MIB),
         name="query",
-    )(start, ids, *factors, inverse_curvature)
+    )(*start, ids, *factors, inverse_curvature)
     return [first] + [
         pl.pallas_call(
             functools.partial(curve_kernel, cut),
@@ -308,7 +316,7 @@
             axis=1,
         )
         factors = lax.psum(partial_value, "width").astype(BF16)
-        curvature, start = load(ids, inverse_curvature)
+        curvature, *start = load(ids, inverse_curvature, proj_in.shape[1])
         (query,) = query_transposed([factors], ids, start, curvature, 1)
         gathered = lax.all_gather(query, ("width", "store"), axis=0)
         blocks = gathered.reshape(planes, stores, query.shape[0], EX_DEV)
@@ -326,7 +334,7 @@
     own = own.astype(BF16)
     factors = [own] + [turn(own, d, planes) for d in range(1, planes)]
     _, inverse_curvature, stored = lax.optimization_barrier((own, inverse_curvature, stored))
-    curvature, start = load(ids, inverse_curvature)
+    curvature, *start = load(ids, inverse_curvature, proj_in.shape[1])
     swap = [(i, i ^ 1) for i in range(stores)]
     others = lax.ppermute(stored, "store", swap)
 

time: 53.7 us -> 53.7 us (level)
  no operation moved by 1% of the time
where the time goes in v7:
time: 53.7 us; the launch traced here: 53.5 us
  starting transfers between devices  31.1 us (58%)
  Pallas kernels  17 us (32%)
  waiting for transfers between devices  5.31 us (10%)
    ppermute x14, starting transfers between devices, body(): lax.ppermute(x, ('width', 'store'), ring_pairs(planes, stores))  18.8 us
    ppermute x6, starting transfers between devices, turn(): lax.ppermute(x, 'width', [(i, (i + d) % planes) for i in range(planes)])  11.1 us
    pallas_call x2, Pallas kernels, project(): pl.pallas_call(functools.partial(project_kernel, planes, turns), in_specs...  6.32 us
    pallas_call x1, Pallas kernels, load(): pl.pallas_call(load_kernel, in_specs=[vmem, pl.BlockSpec(memory_space=plt...  3.61 us
    pallas_call x1, Pallas kernels, query_transposed(): pl.pallas_call(functools.partial(query_kernel, len(factors)), in_specs=[p...  2.88 us
    ppermute x14, waiting for transfers between devices, body(): lax.ppermute(x, ('width', 'store'), ring_pairs(planes, stores))  2.08 us
    ppermute x6, waiting for transfers between devices, turn(): lax.ppermute(x, 'width', [(i, (i + d) % planes) for i in range(planes)])  1.88 us
    pallas_call x2, Pallas kernels, early_scores(): pl.pallas_call(functools.partial(early_kernel, places, planes, spots, boo...  1.8 us
  transfers between devices with their start and end apart: 27, of which 9 were waited for; matrix products, arithmetic and copies ran while one was open for 0% of the time, Pallas kernels for 22%

profile of v7, /device:TPU:0, one launch (start us, length us, event | category | flops | bytes accessed | tf_op | source)
XLA Modules:
  0.0 53.5 jit_solution(10161836020928307233)
XLA Ops:
  0.0 3.9 %project.3 = (bf16[256,128]{1,0:T(8,128)(2,1)S(1)}, bf16[256,128]{1,0:T(8,128)(2,1)S(1)}, bf16[256,128]{1,0:T(8,128)(2,1)S(1)}) custom-call(bf16[1024,2048]{1,0:T(8,128)(2,1)} %act_hbm.3, bf16[1024,2048]{1,0:T(8,128)(2,1)} %grad_hbm.3, bf16[64,2048]{1,0:T(8,128)(2,1)} %bitcast.5, bf16[64,2048]{1,0:T(8,128)(2,1)} %bitcast.7), custom_call_target="tpu_custom_call" | custom-call | flops 402653184 | bytes 12582912 | tf_op jit(solution)/shard_map/project/pallas_call | solution.py:59
  3.9 3.1 %collective-permute-start = (bf16[256,128]{1,0:T(8,128)(2,1)S(1)}, bf16[256,128]{1,0:T(8,128)(2,1)S(1)}, u32[]{:S(2)}, u32[]{:S(2)}) collective-permute-start(bf16[256,128]{1,0:T(8,128)(2,1)S(1)} %get-tuple-element.19), channel_id=1, source_target_pairs={{0,4},{4,8},{8,12},{12,0},{1,5},{5,9},{9,13},{13,1},{2,6},{6,10},{... | collective-permute-start | bytes 196616 | tf_op jit(solution)/shard_map/ppermute | solution.py:303
  7.0 2.6 %collective-permute-start.1 = (bf16[256,128]{1,0:T(8,128)(2,1)S(1)}, bf16[256,128]{1,0:T(8,128)(2,1)S(1)}, u32[]{:S(2)}, u32[]{:S(2)}) collective-permute-start(bf16[256,128]{1,0:T(8,128)(2,1)S(1)} %get-tuple-element.20), channel_id=1, source_target_pairs={{0,8},{4,12},{8,0},{12,4},{1,9},{5,13},{9,1},{13,5},{2,10},{6,14},... | collective-permute-start | bytes 196616 | tf_op jit(solution)/shard_map/ppermute | solution.py:303
  9.6 1.3 %collective-permute-start.2 = (bf16[256,128]{1,0:T(8,128)(2,1)S(1)}, bf16[256,128]{1,0:T(8,128)(2,1)S(1)}, u32[]{:S(2)}, u32[]{:S(2)}) collective-permute-start(bf16[256,128]{1,0:T(8,128)(2,1)S(1)} %get-tuple-element.21), channel_id=1, source_target_pairs={{0,12},{4,0},{8,4},{12,8},{1,13},{5,1},{9,5},{13,9},{2,14},{6,2},{... | collective-permute-start | bytes 196616 | tf_op jit(solution)/shard_map/ppermute | solution.py:303
  10.9 2.4 %project.2 = f32[256,128]{1,0:T(8,128)S(1)} custom-call(bf16[1024,2048]{1,0:T(8,128)(2,1)} %act_hbm.3, bf16[1024,2048]{1,0:T(8,128)(2,1)} %grad_hbm.3, bf16[64,2048]{1,0:T(8,128)(2,1)} %bitcast.6, bf16[64,2048]{1,0:T(8,128)(2,1)} %bitcast.8), custom_call_target="tpu_custom_call" | custom-call | flops 134217728 | bytes 4194304 | tf_op jit(solution)/shard_map/project/pallas_call | solution.py:59
  13.4 0.7 %collective-permute-done.1 = bf16[256,128]{1,0:T(8,128)(2,1)S(1)} collective-permute-done((bf16[256,128]{1,0:T(8,128)(2,1)S(1)}, bf16[256,128]{1,0:T(8,128)(2,1)S(1)}, u32[]{:S(2)}, u32[]{:S(2)}) %collective-permute-start.1) | collective-permute-done | bytes 65568 | tf_op jit(solution)/shard_map/ppermute | solution.py:303
  14.0 0.2 collective-permute-done.2
  14.3 1.6 %collective-permute-start.4 = (bf16[256,128]{1,0:T(8,128)(2,1)S(1)}, bf16[256,128]{1,0:T(8,128)(2,1)S(1)}, u32[]{:S(2)}, u32[]{:S(2)}) collective-permute-start(bf16[256,128]{1,0:T(8,128)(2,1)S(1)} %add_convert_fusion.rest_0_), channel_id=1, source_target_pairs={{0,4},{4,8},{8,12},{12,0},{1,5},{5,9},{9,13},{13,1},{2,6},{6,10},{... | collective-permute-start | bytes 196616 | tf_op jit(solution)/shard_map/ppermute | solution.py:303
  16.0 2.0 %collective-permute-start.5 = (bf16[256,128]{1,0:T(8,128)(2,1)S(1)}, bf16[256,128]{1,0:T(8,128)(2,1)S(1)}, u32[]{:S(2)}, u32[]{:S(2)}) collective-permute-start(bf16[256,128]{1,0:T(8,128)(2,1)S(1)} %add_convert_fusion.rest_0_), channel_id=1, source_target_pairs={{0,8},{4,12},{8,0},{12,4},{1,9},{5,13},{9,1},{13,5},{2,10},{6,14},... | collective-permute-start | bytes 196616 | tf_op jit(solution)/shard_map/ppermute | solution.py:303
  18.0 0.4 collective-permute-start.6
  18.4 0.0 collective-permute-start.3
  18.4 3.6 %load.1 = (bf16[1024,4096]{1,0:T(8,128)(2,1)S(1)}, s32[16]{0:T(128)S(4)}, bf16[512,128]{1,0:T(8,128)(2,1)S(1)}, bf16[128,128]{1,0:T(8,128)(2,1)S(1)}) custom-call(s32[8,128]{1,0:T(8,128)S(1)} %bitcast.3, bf16[1024,4096]{1,0:T(8,128)(2,1)} %hbm_ref), custom_call_target="tpu_custom_call" | custom-call | bytes 33554432 | tf_op jit(solution)/shard_map/load/pallas_call | solution.py:103
  22.0 0.6 %collective-permute-done.5.rest_2_ = bf16[256,128]{1,0:T(8,128)(2,1)S(1)} collective-permute-done((bf16[256,128]{1,0:T(8,128)(2,1)S(1)}, bf16[256,128]{1,0:T(8,128)(2,1)S(1)}, u32[]{:S(2)}, u32[]{:S(2)}) %collective-permute-start.5) | collective-permute-done | bytes 65568 | tf_op jit(solution)/shard_map/ppermute | solution.py:303
  22.7 0.4 collective-permute-done.6.rest_3_
  23.0 2.9 %query.1 = (bf16[512,128]{1,0:T(8,128)(2,1)S(1)}, bf16[128,4096]{1,0:T(8,128)(2,1)S(1)}) custom-call(s32[16]{0:T(128)S(4)} %get-tuple-element.24.start_ref, bf16[512,128]{1,0:T(8,128)(2,1)S(1)} %get-tuple-element.25.pick_ref, bf16[128,128]{1,0:T(8,128)(2,1)S(1)} %get-tuple-element.26.double_ref, s32[8,128]{1,0:T(8,128)S(1)} %bitcast.4, ...), custom_call_target="tpu_custom_call" | custom-call | tf_op jit(solution)/shard_map/query/pallas_call | solution.py:169
  25.9 1.2 %curve.1.rest_2_ = bf16[512,128]{1,0:T(8,128)(2,1)S(1)} custom-call(bf16[128,4096]{1,0:T(8,128)(2,1)S(1)} %get-tuple-element.29.pe_ref, bf16[1024,4096]{1,0:T(8,128)(2,1)S(1)} %get-tuple-element.27.rest_4_.ic_ref), custom_call_target="tpu_custom_call" | custom-call | flops 26843545600 | bytes 4194304 | tf_op jit(solution)/shard_map/curve/pallas_call | solution.py:183
  27.1 0.1 collective-permute-start.17
  27.2 0.5 collective-permute-start.10
  27.7 1.5 %collective-permute-start.14 = (bf16[512,128]{1,0:T(8,128)(2,1)S(1)}, bf16[512,128]{1,0:T(8,128)(2,1)S(1)}, u32[]{:S(2)}, u32[]{:S(2)}) collective-permute-start(bf16[512,128]{1,0:T(8,128)(2,1)S(1)} %curve.1.rest_2_), channel_id=1, source_target_pairs={{0,4},{1,3},{4,8},{5,1},{8,12},{9,5},{12,14},{13,9},{14,10},{15,13... | collective-permute-start | bytes 393224 | tf_op jit(solution)/shard_map/ppermute | solution.py:342
  29.2 0.0 collective-permute-start.7
  29.3 0.0 collective-permute-done.17.rest_3_
  29.3 1.8 %collective-permute-start.18 = (bf16[512,128]{1,0:T(8,128)(2,1)S(1)}, bf16[512,128]{1,0:T(8,128)(2,1)S(1)}, u32[]{:S(2)}, u32[]{:S(2)}) collective-permute-start(bf16[512,128]{1,0:T(8,128)(2,1)S(1)} %collective-permute-done.17.rest_3_), channel_id=1, source_target_pairs={{0,4},{1,3},{4,8},{5,1},{8,12},{9,5},{12,14},{13,9},{14,10},{15,13... | collective-permute-start | bytes 393224 | tf_op jit(solution)/shard_map/ppermute | solution.py:342
  31.1 1.2 %collective-permute-start.11 = (bf16[512,128]{1,0:T(8,128)(2,1)S(1)}, bf16[512,128]{1,0:T(8,128)(2,1)S(1)}, u32[]{:S(2)}, u32[]{:S(2)}) collective-permute-start(bf16[512,128]{1,0:T(8,128)(2,1)S(1)} %collective-permute-done.10.rest_1_), channel_id=1, source_target_pairs={{0,4},{1,3},{4,8},{5,1},{8,12},{9,5},{12,14},{13,9},{14,10},{15,13... | collective-permute-start | bytes 393224 | tf_op jit(solution)/shard_map/ppermute | solution.py:342
  32.4 0.3 collective-permute-done.14.rest_6_
  32.7 1.5 %collective-permute-start.15 = (bf16[512,128]{1,0:T(8,128)(2,1)S(1)}, bf16[512,128]{1,0:T(8,128)(2,1)S(1)}, u32[]{:S(2)}, u32[]{:S(2)}) collective-permute-start(bf16[512,128]{1,0:T(8,128)(2,1)S(1)} %collective-permute-done.14.rest_6_), channel_id=1, source_target_pairs={{0,4},{1,3},{4,8},{5,1},{8,12},{9,5},{12,14},{13,9},{14,10},{15,13... | collective-permute-start | bytes 393224 | tf_op jit(solution)/shard_map/ppermute | solution.py:342
  34.2 0.0 collective-permute-done.7.rest_4_
  34.2 1.4 %collective-permute-start.8 = (bf16[512,128]{1,0:T(8,128)(2,1)S(1)}, bf16[512,128]{1,0:T(8,128)(2,1)S(1)}, u32[]{:S(2)}, u32[]{:S(2)}) collective-permute-start(bf16[512,128]{1,0:T(8,128)(2,1)S(1)} %collective-permute-done.7.rest_4_), channel_id=1, source_target_pairs={{0,4},{1,3},{4,8},{5,1},{8,12},{9,5},{12,14},{13,9},{14,10},{15,13... | collective-permute-start | bytes 393224 | tf_op jit(solution)/shard_map/ppermute | solution.py:342
  35.6 1.4 %collective-permute-start.19 = (bf16[512,128]{1,0:T(8,128)(2,1)S(1)}, bf16[512,128]{1,0:T(8,128)(2,1)S(1)}, u32[]{:S(2)}, u32[]{:S(2)}) collective-permute-start(bf16[512,128]{1,0:T(8,128)(2,1)S(1)} %collective-permute-done.18.rest_7_), channel_id=1, source_target_pairs={{0,4},{1,3},{4,8},{5,1},{8,12},{9,5},{12,14},{13,9},{14,10},{15,13... | collective-permute-start | bytes 393224 | tf_op jit(solution)/shard_map/ppermute | solution.py:342
  37.0 0.0 collective-permute-done.11.rest_5_
  37.0 1.4 %collective-permute-start.12 = (bf16[512,128]{1,0:T(8,128)(2,1)S(1)}, bf16[512,128]{1,0:T(8,128)(2,1)S(1)}, u32[]{:S(2)}, u32[]{:S(2)}) collective-permute-start(bf16[512,128]{1,0:T(8,128)(2,1)S(1)} %collective-permute-done.11.rest_5_), channel_id=1, source_target_pairs={{0,4},{1,3},{4,8},{5,1},{8,12},{9,5},{12,14},{13,9},{14,10},{15,13... | collective-permute-start | bytes 393224 | tf_op jit(solution)/shard_map/ppermute | solution.py:342
  38.4 1.4 %collective-permute-start.16 = (bf16[512,128]{1,0:T(8,128)(2,1)S(1)}, bf16[512,128]{1,0:T(8,128)(2,1)S(1)}, u32[]{:S(2)}, u32[]{:S(2)}) collective-permute-start(bf16[512,128]{1,0:T(8,128)(2,1)S(1)} %collective-permute-done.15.rest_10_), channel_id=1, source_target_pairs={{0,4},{1,3},{4,8},{5,1},{8,12},{9,5},{12,14},{13,9},{14,10},{15,13... | collective-permute-start | bytes 393224 | tf_op jit(solution)/shard_map/ppermute | solution.py:342
  39.8 1.4 %collective-permute-start.9 = (bf16[512,128]{1,0:T(8,128)(2,1)S(1)}, bf16[512,128]{1,0:T(8,128)(2,1)S(1)}, u32[]{:S(2)}, u32[]{:S(2)}) collective-permute-start(bf16[512,128]{1,0:T(8,128)(2,1)S(1)} %collective-permute-done.8.rest_8_), channel_id=1, source_target_pairs={{0,4},{1,3},{4,8},{5,1},{8,12},{9,5},{12,14},{13,9},{14,10},{15,13... | collective-permute-start | bytes 393224 | tf_op jit(solution)/shard_map/ppermute | solution.py:342
  41.2 0.0 collective-permute-done.19.rest_11_
  41.2 1.4 %collective-permute-start.20 = (bf16[512,128]{1,0:T(8,128)(2,1)S(1)}, bf16[512,128]{1,0:T(8,128)(2,1)S(1)}, u32[]{:S(2)}, u32[]{:S(2)}) collective-permute-start(bf16[512,128]{1,0:T(8,128)(2,1)S(1)} %collective-permute-done.19.rest_11_), channel_id=1, source_target_pairs={{0,4},{1,3},{4,8},{5,1},{8,12},{9,5},{12,14},{13,9},{14,10},{15,13... | collective-permute-start | bytes 393224 | tf_op jit(solution)/shard_map/ppermute | solution.py:342
  42.6 1.4 %collective-permute-start.13 = (bf16[512,128]{1,0:T(8,128)(2,1)S(1)}, bf16[512,128]{1,0:T(8,128)(2,1)S(1)}, u32[]{:S(2)}, u32[]{:S(2)}) collective-permute-start(bf16[512,128]{1,0:T(8,128)(2,1)S(1)} %collective-permute-done.12.rest_9_), channel_id=1, source_target_pairs={{0,4},{1,3},{4,8},{5,1},{8,12},{9,5},{12,14},{13,9},{14,10},{15,13... | collective-permute-start | bytes 393224 | tf_op jit(solution)/shard_map/ppermute | solution.py:342
  44.0 1.4 %collective-permute-start.24 = (bf16[512,128]{1,0:T(8,128)(2,1)S(1)}, bf16[512,128]{1,0:T(8,128)(2,1)S(1)}, u32[]{:S(2)}, u32[]{:S(2)}) collective-permute-start(bf16[512,128]{1,0:T(8,128)(2,1)S(1)} %collective-permute-done.16.rest_2_), channel_id=1, source_target_pairs={{0,4},{1,3},{4,8},{5,1},{8,12},{9,5},{12,14},{13,9},{14,10},{15,13... | collective-permute-start | bytes 393224 | tf_op jit(solution)/shard_map/ppermute | solution.py:342
  45.4 0.0 collective-permute-done.9.rest_0_
  45.4 1.4 %collective-permute-start.23 = (bf16[512,128]{1,0:T(8,128)(2,1)S(1)}, bf16[512,128]{1,0:T(8,128)(2,1)S(1)}, u32[]{:S(2)}, u32[]{:S(2)}) collective-permute-start(bf16[512,128]{1,0:T(8,128)(2,1)S(1)} %collective-permute-done.9.rest_0_), channel_id=1, source_target_pairs={{0,4},{1,3},{4,8},{5,1},{8,12},{9,5},{12,14},{13,9},{14,10},{15,13... | collective-permute-start | bytes 393224 | tf_op jit(solution)/shard_map/ppermute | solution.py:342
  46.8 1.0 %early_scores.2.rest_4_ = f32[4,2,256,128]{3,2,1,0:T(8,128)S(1)} custom-call(bf16[256,4096]{1,0:T(8,128)(2,1)S(1)} %copy-done, bf16[256,4096]{1,0:T(8,128)(2,1)S(1)} %collective-permute-done.3.other_ref, bf16[512,128]{1,0:T(8,128)(2,1)S(1)} %get-tuple-element.28.rest_0_, bf16[512,128]{1,0:T(8,128)(2,1)S(1)} %collective-permute-done.10.rest_1_, ...), custom_call_target="tpu_custom_call" | custom-call | tf_op jit(solution)/shard_map/early_scores/pallas_call | solution.py:234
  47.8 0.4 collective-permute-done.13.rest_1_
  48.2 0.8 %early_scores.3 = (f32[512,256]{1,0:T(8,128)S(1)}, f32[256,256]{1,0:T(8,128)S(1)}, f32[256,256]{1,0:T(8,128)S(1)}) custom-call(bf16[256,4096]{1,0:T(8,128)(2,1)S(1)} %copy-done, bf16[256,4096]{1,0:T(8,128)(2,1)S(1)} %collective-permute-done.3.other_ref, bf16[512,128]{1,0:T(8,128)(2,1)S(1)} %collective-permute-done.9.rest_0_, ...), custom_call_target="tpu_custom_call" | custom-call | tf_op jit(solution)/shard_map/early_scores/pallas_call | solution.py:234
  49.1 0.1 collective-permute-start.21
  49.2 0.5 collective-permute-start.22
  49.7 0.1 collective-permute-start.26
  49.7 1.3 %collective-permute-done.23.rest_0_ = bf16[512,128]{1,0:T(8,128)(2,1)S(1)} collective-permute-done((bf16[512,128]{1,0:T(8,128)(2,1)S(1)}, bf16[512,128]{1,0:T(8,128)(2,1)S(1)}, u32[]{:S(2)}, u32[]{:S(2)}) %collective-permute-start.23) | collective-permute-done | bytes 131104 | tf_op jit(solution)/shard_map/ppermute | solution.py:342
  51.1 0.2 collective-permute-done.26.rest_3_
  51.2 1.2 %collective-permute-done.25.rest_2_ = bf16[512,128]{1,0:T(8,128)(2,1)S(1)} collective-permute-done((bf16[512,128]{1,0:T(8,128)(2,1)S(1)}, bf16[512,128]{1,0:T(8,128)(2,1)S(1)}, u32[]{:S(2)}, u32[]{:S(2)}) %collective-permute-start.25) | collective-permute-done | bytes 131104 | tf_op jit(solution)/shard_map/ppermute | solution.py:358
  52.4 1.1 %final_scores.1 = f32[512,256]{1,0:T(8,128)} custom-call(bf16[256,4096]{1,0:T(8,128)(2,1)S(1)} %copy-done, f32[512,256]{1,0:T(8,128)S(1)} %get-tuple-element.30.keep_ref, f32[256,256]{1,0:T(8,128)S(1)} %collective-permute-done.21.got_ref, f32[256,256]{1,0:T(8,128)S(1)} %collective-permute-done.22.more_ref, ...), custom_call_target="tpu_custom_call" | custom-call | tf_op jit(solution)/shard_map/final_scores/pallas_call | solution.py:281
  (19 shorter events, 0.1 us)
Async XLA Ops:
  3.9 9.5 %collective-permute-start = (bf16[256,128]{1,0:T(8,128)(2,1)S(1)}, bf16[256,128]{1,0:T(8,128)(2,1)S(1)}, u32[]{:S(2)}, u32[]{:S(2)}) collective-permute-start(bf16[256,128]{1,0:T(8,128)(2,1)S(1)} %get-tuple-element.19), channel_id=1, source_target_pairs={{0,4},{4,8},{8,12},{12,0},{1,5},{5,9},{9,13},{13,1},{2,6},{6,10},{... | collective-permute-start | bytes 196616 | tf_op jit(solution)/shard_map/ppermute | solution.py:303
  7.0 7.1 %collective-permute-start.1 = (bf16[256,128]{1,0:T(8,128)(2,1)S(1)}, bf16[256,128]{1,0:T(8,128)(2,1)S(1)}, u32[]{:S(2)}, u32[]{:S(2)}) collective-permute-start(bf16[256,128]{1,0:T(8,128)(2,1)S(1)} %get-tuple-element.20), channel_id=1, source_target_pairs={{0,8},{4,12},{8,0},{12,4},{1,9},{5,13},{9,1},{13,5},{2,10},{6,14},... | collective-permute-start | bytes 196616 | tf_op jit(solution)/shard_map/ppermute | solution.py:303
  9.6 8.8 %copy-start = (bf16[256,4096]{1,0:T(8,128)(2,1)S(1)}, bf16[256,4096]{1,0:T(8,128)(2,1)}, u32[]{:S(2)}) copy-start(bf16[256,4096]{1,0:T(8,128)(2,1)} %stored_ref) | copy-start | bytes 6291460
  9.6 8.8 %copy-start.1 = (s32[1,1024]{1,0:T(1,128)S(1)}, s32[1,1024]{1,0:T(1,128)}, u32[]{:S(2)}) copy-start(s32[1,1024]{1,0:T(1,128)} %param.9) | copy-start | bytes 12292
  9.6 4.7 %collective-permute-start.2 = (bf16[256,128]{1,0:T(8,128)(2,1)S(1)}, bf16[256,128]{1,0:T(8,128)(2,1)S(1)}, u32[]{:S(2)}, u32[]{:S(2)}) collective-permute-start(bf16[256,128]{1,0:T(8,128)(2,1)S(1)} %get-tuple-element.21), channel_id=1, source_target_pairs={{0,12},{4,0},{8,4},{12,8},{1,13},{5,1},{9,5},{13,9},{2,14},{6,2},{... | collective-permute-start | bytes 196616 | tf_op jit(solution)/shard_map/ppermute | solution.py:303
  14.3 7.7 %collective-permute-start.4 = (bf16[256,128]{1,0:T(8,128)(2,1)S(1)}, bf16[256,128]{1,0:T(8,128)(2,1)S(1)}, u32[]{:S(2)}, u32[]{:S(2)}) collective-permute-start(bf16[256,128]{1,0:T(8,128)(2,1)S(1)} %add_convert_fusion.rest_0_), channel_id=1, source_target_pairs={{0,4},{4,8},{8,12},{12,0},{1,5},{5,9},{9,13},{13,1},{2,6},{6,10},{... | collective-permute-start | bytes 196616 | tf_op jit(solution)/shard_map/ppermute | solution.py:303
  16.0 6.7 %collective-permute-start.5 = (bf16[256,128]{1,0:T(8,128)(2,1)S(1)}, bf16[256,128]{1,0:T(8,128)(2,1)S(1)}, u32[]{:S(2)}, u32[]{:S(2)}) collective-permute-start(bf16[256,128]{1,0:T(8,128)(2,1)S(1)} %add_convert_fusion.rest_0_), channel_id=1, source_target_pairs={{0,8},{4,12},{8,0},{12,4},{1,9},{5,13},{9,1},{13,5},{2,10},{6,14},... | collective-permute-start | bytes 196616 | tf_op jit(solution)/shard_map/ppermute | solution.py:303
  18.0 5.0 %collective-permute-start.6 = (bf16[256,128]{1,0:T(8,128)(2,1)S(1)}, bf16[256,128]{1,0:T(8,128)(2,1)S(1)}, u32[]{:S(2)}, u32[]{:S(2)}) collective-permute-start(bf16[256,128]{1,0:T(8,128)(2,1)S(1)} %add_convert_fusion.rest_0_), channel_id=1, source_target_pairs={{0,12},{4,0},{8,4},{12,8},{1,13},{5,1},{9,5},{13,9},{2,14},{6,2},{... | collective-permute-start | bytes 196616 | tf_op jit(solution)/shard_map/ppermute | solution.py:303
  18.4 28.4 %collective-permute-start.3 = (bf16[256,4096]{1,0:T(8,128)(2,1)S(1)}, bf16[256,4096]{1,0:T(8,128)(2,1)S(1)}, u32[]{:S(2)}, u32[]{:S(2)}) collective-permute-start(bf16[256,4096]{1,0:T(8,128)(2,1)S(1)} %copy-done), channel_id=1, source_target_pairs={{0,1},{1,0},{2,3},{3,2},{4,5},{5,4},{6,7},{7,6},{8,9},{9,8},{10,11... | collective-permute-start | bytes 6291464 | tf_op jit(solution)/shard_map/ppermute | solution.py:339
  27.1 2.1 %collective-permute-start.17 = (bf16[512,128]{1,0:T(8,128)(2,1)S(1)}, bf16[512,128]{1,0:T(8,128)(2,1)S(1)}, u32[]{:S(2)}, u32[]{:S(2)}) collective-permute-start(bf16[512,128]{1,0:T(8,128)(2,1)S(1)} %curve.1.rest_2_), channel_id=1, source_target_pairs={{0,1},{1,0},{2,3},{3,2},{4,5},{5,4},{6,7},{7,6},{8,9},{9,8},{10,11... | collective-permute-start | bytes 393224 | tf_op jit(solution)/shard_map/ppermute | solution.py:343
  27.2 3.9 %collective-permute-start.10 = (bf16[512,128]{1,0:T(8,128)(2,1)S(1)}, bf16[512,128]{1,0:T(8,128)(2,1)S(1)}, u32[]{:S(2)}, u32[]{:S(2)}) collective-permute-start(bf16[512,128]{1,0:T(8,128)(2,1)S(1)} %get-tuple-element.28.rest_0_), channel_id=1, source_target_pairs={{0,1},{1,0},{2,3},{3,2},{4,5},{5,4},{6,7},{7,6},{8,9},{9,8},{10,11... | collective-permute-start | bytes 393224 | tf_op jit(solution)/shard_map/ppermute | solution.py:343
  27.7 5.0 %collective-permute-start.14 = (bf16[512,128]{1,0:T(8,128)(2,1)S(1)}, bf16[512,128]{1,0:T(8,128)(2,1)S(1)}, u32[]{:S(2)}, u32[]{:S(2)}) collective-permute-start(bf16[512,128]{1,0:T(8,128)(2,1)S(1)} %curve.1.rest_2_), channel_id=1, source_target_pairs={{0,4},{1,3},{4,8},{5,1},{8,12},{9,5},{12,14},{13,9},{14,10},{15,13... | collective-permute-start | bytes 393224 | tf_op jit(solution)/shard_map/ppermute | solution.py:342
  29.2 5.0 %collective-permute-start.7 = (bf16[512,128]{1,0:T(8,128)(2,1)S(1)}, bf16[512,128]{1,0:T(8,128)(2,1)S(1)}, u32[]{:S(2)}, u32[]{:S(2)}) collective-permute-start(bf16[512,128]{1,0:T(8,128)(2,1)S(1)} %get-tuple-element.28.rest_0_), channel_id=1, source_target_pairs={{0,4},{1,3},{4,8},{5,1},{8,12},{9,5},{12,14},{13,9},{14,10},{15,13... | collective-permute-start | bytes 393224 | tf_op jit(solution)/shard_map/ppermute | solution.py:342
  29.3 6.3 %collective-permute-start.18 = (bf16[512,128]{1,0:T(8,128)(2,1)S(1)}, bf16[512,128]{1,0:T(8,128)(2,1)S(1)}, u32[]{:S(2)}, u32[]{:S(2)}) collective-permute-start(bf16[512,128]{1,0:T(8,128)(2,1)S(1)} %collective-permute-done.17.rest_3_), channel_id=1, source_target_pairs={{0,4},{1,3},{4,8},{5,1},{8,12},{9,5},{12,14},{13,9},{14,10},{15,13... | collective-permute-start | bytes 393224 | tf_op jit(solution)/shard_map/ppermute | solution.py:342
  31.1 5.9 %collective-permute-start.11 = (bf16[512,128]{1,0:T(8,128)(2,1)S(1)}, bf16[512,128]{1,0:T(8,128)(2,1)S(1)}, u32[]{:S(2)}, u32[]{:S(2)}) collective-permute-start(bf16[512,128]{1,0:T(8,128)(2,1)S(1)} %collective-permute-done.10.rest_1_), channel_id=1, source_target_pairs={{0,4},{1,3},{4,8},{5,1},{8,12},{9,5},{12,14},{13,9},{14,10},{15,13... | collective-permute-start | bytes 393224 | tf_op jit(solution)/shard_map/ppermute | solution.py:342
  32.7 5.7 %collective-permute-start.15 = (bf16[512,128]{1,0:T(8,128)(2,1)S(1)}, bf16[512,128]{1,0:T(8,128)(2,1)S(1)}, u32[]{:S(2)}, u32[]{:S(2)}) collective-permute-start(bf16[512,128]{1,0:T(8,128)(2,1)S(1)} %collective-permute-done.14.rest_6_), channel_id=1, source_target_pairs={{0,4},{1,3},{4,8},{5,1},{8,12},{9,5},{12,14},{13,9},{14,10},{15,13... | collective-permute-start | bytes 393224 | tf_op jit(solution)/shard_map/ppermute | solution.py:342
  34.2 5.6 %collective-permute-start.8 = (bf16[512,128]{1,0:T(8,128)(2,1)S(1)}, bf16[512,128]{1,0:T(8,128)(2,1)S(1)}, u32[]{:S(2)}, u32[]{:S(2)}) collective-permute-start(bf16[512,128]{1,0:T(8,128)(2,1)S(1)} %collective-permute-done.7.rest_4_), channel_id=1, source_target_pairs={{0,4},{1,3},{4,8},{5,1},{8,12},{9,5},{12,14},{13,9},{14,10},{15,13... | collective-permute-start | bytes 393224 | tf_op jit(solution)/shard_map/ppermute | solution.py:342
  35.6 5.6 %collective-permute-start.19 = (bf16[512,128]{1,0:T(8,128)(2,1)S(1)}, bf16[512,128]{1,0:T(8,128)(2,1)S(1)}, u32[]{:S(2)}, u32[]{:S(2)}) collective-permute-start(bf16[512,128]{1,0:T(8,128)(2,1)S(1)} %collective-permute-done.18.rest_7_), channel_id=1, source_target_pairs={{0,4},{1,3},{4,8},{5,1},{8,12},{9,5},{12,14},{13,9},{14,10},{15,13... | collective-permute-start | bytes 393224 | tf_op jit(solution)/shard_map/ppermute | solution.py:342
  37.0 5.6 %collective-permute-start.12 = (bf16[512,128]{1,0:T(8,128)(2,1)S(1)}, bf16[512,128]{1,0:T(8,128)(2,1)S(1)}, u32[]{:S(2)}, u32[]{:S(2)}) collective-permute-start(bf16[512,128]{1,0:T(8,128)(2,1)S(1)} %collective-permute-done.11.rest_5_), channel_id=1, source_target_pairs={{0,4},{1,3},{4,8},{5,1},{8,12},{9,5},{12,14},{13,9},{14,10},{15,13... | collective-permute-start | bytes 393224 | tf_op jit(solution)/shard_map/ppermute | solution.py:342
  38.4 5.6 %collective-permute-start.16 = (bf16[512,128]{1,0:T(8,128)(2,1)S(1)}, bf16[512,128]{1,0:T(8,128)(2,1)S(1)}, u32[]{:S(2)}, u32[]{:S(2)}) collective-permute-start(bf16[512,128]{1,0:T(8,128)(2,1)S(1)} %collective-permute-done.15.rest_10_), channel_id=1, source_target_pairs={{0,4},{1,3},{4,8},{5,1},{8,12},{9,5},{12,14},{13,9},{14,10},{15,13... | collective-permute-start | bytes 393224 | tf_op jit(solution)/shard_map/ppermute | solution.py:342
  39.8 5.6 %collective-permute-start.9 = (bf16[512,128]{1,0:T(8,128)(2,1)S(1)}, bf16[512,128]{1,0:T(8,128)(2,1)S(1)}, u32[]{:S(2)}, u32[]{:S(2)}) collective-permute-start(bf16[512,128]{1,0:T(8,128)(2,1)S(1)} %collective-permute-done.8.rest_8_), channel_id=1, source_target_pairs={{0,4},{1,3},{4,8},{5,1},{8,12},{9,5},{12,14},{13,9},{14,10},{15,13... | collective-permute-start | bytes 393224 | tf_op jit(solution)/shard_map/ppermute | solution.py:342
  41.2 6.6 %collective-permute-start.20 = (bf16[512,128]{1,0:T(8,128)(2,1)S(1)}, bf16[512,128]{1,0:T(8,128)(2,1)S(1)}, u32[]{:S(2)}, u32[]{:S(2)}) collective-permute-start(bf16[512,128]{1,0:T(8,128)(2,1)S(1)} %collective-permute-done.19.rest_11_), channel_id=1, source_target_pairs={{0,4},{1,3},{4,8},{5,1},{8,12},{9,5},{12,14},{13,9},{14,10},{15,13... | collective-permute-start | bytes 393224 | tf_op jit(solution)/shard_map/ppermute | solution.py:342
  42.6 5.6 %collective-permute-start.13 = (bf16[512,128]{1,0:T(8,128)(2,1)S(1)}, bf16[512,128]{1,0:T(8,128)(2,1)S(1)}, u32[]{:S(2)}, u32[]{:S(2)}) collective-permute-start(bf16[512,128]{1,0:T(8,128)(2,1)S(1)} %collective-permute-done.12.rest_9_), channel_id=1, source_target_pairs={{0,4},{1,3},{4,8},{5,1},{8,12},{9,5},{12,14},{13,9},{14,10},{15,13... | collective-permute-start | bytes 393224 | tf_op jit(solution)/shard_map/ppermute | solution.py:342
  44.0 5.6 %collective-permute-start.24 = (bf16[512,128]{1,0:T(8,128)(2,1)S(1)}, bf16[512,128]{1,0:T(8,128)(2,1)S(1)}, u32[]{:S(2)}, u32[]{:S(2)}) collective-permute-start(bf16[512,128]{1,0:T(8,128)(2,1)S(1)} %collective-permute-done.16.rest_2_), channel_id=1, source_target_pairs={{0,4},{1,3},{4,8},{5,1},{8,12},{9,5},{12,14},{13,9},{14,10},{15,13... | collective-permute-start | bytes 393224 | tf_op jit(solution)/shard_map/ppermute | solution.py:342
  45.4 5.6 %collective-permute-start.23 = (bf16[512,128]{1,0:T(8,128)(2,1)S(1)}, bf16[512,128]{1,0:T(8,128)(2,1)S(1)}, u32[]{:S(2)}, u32[]{:S(2)}) collective-permute-start(bf16[512,128]{1,0:T(8,128)(2,1)S(1)} %collective-permute-done.9.rest_0_), channel_id=1, source_target_pairs={{0,4},{1,3},{4,8},{5,1},{8,12},{9,5},{12,14},{13,9},{14,10},{15,13... | collective-permute-start | bytes 393224 | tf_op jit(solution)/shard_map/ppermute | solution.py:342
  49.1 3.3 %collective-permute-start.21 = (f32[256,256]{1,0:T(8,128)S(1)}, f32[256,256]{1,0:T(8,128)S(1)}, u32[]{:S(2)}, u32[]{:S(2)}) collective-permute-start(f32[256,256]{1,0:T(8,128)S(1)} %get-tuple-element.31), channel_id=1, source_target_pairs={{0,1},{1,0},{2,3},{3,2},{4,5},{5,4},{6,7},{7,6},{8,9},{9,8},{10,11... | collective-permute-start | bytes 786440 | tf_op jit(solution)/shard_map/ppermute | solution.py:357
  49.2 3.2 %collective-permute-start.22 = (f32[256,256]{1,0:T(8,128)S(1)}, f32[256,256]{1,0:T(8,128)S(1)}, u32[]{:S(2)}, u32[]{:S(2)}) collective-permute-start(f32[256,256]{1,0:T(8,128)S(1)} %get-tuple-element.32), channel_id=1, source_target_pairs={{0,1},{1,0},{2,3},{3,2},{4,5},{5,4},{6,7},{7,6},{8,9},{9,8},{10,11... | collective-permute-start | bytes 786440 | tf_op jit(solution)/shard_map/ppermute | solution.py:357
  49.7 1.6 %collective-permute-start.26 = (bf16[512,128]{1,0:T(8,128)(2,1)S(1)}, bf16[512,128]{1,0:T(8,128)(2,1)S(1)}, u32[]{:S(2)}, u32[]{:S(2)}) collective-permute-start(bf16[512,128]{1,0:T(8,128)(2,1)S(1)} %collective-permute-done.24.rest_1_), channel_id=1, source_target_pairs={{0,1},{1,0},{2,3},{3,2},{4,5},{5,4},{6,7},{7,6},{8,9},{9,8},{10,11... | collective-permute-start | bytes 393224 | tf_op jit(solution)/shard_map/ppermute | solution.py:358
  51.1 1.3 %collective-permute-start.25 = (bf16[512,128]{1,0:T(8,128)(2,1)S(1)}, bf16[512,128]{1,0:T(8,128)(2,1)S(1)}, u32[]{:S(2)}, u32[]{:S(2)}) collective-permute-start(bf16[512,128]{1,0:T(8,128)(2,1)S(1)} %collective-permute-done.23.rest_0_), channel_id=1, source_target_pairs={{0,1},{1,0},{2,3},{3,2},{4,5},{5,4},{6,7},{7,6},{8,9},{9,8},{10,11... | collective-permute-start | bytes 393224 | tf_op jit(solution)/shard_map/ppermute | solution.py:358

commit v8 on v6

--- a/solution.py
+++ b/solution.py
@@ -338,7 +338,7 @@
     early, spots = list(streams), [(0, 0), (0, half)]
     total = None
     for step in range(1, places // 2):
-        if step == places // 2 - 1:
+        if step == places // 2 - 2:
             total = early_scores(stored, others, early, spots, None, False, places, planes)
             early, spots = [], []
         streams = [on(x) for x in streams]

time: 53.7 us -> 53.7 us (level)
  no operation moved by 1% of the time
where the time goes in v8:
time: 53.7 us; the launch traced here: 53.5 us
  starting transfers between devices  31.1 us (58%)
  Pallas kernels  17 us (32%)
  waiting for transfers between devices  5.3 us (10%)
    ppermute x14, starting transfers between devices, body(): lax.ppermute(x, ('width', 'store'), ring_pairs(planes, stores))  18.8 us
    ppermute x6, starting transfers between devices, turn(): lax.ppermute(x, 'width', [(i, (i + d) % planes) for i in range(planes)])  11.1 us
    pallas_call x2, Pallas kernels, project(): pl.pallas_call(functools.partial(project_kernel, planes, turns), in_specs...  6.32 us
    pallas_call x1, Pallas kernels, load(): pl.pallas_call(load_kernel, in_specs=[vmem, pl.BlockSpec(memory_space=plt...  3.61 us
    pallas_call x1, Pallas kernels, query_transposed(): pl.pallas_call(functools.partial(query_kernel, len(factors)), in_specs=[p...  2.89 us
    ppermute x14, waiting for transfers between devices, body(): lax.ppermute(x, ('width', 'store'), ring_pairs(planes, stores))  2.07 us
    ppermute x6, waiting for transfers between devices, turn(): lax.ppermute(x, 'width', [(i, (i + d) % planes) for i in range(planes)])  1.88 us
    pallas_call x2, Pallas kernels, early_scores(): pl.pallas_call(functools.partial(early_kernel, places, planes, spots, boo...  1.82 us
  transfers between devices with their start and end apart: 27, of which 9 were waited for; matrix products, arithmetic and copies ran while one was open for 0% of the time, Pallas kernels for 22%

profile of v8, /device:TPU:0, one launch (start us, length us, event | category | flops | bytes accessed | tf_op | source)
XLA Modules:
  0.0 53.5 jit_solution(2838091149665636839)
XLA Ops:
  0.0 3.9 %project.3 = (bf16[256,128]{1,0:T(8,128)(2,1)S(1)}, bf16[256,128]{1,0:T(8,128)(2,1)S(1)}, bf16[256,128]{1,0:T(8,128)(2,1)S(1)}) custom-call(bf16[1024,2048]{1,0:T(8,128)(2,1)} %act_hbm.3, bf16[1024,2048]{1,0:T(8,128)(2,1)} %grad_hbm.3, bf16[64,2048]{1,0:T(8,128)(2,1)} %bitcast.5, bf16[64,2048]{1,0:T(8,128)(2,1)} %bitcast.7), custom_call_target="tpu_custom_call" | custom-call | flops 402653184 | bytes 12582912 | tf_op jit(solution)/shard_map/project/pallas_call | solution.py:59
  3.9 3.1 %collective-permute-start = (bf16[256,128]{1,0:T(8,128)(2,1)S(1)}, bf16[256,128]{1,0:T(8,128)(2,1)S(1)}, u32[]{:S(2)}, u32[]{:S(2)}) collective-permute-start(bf16[256,128]{1,0:T(8,128)(2,1)S(1)} %get-tuple-element.17), channel_id=1, source_target_pairs={{0,4},{4,8},{8,12},{12,0},{1,5},{5,9},{9,13},{13,1},{2,6},{6,10},{... | collective-permute-start | bytes 196616 | tf_op jit(solution)/shard_map/ppermute | solution.py:295
  7.0 2.6 %collective-permute-start.1 = (bf16[256,128]{1,0:T(8,128)(2,1)S(1)}, bf16[256,128]{1,0:T(8,128)(2,1)S(1)}, u32[]{:S(2)}, u32[]{:S(2)}) collective-permute-start(bf16[256,128]{1,0:T(8,128)(2,1)S(1)} %get-tuple-element.18), channel_id=1, source_target_pairs={{0,8},{4,12},{8,0},{12,4},{1,9},{5,13},{9,1},{13,5},{2,10},{6,14},... | collective-permute-start | bytes 196616 | tf_op jit(solution)/shard_map/ppermute | solution.py:295
  9.6 1.3 %collective-permute-start.2 = (bf16[256,128]{1,0:T(8,128)(2,1)S(1)}, bf16[256,128]{1,0:T(8,128)(2,1)S(1)}, u32[]{:S(2)}, u32[]{:S(2)}) collective-permute-start(bf16[256,128]{1,0:T(8,128)(2,1)S(1)} %get-tuple-element.19), channel_id=1, source_target_pairs={{0,12},{4,0},{8,4},{12,8},{1,13},{5,1},{9,5},{13,9},{2,14},{6,2},{... | collective-permute-start | bytes 196616 | tf_op jit(solution)/shard_map/ppermute | solution.py:295
  10.9 2.4 %project.2 = f32[256,128]{1,0:T(8,128)S(1)} custom-call(bf16[1024,2048]{1,0:T(8,128)(2,1)} %act_hbm.3, bf16[1024,2048]{1,0:T(8,128)(2,1)} %grad_hbm.3, bf16[64,2048]{1,0:T(8,128)(2,1)} %bitcast.6, bf16[64,2048]{1,0:T(8,128)(2,1)} %bitcast.8), custom_call_target="tpu_custom_call" | custom-call | flops 134217728 | bytes 4194304 | tf_op jit(solution)/shard_map/project/pallas_call | solution.py:59
  13.4 0.7 %collective-permute-done.1 = bf16[256,128]{1,0:T(8,128)(2,1)S(1)} collective-permute-done((bf16[256,128]{1,0:T(8,128)(2,1)S(1)}, bf16[256,128]{1,0:T(8,128)(2,1)S(1)}, u32[]{:S(2)}, u32[]{:S(2)}) %collective-permute-start.1) | collective-permute-done | bytes 65568 | tf_op jit(solution)/shard_map/ppermute | solution.py:295
  14.0 0.2 collective-permute-done.2
  14.3 1.6 %collective-permute-start.4 = (bf16[256,128]{1,0:T(8,128)(2,1)S(1)}, bf16[256,128]{1,0:T(8,128)(2,1)S(1)}, u32[]{:S(2)}, u32[]{:S(2)}) collective-permute-start(bf16[256,128]{1,0:T(8,128)(2,1)S(1)} %add_convert_fusion.rest_0_), channel_id=1, source_target_pairs={{0,4},{4,8},{8,12},{12,0},{1,5},{5,9},{9,13},{13,1},{2,6},{6,10},{... | collective-permute-start | bytes 196616 | tf_op jit(solution)/shard_map/ppermute | solution.py:295
  16.0 2.0 %collective-permute-start.5 = (bf16[256,128]{1,0:T(8,128)(2,1)S(1)}, bf16[256,128]{1,0:T(8,128)(2,1)S(1)}, u32[]{:S(2)}, u32[]{:S(2)}) collective-permute-start(bf16[256,128]{1,0:T(8,128)(2,1)S(1)} %add_convert_fusion.rest_0_), channel_id=1, source_target_pairs={{0,8},{4,12},{8,0},{12,4},{1,9},{5,13},{9,1},{13,5},{2,10},{6,14},... | collective-permute-start | bytes 196616 | tf_op jit(solution)/shard_map/ppermute | solution.py:295
  18.0 0.4 collective-permute-start.6
  18.4 3.6 %load.1 = (bf16[1024,4096]{1,0:T(8,128)(2,1)S(1)}, s32[16]{0:T(128)S(4)}) custom-call(s32[8,128]{1,0:T(8,128)S(1)} %bitcast.3, bf16[1024,4096]{1,0:T(8,128)(2,1)} %hbm_ref), custom_call_target="tpu_custom_call" | custom-call | bytes 33554432 | tf_op jit(solution)/shard_map/load/pallas_call | solution.py:94
  22.0 0.0 collective-permute-done.4.rest_1_
  22.0 0.6 %collective-permute-done.5.rest_2_ = bf16[256,128]{1,0:T(8,128)(2,1)S(1)} collective-permute-done((bf16[256,128]{1,0:T(8,128)(2,1)S(1)}, bf16[256,128]{1,0:T(8,128)(2,1)S(1)}, u32[]{:S(2)}, u32[]{:S(2)}) %collective-permute-start.5) | collective-permute-done | bytes 65568 | tf_op jit(solution)/shard_map/ppermute | solution.py:295
  22.6 0.4 collective-permute-done.6.rest_3_
  23.0 2.9 %query.1 = (bf16[512,128]{1,0:T(8,128)(2,1)S(1)}, bf16[128,4096]{1,0:T(8,128)(2,1)S(1)}) custom-call(s32[16]{0:T(128)S(4)} %get-tuple-element.22.start_ref, s32[8,128]{1,0:T(8,128)S(1)} %bitcast.4, bf16[256,128]{1,0:T(8,128)(2,1)S(1)} %add_convert_fusion.rest_0_, bf16[256,128]{1,0:T(8,128)(2,1)S(1)} %collective-permute-done.4.rest_1_, ...), custom_call_target="tpu_custom_call" | custom-call | tf_op jit(solution)/shard_map/query/pallas_call | solution.py:161
  25.9 1.2 %curve.1.rest_2_ = bf16[512,128]{1,0:T(8,128)(2,1)S(1)} custom-call(bf16[128,4096]{1,0:T(8,128)(2,1)S(1)} %get-tuple-element.25.pe_ref, bf16[1024,4096]{1,0:T(8,128)(2,1)S(1)} %get-tuple-element.23.rest_4_.ic_ref), custom_call_target="tpu_custom_call" | custom-call | flops 26843545600 | bytes 4194304 | tf_op jit(solution)/shard_map/curve/pallas_call | solution.py:175
  27.1 0.1 collective-permute-start.14
  27.2 0.5 collective-permute-start.9
  27.7 1.5 %collective-permute-start.12 = (bf16[512,128]{1,0:T(8,128)(2,1)S(1)}, bf16[512,128]{1,0:T(8,128)(2,1)S(1)}, u32[]{:S(2)}, u32[]{:S(2)}) collective-permute-start(bf16[512,128]{1,0:T(8,128)(2,1)S(1)} %curve.1.rest_2_), channel_id=1, source_target_pairs={{0,4},{1,3},{4,8},{5,1},{8,12},{9,5},{12,14},{13,9},{14,10},{15,13... | collective-permute-start | bytes 393224 | tf_op jit(solution)/shard_map/ppermute | solution.py:334
  29.2 0.0 collective-permute-start.7
  29.3 0.0 collective-permute-done.14.rest_3_
  29.3 1.9 %collective-permute-start.15 = (bf16[512,128]{1,0:T(8,128)(2,1)S(1)}, bf16[512,128]{1,0:T(8,128)(2,1)S(1)}, u32[]{:S(2)}, u32[]{:S(2)}) collective-permute-start(bf16[512,128]{1,0:T(8,128)(2,1)S(1)} %collective-permute-done.14.rest_3_), channel_id=1, source_target_pairs={{0,4},{1,3},{4,8},{5,1},{8,12},{9,5},{12,14},{13,9},{14,10},{15,13... | collective-permute-start | bytes 393224 | tf_op jit(solution)/shard_map/ppermute | solution.py:334
  31.1 1.2 %collective-permute-start.10 = (bf16[512,128]{1,0:T(8,128)(2,1)S(1)}, bf16[512,128]{1,0:T(8,128)(2,1)S(1)}, u32[]{:S(2)}, u32[]{:S(2)}) collective-permute-start(bf16[512,128]{1,0:T(8,128)(2,1)S(1)} %collective-permute-done.9.rest_1_), channel_id=1, source_target_pairs={{0,4},{1,3},{4,8},{5,1},{8,12},{9,5},{12,14},{13,9},{14,10},{15,13... | collective-permute-start | bytes 393224 | tf_op jit(solution)/shard_map/ppermute | solution.py:334
  32.4 0.3 collective-permute-done.12.rest_6_
  32.7 1.5 %collective-permute-start.13 = (bf16[512,128]{1,0:T(8,128)(2,1)S(1)}, bf16[512,128]{1,0:T(8,128)(2,1)S(1)}, u32[]{:S(2)}, u32[]{:S(2)}) collective-permute-start(bf16[512,128]{1,0:T(8,128)(2,1)S(1)} %collective-permute-done.12.rest_6_), channel_id=1, source_target_pairs={{0,4},{1,3},{4,8},{5,1},{8,12},{9,5},{12,14},{13,9},{14,10},{15,13... | collective-permute-start | bytes 393224 | tf_op jit(solution)/shard_map/ppermute | solution.py:334
  34.2 0.0 collective-permute-done.7.rest_4_
  34.2 1.4 %collective-permute-start.8 = (bf16[512,128]{1,0:T(8,128)(2,1)S(1)}, bf16[512,128]{1,0:T(8,128)(2,1)S(1)}, u32[]{:S(2)}, u32[]{:S(2)}) collective-permute-start(bf16[512,128]{1,0:T(8,128)(2,1)S(1)} %collective-permute-done.7.rest_4_), channel_id=1, source_target_pairs={{0,4},{1,3},{4,8},{5,1},{8,12},{9,5},{12,14},{13,9},{14,10},{15,13... | collective-permute-start | bytes 393224 | tf_op jit(solution)/shard_map/ppermute | solution.py:334
  35.6 1.4 %collective-permute-start.16 = (bf16[512,128]{1,0:T(8,128)(2,1)S(1)}, bf16[512,128]{1,0:T(8,128)(2,1)S(1)}, u32[]{:S(2)}, u32[]{:S(2)}) collective-permute-start(bf16[512,128]{1,0:T(8,128)(2,1)S(1)} %collective-permute-done.15.rest_7_), channel_id=1, source_target_pairs={{0,4},{1,3},{4,8},{5,1},{8,12},{9,5},{12,14},{13,9},{14,10},{15,13... | collective-permute-start | bytes 393224 | tf_op jit(solution)/shard_map/ppermute | solution.py:334
  37.0 0.0 collective-permute-done.10.rest_5_
  37.0 1.4 %collective-permute-start.11 = (bf16[512,128]{1,0:T(8,128)(2,1)S(1)}, bf16[512,128]{1,0:T(8,128)(2,1)S(1)}, u32[]{:S(2)}, u32[]{:S(2)}) collective-permute-start(bf16[512,128]{1,0:T(8,128)(2,1)S(1)} %collective-permute-done.10.rest_5_), channel_id=1, source_target_pairs={{0,4},{1,3},{4,8},{5,1},{8,12},{9,5},{12,14},{13,9},{14,10},{15,13... | collective-permute-start | bytes 393224 | tf_op jit(solution)/shard_map/ppermute | solution.py:334
  38.4 0.0 collective-permute-done.13.rest_2_
  38.4 1.4 %collective-permute-start.19 = (bf16[512,128]{1,0:T(8,128)(2,1)S(1)}, bf16[512,128]{1,0:T(8,128)(2,1)S(1)}, u32[]{:S(2)}, u32[]{:S(2)}) collective-permute-start(bf16[512,128]{1,0:T(8,128)(2,1)S(1)} %collective-permute-done.13.rest_2_), channel_id=1, source_target_pairs={{0,4},{1,3},{4,8},{5,1},{8,12},{9,5},{12,14},{13,9},{14,10},{15,13... | collective-permute-start | bytes 393224 | tf_op jit(solution)/shard_map/ppermute | solution.py:334
  39.8 1.4 %collective-permute-start.17 = (bf16[512,128]{1,0:T(8,128)(2,1)S(1)}, bf16[512,128]{1,0:T(8,128)(2,1)S(1)}, u32[]{:S(2)}, u32[]{:S(2)}) collective-permute-start(bf16[512,128]{1,0:T(8,128)(2,1)S(1)} %collective-permute-done.8.rest_0_), channel_id=1, source_target_pairs={{0,4},{1,3},{4,8},{5,1},{8,12},{9,5},{12,14},{13,9},{14,10},{15,13... | collective-permute-start | bytes 393224 | tf_op jit(solution)/shard_map/ppermute | solution.py:334
  41.2 0.0 collective-permute-done.16.rest_3_
  41.2 1.4 %collective-permute-start.20 = (bf16[512,128]{1,0:T(8,128)(2,1)S(1)}, bf16[512,128]{1,0:T(8,128)(2,1)S(1)}, u32[]{:S(2)}, u32[]{:S(2)}) collective-permute-start(bf16[512,128]{1,0:T(8,128)(2,1)S(1)} %collective-permute-done.16.rest_3_), channel_id=1, source_target_pairs={{0,4},{1,3},{4,8},{5,1},{8,12},{9,5},{12,14},{13,9},{14,10},{15,13... | collective-permute-start | bytes 393224 | tf_op jit(solution)/shard_map/ppermute | solution.py:334
  42.6 1.4 %collective-permute-start.18 = (bf16[512,128]{1,0:T(8,128)(2,1)S(1)}, bf16[512,128]{1,0:T(8,128)(2,1)S(1)}, u32[]{:S(2)}, u32[]{:S(2)}) collective-permute-start(bf16[512,128]{1,0:T(8,128)(2,1)S(1)} %collective-permute-done.11.rest_1_), channel_id=1, source_target_pairs={{0,4},{1,3},{4,8},{5,1},{8,12},{9,5},{12,14},{13,9},{14,10},{15,13... | collective-permute-start | bytes 393224 | tf_op jit(solution)/shard_map/ppermute | solution.py:334
  44.0 1.4 %collective-permute-start.24 = (bf16[512,128]{1,0:T(8,128)(2,1)S(1)}, bf16[512,128]{1,0:T(8,128)(2,1)S(1)}, u32[]{:S(2)}, u32[]{:S(2)}) collective-permute-start(bf16[512,128]{1,0:T(8,128)(2,1)S(1)} %collective-permute-done.19.rest_6_), channel_id=1, source_target_pairs={{0,4},{1,3},{4,8},{5,1},{8,12},{9,5},{12,14},{13,9},{14,10},{15,13... | collective-permute-start | bytes 393224 | tf_op jit(solution)/shard_map/ppermute | solution.py:334
  45.4 1.4 %collective-permute-start.23 = (bf16[512,128]{1,0:T(8,128)(2,1)S(1)}, bf16[512,128]{1,0:T(8,128)(2,1)S(1)}, u32[]{:S(2)}, u32[]{:S(2)}) collective-permute-start(bf16[512,128]{1,0:T(8,128)(2,1)S(1)} %collective-permute-done.17.rest_4_), channel_id=1, source_target_pairs={{0,4},{1,3},{4,8},{5,1},{8,12},{9,5},{12,14},{13,9},{14,10},{15,13... | collective-permute-start | bytes 393224 | tf_op jit(solution)/shard_map/ppermute | solution.py:334
  46.8 0.7 %early_scores.2.rest_8_ = f32[4,2,256,128]{3,2,1,0:T(8,128)S(1)} custom-call(bf16[256,4096]{1,0:T(8,128)(2,1)S(1)} %copy-done, bf16[256,4096]{1,0:T(8,128)(2,1)S(1)} %collective-permute-done.3.other_ref, bf16[512,128]{1,0:T(8,128)(2,1)S(1)} %get-tuple-element.24.rest_0_, bf16[512,128]{1,0:T(8,128)(2,1)S(1)} %collective-permute-done.9.rest_1_, ...), custom_call_target="tpu_custom_call" | custom-call | tf_op jit(solution)/shard_map/early_scores/pallas_call | solution.py:226
  47.5 0.7 %collective-permute-done.18.rest_5_ = bf16[512,128]{1,0:T(8,128)(2,1)S(1)} collective-permute-done((bf16[512,128]{1,0:T(8,128)(2,1)S(1)}, bf16[512,128]{1,0:T(8,128)(2,1)S(1)}, u32[]{:S(2)}, u32[]{:S(2)}) %collective-permute-start.18) | collective-permute-done | bytes 131104 | tf_op jit(solution)/shard_map/ppermute | solution.py:334
  48.3 1.2 %early_scores.3 = (f32[512,256]{1,0:T(8,128)S(1)}, f32[256,256]{1,0:T(8,128)S(1)}, f32[256,256]{1,0:T(8,128)S(1)}) custom-call(bf16[256,4096]{1,0:T(8,128)(2,1)S(1)} %copy-done, bf16[256,4096]{1,0:T(8,128)(2,1)S(1)} %collective-permute-done.3.other_ref, bf16[512,128]{1,0:T(8,128)(2,1)S(1)} %collective-permute-done.8.rest_0_, ...), custom_call_target="tpu_custom_call" | custom-call | tf_op jit(solution)/shard_map/early_scores/pallas_call | solution.py:226
  49.4 0.1 collective-permute-start.21
  49.5 0.5 collective-permute-start.22
  50.0 0.1 collective-permute-start.26
  50.1 1.0 %collective-permute-done.23.rest_0_ = bf16[512,128]{1,0:T(8,128)(2,1)S(1)} collective-permute-done((bf16[512,128]{1,0:T(8,128)(2,1)S(1)}, bf16[512,128]{1,0:T(8,128)(2,1)S(1)}, u32[]{:S(2)}, u32[]{:S(2)}) %collective-permute-start.23) | collective-permute-done | bytes 131104 | tf_op jit(solution)/shard_map/ppermute | solution.py:334
  51.1 0.5 collective-permute-done.26.rest_3_
  51.6 0.8 %collective-permute-done.25.rest_2_ = bf16[512,128]{1,0:T(8,128)(2,1)S(1)} collective-permute-done((bf16[512,128]{1,0:T(8,128)(2,1)S(1)}, bf16[512,128]{1,0:T(8,128)(2,1)S(1)}, u32[]{:S(2)}, u32[]{:S(2)}) %collective-permute-start.25) | collective-permute-done | bytes 131104 | tf_op jit(solution)/shard_map/ppermute | solution.py:350
  52.4 1.1 %final_scores.1 = f32[512,256]{1,0:T(8,128)} custom-call(bf16[256,4096]{1,0:T(8,128)(2,1)S(1)} %copy-done, f32[512,256]{1,0:T(8,128)S(1)} %get-tuple-element.26.keep_ref, f32[256,256]{1,0:T(8,128)S(1)} %collective-permute-done.21.got_ref, f32[256,256]{1,0:T(8,128)S(1)} %collective-permute-done.22.more_ref, ...), custom_call_target="tpu_custom_call" | custom-call | tf_op jit(solution)/shard_map/final_scores/pallas_call | solution.py:273
  (19 shorter events, 0.1 us)
Async XLA Ops:
  3.9 9.5 %collective-permute-start = (bf16[256,128]{1,0:T(8,128)(2,1)S(1)}, bf16[256,128]{1,0:T(8,128)(2,1)S(1)}, u32[]{:S(2)}, u32[]{:S(2)}) collective-permute-start(bf16[256,128]{1,0:T(8,128)(2,1)S(1)} %get-tuple-element.17), channel_id=1, source_target_pairs={{0,4},{4,8},{8,12},{12,0},{1,5},{5,9},{9,13},{13,1},{2,6},{6,10},{... | collective-permute-start | bytes 196616 | tf_op jit(solution)/shard_map/ppermute | solution.py:295
  7.0 7.1 %collective-permute-start.1 = (bf16[256,128]{1,0:T(8,128)(2,1)S(1)}, bf16[256,128]{1,0:T(8,128)(2,1)S(1)}, u32[]{:S(2)}, u32[]{:S(2)}) collective-permute-start(bf16[256,128]{1,0:T(8,128)(2,1)S(1)} %get-tuple-element.18), channel_id=1, source_target_pairs={{0,8},{4,12},{8,0},{12,4},{1,9},{5,13},{9,1},{13,5},{2,10},{6,14},... | collective-permute-start | bytes 196616 | tf_op jit(solution)/shard_map/ppermute | solution.py:295
  9.6 8.8 %copy-start = (bf16[256,4096]{1,0:T(8,128)(2,1)S(1)}, bf16[256,4096]{1,0:T(8,128)(2,1)}, u32[]{:S(2)}) copy-start(bf16[256,4096]{1,0:T(8,128)(2,1)} %stored_ref) | copy-start | bytes 6291460
  9.6 8.8 %copy-start.1 = (s32[1,1024]{1,0:T(1,128)S(1)}, s32[1,1024]{1,0:T(1,128)}, u32[]{:S(2)}) copy-start(s32[1,1024]{1,0:T(1,128)} %param.9) | copy-start | bytes 12292
  9.6 4.7 %collective-permute-start.2 = (bf16[256,128]{1,0:T(8,128)(2,1)S(1)}, bf16[256,128]{1,0:T(8,128)(2,1)S(1)}, u32[]{:S(2)}, u32[]{:S(2)}) collective-permute-start(bf16[256,128]{1,0:T(8,128)(2,1)S(1)} %get-tuple-element.19), channel_id=1, source_target_pairs={{0,12},{4,0},{8,4},{12,8},{1,13},{5,1},{9,5},{13,9},{2,14},{6,2},{... | collective-permute-start | bytes 196616 | tf_op jit(solution)/shard_map/ppermute | solution.py:295
  14.3 7.7 %collective-permute-start.4 = (bf16[256,128]{1,0:T(8,128)(2,1)S(1)}, bf16[256,128]{1,0:T(8,128)(2,1)S(1)}, u32[]{:S(2)}, u32[]{:S(2)}) collective-permute-start(bf16[256,128]{1,0:T(8,128)(2,1)S(1)} %add_convert_fusion.rest_0_), channel_id=1, source_target_pairs={{0,4},{4,8},{8,12},{12,0},{1,5},{5,9},{9,13},{13,1},{2,6},{6,10},{... | collective-permute-start | bytes 196616 | tf_op jit(solution)/shard_map/ppermute | solution.py:295
  16.0 6.7 %collective-permute-start.5 = (bf16[256,128]{1,0:T(8,128)(2,1)S(1)}, bf16[256,128]{1,0:T(8,128)(2,1)S(1)}, u32[]{:S(2)}, u32[]{:S(2)}) collective-permute-start(bf16[256,128]{1,0:T(8,128)(2,1)S(1)} %add_convert_fusion.rest_0_), channel_id=1, source_target_pairs={{0,8},{4,12},{8,0},{12,4},{1,9},{5,13},{9,1},{13,5},{2,10},{6,14},... | collective-permute-start | bytes 196616 | tf_op jit(solution)/shard_map/ppermute | solution.py:295
  18.0 5.0 %collective-permute-start.6 = (bf16[256,128]{1,0:T(8,128)(2,1)S(1)}, bf16[256,128]{1,0:T(8,128)(2,1)S(1)}, u32[]{:S(2)}, u32[]{:S(2)}) collective-permute-start(bf16[256,128]{1,0:T(8,128)(2,1)S(1)} %add_convert_fusion.rest_0_), channel_id=1, source_target_pairs={{0,12},{4,0},{8,4},{12,8},{1,13},{5,1},{9,5},{13,9},{2,14},{6,2},{... | collective-permute-start | bytes 196616 | tf_op jit(solution)/shard_map/ppermute | solution.py:295
  18.4 28.5 %collective-permute-start.3 = (bf16[256,4096]{1,0:T(8,128)(2,1)S(1)}, bf16[256,4096]{1,0:T(8,128)(2,1)S(1)}, u32[]{:S(2)}, u32[]{:S(2)}) collective-permute-start(bf16[256,4096]{1,0:T(8,128)(2,1)S(1)} %copy-done), channel_id=1, source_target_pairs={{0,1},{1,0},{2,3},{3,2},{4,5},{5,4},{6,7},{7,6},{8,9},{9,8},{10,11... | collective-permute-start | bytes 6291464 | tf_op jit(solution)/shard_map/ppermute | solution.py:331
  27.1 2.1 %collective-permute-start.14 = (bf16[512,128]{1,0:T(8,128)(2,1)S(1)}, bf16[512,128]{1,0:T(8,128)(2,1)S(1)}, u32[]{:S(2)}, u32[]{:S(2)}) collective-permute-start(bf16[512,128]{1,0:T(8,128)(2,1)S(1)} %curve.1.rest_2_), channel_id=1, source_target_pairs={{0,1},{1,0},{2,3},{3,2},{4,5},{5,4},{6,7},{7,6},{8,9},{9,8},{10,11... | collective-permute-start | bytes 393224 | tf_op jit(solution)/shard_map/ppermute | solution.py:335
  27.2 3.9 %collective-permute-start.9 = (bf16[512,128]{1,0:T(8,128)(2,1)S(1)}, bf16[512,128]{1,0:T(8,128)(2,1)S(1)}, u32[]{:S(2)}, u32[]{:S(2)}) collective-permute-start(bf16[512,128]{1,0:T(8,128)(2,1)S(1)} %get-tuple-element.24.rest_0_), channel_id=1, source_target_pairs={{0,1},{1,0},{2,3},{3,2},{4,5},{5,4},{6,7},{7,6},{8,9},{9,8},{10,11... | collective-permute-start | bytes 393224 | tf_op jit(solution)/shard_map/ppermute | solution.py:335
  27.7 5.0 %collective-permute-start.12 = (bf16[512,128]{1,0:T(8,128)(2,1)S(1)}, bf16[512,128]{1,0:T(8,128)(2,1)S(1)}, u32[]{:S(2)}, u32[]{:S(2)}) collective-permute-start(bf16[512,128]{1,0:T(8,128)(2,1)S(1)} %curve.1.rest_2_), channel_id=1, source_target_pairs={{0,4},{1,3},{4,8},{5,1},{8,12},{9,5},{12,14},{13,9},{14,10},{15,13... | collective-permute-start | bytes 393224 | tf_op jit(solution)/shard_map/ppermute | solution.py:334
  29.2 5.0 %collective-permute-start.7 = (bf16[512,128]{1,0:T(8,128)(2,1)S(1)}, bf16[512,128]{1,0:T(8,128)(2,1)S(1)}, u32[]{:S(2)}, u32[]{:S(2)}) collective-permute-start(bf16[512,128]{1,0:T(8,128)(2,1)S(1)} %get-tuple-element.24.rest_0_), channel_id=1, source_target_pairs={{0,4},{1,3},{4,8},{5,1},{8,12},{9,5},{12,14},{13,9},{14,10},{15,13... | collective-permute-start | bytes 393224 | tf_op jit(solution)/shard_map/ppermute | solution.py:334
  29.3 6.3 %collective-permute-start.15 = (bf16[512,128]{1,0:T(8,128)(2,1)S(1)}, bf16[512,128]{1,0:T(8,128)(2,1)S(1)}, u32[]{:S(2)}, u32[]{:S(2)}) collective-permute-start(bf16[512,128]{1,0:T(8,128)(2,1)S(1)} %collective-permute-done.14.rest_3_), channel_id=1, source_target_pairs={{0,4},{1,3},{4,8},{5,1},{8,12},{9,5},{12,14},{13,9},{14,10},{15,13... | collective-permute-start | bytes 393224 | tf_op jit(solution)/shard_map/ppermute | solution.py:334
  31.1 5.9 %collective-permute-start.10 = (bf16[512,128]{1,0:T(8,128)(2,1)S(1)}, bf16[512,128]{1,0:T(8,128)(2,1)S(1)}, u32[]{:S(2)}, u32[]{:S(2)}) collective-permute-start(bf16[512,128]{1,0:T(8,128)(2,1)S(1)} %collective-permute-done.9.rest_1_), channel_id=1, source_target_pairs={{0,4},{1,3},{4,8},{5,1},{8,12},{9,5},{12,14},{13,9},{14,10},{15,13... | collective-permute-start | bytes 393224 | tf_op jit(solution)/shard_map/ppermute | solution.py:334
  32.7 5.7 %collective-permute-start.13 = (bf16[512,128]{1,0:T(8,128)(2,1)S(1)}, bf16[512,128]{1,0:T(8,128)(2,1)S(1)}, u32[]{:S(2)}, u32[]{:S(2)}) collective-permute-start(bf16[512,128]{1,0:T(8,128)(2,1)S(1)} %collective-permute-done.12.rest_6_), channel_id=1, source_target_pairs={{0,4},{1,3},{4,8},{5,1},{8,12},{9,5},{12,14},{13,9},{14,10},{15,13... | collective-permute-start | bytes 393224 | tf_op jit(solution)/shard_map/ppermute | solution.py:334
  34.2 5.6 %collective-permute-start.8 = (bf16[512,128]{1,0:T(8,128)(2,1)S(1)}, bf16[512,128]{1,0:T(8,128)(2,1)S(1)}, u32[]{:S(2)}, u32[]{:S(2)}) collective-permute-start(bf16[512,128]{1,0:T(8,128)(2,1)S(1)} %collective-permute-done.7.rest_4_), channel_id=1, source_target_pairs={{0,4},{1,3},{4,8},{5,1},{8,12},{9,5},{12,14},{13,9},{14,10},{15,13... | collective-permute-start | bytes 393224 | tf_op jit(solution)/shard_map/ppermute | solution.py:334
  35.6 5.6 %collective-permute-start.16 = (bf16[512,128]{1,0:T(8,128)(2,1)S(1)}, bf16[512,128]{1,0:T(8,128)(2,1)S(1)}, u32[]{:S(2)}, u32[]{:S(2)}) collective-permute-start(bf16[512,128]{1,0:T(8,128)(2,1)S(1)} %collective-permute-done.15.rest_7_), channel_id=1, source_target_pairs={{0,4},{1,3},{4,8},{5,1},{8,12},{9,5},{12,14},{13,9},{14,10},{15,13... | collective-permute-start | bytes 393224 | tf_op jit(solution)/shard_map/ppermute | solution.py:334
  37.0 5.6 %collective-permute-start.11 = (bf16[512,128]{1,0:T(8,128)(2,1)S(1)}, bf16[512,128]{1,0:T(8,128)(2,1)S(1)}, u32[]{:S(2)}, u32[]{:S(2)}) collective-permute-start(bf16[512,128]{1,0:T(8,128)(2,1)S(1)} %collective-permute-done.10.rest_5_), channel_id=1, source_target_pairs={{0,4},{1,3},{4,8},{5,1},{8,12},{9,5},{12,14},{13,9},{14,10},{15,13... | collective-permute-start | bytes 393224 | tf_op jit(solution)/shard_map/ppermute | solution.py:334
  38.4 5.6 %collective-permute-start.19 = (bf16[512,128]{1,0:T(8,128)(2,1)S(1)}, bf16[512,128]{1,0:T(8,128)(2,1)S(1)}, u32[]{:S(2)}, u32[]{:S(2)}) collective-permute-start(bf16[512,128]{1,0:T(8,128)(2,1)S(1)} %collective-permute-done.13.rest_2_), channel_id=1, source_target_pairs={{0,4},{1,3},{4,8},{5,1},{8,12},{9,5},{12,14},{13,9},{14,10},{15,13... | collective-permute-start | bytes 393224 | tf_op jit(solution)/shard_map/ppermute | solution.py:334
  39.8 5.6 %collective-permute-start.17 = (bf16[512,128]{1,0:T(8,128)(2,1)S(1)}, bf16[512,128]{1,0:T(8,128)(2,1)S(1)}, u32[]{:S(2)}, u32[]{:S(2)}) collective-permute-start(bf16[512,128]{1,0:T(8,128)(2,1)S(1)} %collective-permute-done.8.rest_0_), channel_id=1, source_target_pairs={{0,4},{1,3},{4,8},{5,1},{8,12},{9,5},{12,14},{13,9},{14,10},{15,13... | collective-permute-start | bytes 393224 | tf_op jit(solution)/shard_map/ppermute | solution.py:334
  41.2 6.3 %collective-permute-start.20 = (bf16[512,128]{1,0:T(8,128)(2,1)S(1)}, bf16[512,128]{1,0:T(8,128)(2,1)S(1)}, u32[]{:S(2)}, u32[]{:S(2)}) collective-permute-start(bf16[512,128]{1,0:T(8,128)(2,1)S(1)} %collective-permute-done.16.rest_3_), channel_id=1, source_target_pairs={{0,4},{1,3},{4,8},{5,1},{8,12},{9,5},{12,14},{13,9},{14,10},{15,13... | collective-permute-start | bytes 393224 | tf_op jit(solution)/shard_map/ppermute | solution.py:334
  42.6 5.6 %collective-permute-start.18 = (bf16[512,128]{1,0:T(8,128)(2,1)S(1)}, bf16[512,128]{1,0:T(8,128)(2,1)S(1)}, u32[]{:S(2)}, u32[]{:S(2)}) collective-permute-start(bf16[512,128]{1,0:T(8,128)(2,1)S(1)} %collective-permute-done.11.rest_1_), channel_id=1, source_target_pairs={{0,4},{1,3},{4,8},{5,1},{8,12},{9,5},{12,14},{13,9},{14,10},{15,13... | collective-permute-start | bytes 393224 | tf_op jit(solution)/shard_map/ppermute | solution.py:334
  44.0 6.0 %collective-permute-start.24 = (bf16[512,128]{1,0:T(8,128)(2,1)S(1)}, bf16[512,128]{1,0:T(8,128)(2,1)S(1)}, u32[]{:S(2)}, u32[]{:S(2)}) collective-permute-start(bf16[512,128]{1,0:T(8,128)(2,1)S(1)} %collective-permute-done.19.rest_6_), channel_id=1, source_target_pairs={{0,4},{1,3},{4,8},{5,1},{8,12},{9,5},{12,14},{13,9},{14,10},{15,13... | collective-permute-start | bytes 393224 | tf_op jit(solution)/shard_map/ppermute | solution.py:334
  45.4 5.6 %collective-permute-start.23 = (bf16[512,128]{1,0:T(8,128)(2,1)S(1)}, bf16[512,128]{1,0:T(8,128)(2,1)S(1)}, u32[]{:S(2)}, u32[]{:S(2)}) collective-permute-start(bf16[512,128]{1,0:T(8,128)(2,1)S(1)} %collective-permute-done.17.rest_4_), channel_id=1, source_target_pairs={{0,4},{1,3},{4,8},{5,1},{8,12},{9,5},{12,14},{13,9},{14,10},{15,13... | collective-permute-start | bytes 393224 | tf_op jit(solution)/shard_map/ppermute | solution.py:334
  49.4 3.0 %collective-permute-start.21 = (f32[256,256]{1,0:T(8,128)S(1)}, f32[256,256]{1,0:T(8,128)S(1)}, u32[]{:S(2)}, u32[]{:S(2)}) collective-permute-start(f32[256,256]{1,0:T(8,128)S(1)} %get-tuple-element.27), channel_id=1, source_target_pairs={{0,1},{1,0},{2,3},{3,2},{4,5},{5,4},{6,7},{7,6},{8,9},{9,8},{10,11... | collective-permute-start | bytes 786440 | tf_op jit(solution)/shard_map/ppermute | solution.py:349
  49.5 2.9 %collective-permute-start.22 = (f32[256,256]{1,0:T(8,128)S(1)}, f32[256,256]{1,0:T(8,128)S(1)}, u32[]{:S(2)}, u32[]{:S(2)}) collective-permute-start(f32[256,256]{1,0:T(8,128)S(1)} %get-tuple-element.28), channel_id=1, source_target_pairs={{0,1},{1,0},{2,3},{3,2},{4,5},{5,4},{6,7},{7,6},{8,9},{9,8},{10,11... | collective-permute-start | bytes 786440 | tf_op jit(solution)/shard_map/ppermute | solution.py:349
  50.0 1.6 %collective-permute-start.26 = (bf16[512,128]{1,0:T(8,128)(2,1)S(1)}, bf16[512,128]{1,0:T(8,128)(2,1)S(1)}, u32[]{:S(2)}, u32[]{:S(2)}) collective-permute-start(bf16[512,128]{1,0:T(8,128)(2,1)S(1)} %collective-permute-done.24.rest_1_), channel_id=1, source_target_pairs={{0,1},{1,0},{2,3},{3,2},{4,5},{5,4},{6,7},{7,6},{8,9},{9,8},{10,11... | collective-permute-start | bytes 393224 | tf_op jit(solution)/shard_map/ppermute | solution.py:350
  51.1 1.3 %collective-permute-start.25 = (bf16[512,128]{1,0:T(8,128)(2,1)S(1)}, bf16[512,128]{1,0:T(8,128)(2,1)S(1)}, u32[]{:S(2)}, u32[]{:S(2)}) collective-permute-start(bf16[512,128]{1,0:T(8,128)(2,1)S(1)} %collective-permute-done.23.rest_0_), channel_id=1, source_target_pairs={{0,1},{1,0},{2,3},{3,2},{4,5},{5,4},{6,7},{7,6},{8,9},{9,8},{10,11... | collective-permute-start | bytes 393224 | tf_op jit(solution)/shard_map/ppermute | solution.py:350
